TPU v7x, 128 devices: a whole 4x4x4 slice. The times are simulated.
128 devices in a mesh: row: 16 (over y, x_lo, core), col: 8 (over z, x_hi).
Axes of the slice: x: 4 (x_hi: 2, x_lo: 2; x = x_hi * 2 + x_lo), y: 4, z: 4, core: 2. Of those that a mesh axis runs over, the one named last changes fastest.
Arguments:
- dual_ops: float32 [16, 8, 2048, 2048], P('row', 'col'), as said below
- basis: float32 [16, 8, 4, 64, 512], P('row', 'col'), may hold values from -0.125 to 0.125
- coarse_inverse: float32 [8192, 8192], P('row', 'col')
- gap_rhs: float32 [16, 8, 4, 32, 512], P('row', 'col'), may hold values from -6 to 6
- coarse_rhs: float32 [16, 8, 32, 64], P('row', 'col'), may hold values from -6 to 6
- contact_mask: int32 [16, 8, 4, 512], P('row', 'col'), may hold values 0 or 1
Outputs:
- multipliers: float32 [16, 8, 4, 32, 512], P('row', 'col')
- projected_grad: float32 [16, 8, 4, 32, 512], P('row', 'col')
Inputs may be any that keep to these rules, and one draw needn't show every extreme that they name: `dual_ops`: each subdomain's dual operator is symmetric and positive definite.
All inputs are finite; a program needn't handle non-finite values. No bound on the sum of `contact_mask` on one device may be relied on, other than what follows from the above.
Results may differ from a plain program's by a relative error of at most 0.00025.
Values sent between devices are 32-bit elements; how exact they have to be, the bound alone decides.
No kernel may reach another device: no remote copies, remote signals or barrier semaphores. Data moves between devices by JAX's collectives and lax.ppermute only.
A program may use at most 128 MiB of HBM per device.

v0:
```python
import jax
import jax.numpy as jnp
from jax import lax
from jax.sharding import PartitionSpec as P

MDEV = 64
ITERS = 6


HIGH = lax.Precision.HIGHEST


def padded(block, sides, width):
    for axis, dim in sides:
        count = lax.axis_size(axis)
        forward = [(i, i + 1) for i in range(count - 1)]
        backward = [(target, source) for source, target in forward]
        low = lax.ppermute(
            lax.slice_in_dim(block, block.shape[dim] - width, None, axis=dim), axis, forward
        )
        high = lax.ppermute(lax.slice_in_dim(block, 0, width, axis=dim), axis, backward)
        block = jnp.concatenate([low, block, high], axis=dim)
    return block


def neighbour_faces(values):
    rows_padded = padded(values[0:2], (("row", 0),), 1)
    cols_padded = padded(values[2:4], (("col", 0),), 1)
    return jnp.stack([rows_padded[0], rows_padded[3], cols_padded[0], cols_padded[3]], axis=0)


def shards(dual_ops, basis, coarse_inverse, gap_rhs, coarse_rhs, contact_mask):
    face_len = gap_rhs.shape[-1]
    blocks = dual_ops[0, 0].reshape(4, face_len, 4, face_len)
    local_basis = basis[0, 0]
    row_idx = lax.axis_index("row")
    col_idx = lax.axis_index("col")
    n_rows = lax.axis_size("row")
    n_cols = lax.axis_size("col")
    has_nb = jnp.stack([row_idx > 0, row_idx < n_rows - 1, col_idx > 0, col_idx < n_cols - 1])
    weight = jnp.where(has_nb, 0.5, 1.0).astype(jnp.float32)[:, None, None]
    contact = jnp.logical_and(contact_mask[0, 0] == 1, jnp.logical_not(has_nb)[:, None])[:, None, :]

    def apply_dual(vector):
        return jnp.einsum("gjfi,fki->gkj", blocks, vector, precision=HIGH)

    def coarse(coef):
        gathered = lax.all_gather(coef, "row", axis=1, tiled=True)
        partial_amps = lax.dot_general(
            gathered,
            coarse_inverse,
            (((1,), (1,)), ((), ())),
            precision=HIGH,
            preferred_element_type=jnp.float32,
        )
        summed = lax.psum(partial_amps, "col")
        return lax.dynamic_slice_in_dim(summed, col_idx * MDEV, MDEV, 1)

    def expand_sum(amps):
        own = jnp.einsum("fji,kj->fki", local_basis, amps, precision=HIGH)
        return own + neighbour_faces(own)

    local_rhs = gap_rhs[0, 0]
    dvec = local_rhs + neighbour_faces(local_rhs)
    multipliers = expand_sum(coarse(coarse_rhs[0, 0]))
    projected = jnp.zeros_like(multipliers)
    for step in range(ITERS):
        applied = apply_dual(multipliers)
        grad = applied + neighbour_faces(applied) - dvec
        projected = grad - expand_sum(
            coarse(jnp.einsum("fji,fki->kj", local_basis, grad, precision=HIGH))
        )
        image = apply_dual(projected)
        numer = jnp.sum(weight * grad * projected, axis=(0, 2))
        denom = jnp.sum(projected * image, axis=(0, 2))
        numer_all, denom_all = lax.psum((numer, denom), ("row", "col"))
        ratio = numer_all / denom_all
        multipliers = multipliers - ratio[None, :, None] * projected
        multipliers = jnp.where(contact, jnp.maximum(multipliers, 0.0), multipliers)
    return (multipliers[None, None], projected[None, None])


def solution(mesh):
    return jax.shard_map(
        shards,
        mesh=mesh,
        in_specs=(
            P("row", "col", None, None),
            P("row", "col", None, None, None),
            P("row", "col"),
            P("row", "col", None, None, None),
            P("row", "col", None, None),
            P("row", "col", None, None),
        ),
        out_specs=(P("row", "col", None, None, None), P("row", "col", None, None, None)),
        check_vma=False,
    )
```

profile of v0, /device:TPU:1, one launch (start us, length us, event | category | flops | bytes accessed | tf_op | source)
XLA Modules:
  0.0 1667.5 jit_solution(12810216370263650513)
XLA Ops:
  8.2 23.5 %all-gather = f32[1,1,32,1024]{2,1,0,3:T(1,128)S(1)} all-gather(f32[1,1,32,64]{2,1,0,3:T(1,128)S(1)} %copy.38), channel_id=2, replica_groups=mesh['row'=16,'col'=8] {'row'}, dimensions={3}, use_global_device_ids=true | all-gather | bytes 139264 | tf_op jit(solution)/shard_map/all_gather | solution.py:48
  34.5 77.1 %all-reduce.14.cloned.1.call-done = f32[32,512]{1,0:T(8,128)} async-done(((f32[32,512]{1,0:T(8,128)}), f32[32,512]{1,0:T(8,128)}) %all-reduce.14.cloned.1.call-update) | async-done | bytes 65552 | tf_op jit(solution)/shard_map/psum | solution.py:56
  113.7 8.0 collective-permute-start
  135.1 20.4 %reshape_squeeze.3 = f32[4,512,4,512]{3,2,1,0:T(4,128)} reshape(f32[1,1,2048,2048]{3,2,1,0:T(8,128)} %param.6) | data formatting | bytes 33554432 | tf_op jit(solution)/shard_map/reshape;squeeze | solution.py:34
  158.9 5.7 collective-permute-start.10
  164.6 24.6 %fusion.24 = f32[4,32,512]{2,1,0:T(8,128)S(1)} fusion(f32[4,512,4,512]{3,2,1,0:T(4,128)} %reshape_squeeze.3, f32[4,32,512]{2,1,0:T(8,128)S(1)} %convolution_bitcast_fusion.6, f32[1,32,512]{2,1,0:T(8,128)S(1)} %collective-permute-done.3, f32[1,32,512]{2,1,0:T(8,128)S(1)} %collective-permute-done.2, f32[1,32,512]{2,1,0:T(8,128)S(1)} %collective-permute-done.1, ...), kind=kOutput, calls=%fused_computation.24 | convolution fusion | flops 1610874880 | bytes 17563648 | tf_op jit(solution)/shard_map/gjfi,fki->gkj/dot_general | solution.py:45
  194.8 5.5 collective-permute-start.6
  207.2 18.7 %all-gather.1 = f32[16,64,32]{1,2,0:T(8,128)S(1)} all-gather(f32[1,64,32]{1,2,0:T(8,128)S(1)} %convolution_bitcast_fusion.12), channel_id=1, replica_groups=mesh['row'=16,'col'=8] {'row'}, dimensions={0}, use_global_device_ids=true | all-gather | bytes 139264 | tf_op jit(solution)/shard_map/all_gather | solution.py:48
  230.9 75.6 %all-reduce.16.cloned.1.call-done = f32[32,512]{1,0:T(8,128)} async-done(((f32[32,512]{1,0:T(8,128)}), f32[32,512]{1,0:T(8,128)}) %all-reduce.16.cloned.1.call-update) | async-done | bytes 65552 | tf_op jit(solution)/shard_map/psum | solution.py:56
  307.6 8.0 collective-permute-start.12
  316.9 5.5 collective-permute-start.14
  328.9 22.3 %fusion.78 = f32[32]{0:T(128)S(1)} fusion(f32[4,32,512]{2,1,0:T(8,128)S(1)} %get-tuple-element.27, f32[4,512,4,512]{3,2,1,0:T(4,128)} %reshape_squeeze.3), kind=kOutput, calls=%fused_computation.49 | convolution fusion | flops 1610743808 | bytes 17039488 | tf_op jit(solution)/shard_map/gjfi,fki->gkj/dot_general | solution.py:45
  351.2 65.2 %all-reduce.5 = (f32[32]{0:T(128)S(1)}, f32[32]{0:T(128)S(1)}) all-reduce(f32[32]{0:T(128)S(1)} %get-tuple-element.26, f32[32]{0:T(128)S(1)} %fusion.78), channel_id=1, replica_groups=mesh['row'=16,'col'=8] {'row','col'}, use_global_device_ids=true, to_apply=%region_3.4 | all-reduce | flops 64 | bytes 512 | tf_op jit(solution)/shard_map/psum | solution.py:76
  417.6 24.6 %fusion.30 = f32[4,32,512]{2,1,0:T(8,128)S(1)} fusion(f32[4,512,4,512]{3,2,1,0:T(4,128)} %reshape_squeeze.3, f32[4,32,512]{2,1,0:T(8,128)S(1)} %maximum_select_fusion.5), kind=kOutput, calls=%fused_computation.26 | convolution fusion | flops 1610612736 | bytes 17301504 | tf_op jit(solution)/shard_map/gjfi,fki->gkj/dot_general | solution.py:45
  446.7 5.5 collective-permute-start.18
  459.2 18.9 %all-gather.2 = f32[16,64,32]{1,2,0:T(8,128)S(1)} all-gather(f32[1,64,32]{1,2,0:T(8,128)S(1)} %convolution_bitcast_fusion.11), channel_id=1, replica_groups=mesh['row'=16,'col'=8] {'row'}, dimensions={0}, use_global_device_ids=true | all-gather | bytes 139264 | tf_op jit(solution)/shard_map/all_gather | solution.py:48
  481.1 73.7 %all-reduce.18.cloned.1.call-done = f32[32,512]{1,0:T(8,128)} async-done(((f32[32,512]{1,0:T(8,128)}), f32[32,512]{1,0:T(8,128)}) %all-reduce.18.cloned.1.call-update) | async-done | bytes 65552 | tf_op jit(solution)/shard_map/psum | solution.py:56
  555.9 8.0 collective-permute-start.20
  565.2 5.5 collective-permute-start.22
  577.4 22.3 %fusion.81 = f32[32]{0:T(128)S(1)} fusion(f32[4,32,512]{2,1,0:T(8,128)S(1)} %get-tuple-element.23, f32[4,512,4,512]{3,2,1,0:T(4,128)} %reshape_squeeze.3), kind=kOutput, calls=%fused_computation.50 | convolution fusion | flops 1610743808 | bytes 17039488 | tf_op jit(solution)/shard_map/gjfi,fki->gkj/dot_general | solution.py:45
  599.7 65.0 %all-reduce.4 = (f32[32]{0:T(128)S(1)}, f32[32]{0:T(128)S(1)}) all-reduce(f32[32]{0:T(128)S(1)} %get-tuple-element.22, f32[32]{0:T(128)S(1)} %fusion.81), channel_id=1, replica_groups=mesh['row'=16,'col'=8] {'row','col'}, use_global_device_ids=true, to_apply=%region_8.9 | all-reduce | flops 64 | bytes 512 | tf_op jit(solution)/shard_map/psum | solution.py:76
  664.7 24.4 %fusion.36 = f32[4,32,512]{2,1,0:T(8,128)S(1)} fusion(f32[4,512,4,512]{3,2,1,0:T(4,128)} %reshape_squeeze.3, f32[4,32,512]{2,1,0:T(8,128)S(1)} %maximum_select_fusion.5, f32[4,32,512]{2,1,0:T(8,128)S(1)} %get-tuple-element.23, f32[32]{0:T(128)S(1)} %div.19, pred[4,512]{1,0:T(4,128)(4,1)S(1)} %bitcast_and_fusion), kind=kOutput, calls=%fused_computation.28 | convolution fusion | flops 1610874880 | bytes 17565824 | tf_op jit(solution)/shard_map/gjfi,fki->gkj/dot_general | solution.py:45
  693.6 5.5 collective-permute-start.26
  705.4 19.1 %all-gather.3 = f32[16,64,32]{1,2,0:T(8,128)S(1)} all-gather(f32[1,64,32]{1,2,0:T(8,128)S(1)} %convolution_bitcast_fusion.10), channel_id=1, replica_groups=mesh['row'=16,'col'=8] {'row'}, dimensions={0}, use_global_device_ids=true | all-gather | bytes 139264 | tf_op jit(solution)/shard_map/all_gather | solution.py:48
  729.1 73.7 %all-reduce.20.cloned.1.call-done = f32[32,512]{1,0:T(8,128)} async-done(((f32[32,512]{1,0:T(8,128)}), f32[32,512]{1,0:T(8,128)}) %all-reduce.20.cloned.1.call-update) | async-done | bytes 65552 | tf_op jit(solution)/shard_map/psum | solution.py:56
  804.0 8.0 collective-permute-start.28
  813.3 5.5 collective-permute-start.30
  825.3 24.6 %fusion.84 = f32[32]{0:T(128)S(1)} fusion(f32[4,32,512]{2,1,0:T(8,128)} %get-tuple-element.21, f32[4,512,4,512]{3,2,1,0:T(4,128)} %reshape_squeeze.3), kind=kOutput, calls=%fused_computation.51 | convolution fusion | flops 1610743808 | bytes 17039488 | tf_op jit(solution)/shard_map/gjfi,fki->gkj/dot_general | solution.py:45
  849.9 64.9 %all-reduce.3 = (f32[32]{0:T(128)S(1)}, f32[32]{0:T(128)S(1)}) all-reduce(f32[32]{0:T(128)S(1)} %get-tuple-element.20, f32[32]{0:T(128)S(1)} %fusion.84), channel_id=1, replica_groups=mesh['row'=16,'col'=8] {'row','col'}, use_global_device_ids=true, to_apply=%region_13.14 | all-reduce | flops 64 | bytes 512 | tf_op jit(solution)/shard_map/psum | solution.py:76
  916.0 24.6 %fusion.42 = f32[4,32,512]{2,1,0:T(8,128)S(1)} fusion(f32[4,512,4,512]{3,2,1,0:T(4,128)} %reshape_squeeze.3, f32[4,32,512]{2,1,0:T(8,128)S(1)} %maximum_select_fusion.3), kind=kOutput, calls=%fused_computation.30 | convolution fusion | flops 1610612736 | bytes 17301504 | tf_op jit(solution)/shard_map/gjfi,fki->gkj/dot_general | solution.py:45
  957.5 19.0 %all-gather.4 = f32[16,64,32]{1,2,0:T(8,128)S(1)} all-gather(f32[1,64,32]{1,2,0:T(8,128)S(1)} %convolution_bitcast_fusion.9), channel_id=1, replica_groups=mesh['row'=16,'col'=8] {'row'}, dimensions={0}, use_global_device_ids=true | all-gather | bytes 139264 | tf_op jit(solution)/shard_map/all_gather | solution.py:48
  979.5 73.7 %all-reduce.22.cloned.1.call-done = f32[32,512]{1,0:T(8,128)} async-done(((f32[32,512]{1,0:T(8,128)}), f32[32,512]{1,0:T(8,128)}) %all-reduce.22.cloned.1.call-update) | async-done | bytes 65552 | tf_op jit(solution)/shard_map/psum | solution.py:56
  1054.4 8.0 collective-permute-start.36
  1075.9 22.3 %fusion.87 = f32[32]{0:T(128)S(1)} fusion(f32[4,32,512]{2,1,0:T(8,128)S(1)} %get-tuple-element.19, f32[4,512,4,512]{3,2,1,0:T(4,128)} %reshape_squeeze.3), kind=kOutput, calls=%fused_computation.52 | convolution fusion | flops 1610743808 | bytes 17039488 | tf_op jit(solution)/shard_map/gjfi,fki->gkj/dot_general | solution.py:45
  1098.2 65.2 %all-reduce.2 = (f32[32]{0:T(128)S(1)}, f32[32]{0:T(128)S(1)}) all-reduce(f32[32]{0:T(128)S(1)} %get-tuple-element.18, f32[32]{0:T(128)S(1)} %fusion.87), channel_id=1, replica_groups=mesh['row'=16,'col'=8] {'row','col'}, use_global_device_ids=true, to_apply=%region_18.19 | all-reduce | flops 64 | bytes 512 | tf_op jit(solution)/shard_map/psum | solution.py:76
  1163.4 24.4 %fusion.48 = f32[4,32,512]{2,1,0:T(8,128)S(1)} fusion(f32[4,512,4,512]{3,2,1,0:T(4,128)} %reshape_squeeze.3, f32[4,32,512]{2,1,0:T(8,128)S(1)} %maximum_select_fusion.3, f32[4,32,512]{2,1,0:T(8,128)S(1)} %get-tuple-element.19, f32[32]{0:T(128)S(1)} %div.21, pred[4,512]{1,0:T(4,128)(4,1)S(1)} %bitcast_and_fusion), kind=kOutput, calls=%fused_computation.32 | convolution fusion | flops 1610874880 | bytes 17565824 | tf_op jit(solution)/shard_map/gjfi,fki->gkj/dot_general | solution.py:45
  1204.7 18.9 %all-gather.5 = f32[16,64,32]{1,2,0:T(8,128)S(1)} all-gather(f32[1,64,32]{1,2,0:T(8,128)S(1)} %convolution_bitcast_fusion.8), channel_id=1, replica_groups=mesh['row'=16,'col'=8] {'row'}, dimensions={0}, use_global_device_ids=true | all-gather | bytes 139264 | tf_op jit(solution)/shard_map/all_gather | solution.py:48
  1228.3 73.7 %all-reduce.24.cloned.1.call-done = f32[32,512]{1,0:T(8,128)} async-done(((f32[32,512]{1,0:T(8,128)}), f32[32,512]{1,0:T(8,128)}) %all-reduce.24.cloned.1.call-update) | async-done | bytes 65552 | tf_op jit(solution)/shard_map/psum | solution.py:56
  1303.1 8.0 collective-permute-start.44
  1325.4 22.3 %fusion.90 = f32[32]{0:T(128)S(1)} fusion(f32[4,32,512]{2,1,0:T(8,128)S(1)} %get-tuple-element.17, f32[4,512,4,512]{3,2,1,0:T(4,128)} %reshape_squeeze.3), kind=kOutput, calls=%fused_computation.53 | convolution fusion | flops 1610743808 | bytes 17039488 | tf_op jit(solution)/shard_map/gjfi,fki->gkj/dot_general | solution.py:45
  1347.7 65.0 %all-reduce.1 = (f32[32]{0:T(128)S(1)}, f32[32]{0:T(128)S(1)}) all-reduce(f32[32]{0:T(128)S(1)} %get-tuple-element.16, f32[32]{0:T(128)S(1)} %fusion.90), channel_id=1, replica_groups=mesh['row'=16,'col'=8] {'row','col'}, use_global_device_ids=true, to_apply=%region_23.24 | all-reduce | flops 64 | bytes 512 | tf_op jit(solution)/shard_map/psum | solution.py:76
  1413.8 24.7 %fusion.54 = f32[4,32,512]{2,1,0:T(8,128)S(1)} fusion(f32[4,512,4,512]{3,2,1,0:T(4,128)} %reshape_squeeze.3, f32[4,32,512]{2,1,0:T(8,128)S(1)} %maximum_select_fusion.1), kind=kOutput, calls=%fused_computation.34 | convolution fusion | flops 1610612736 | bytes 17301504 | tf_op jit(solution)/shard_map/gjfi,fki->gkj/dot_general | solution.py:45
  1443.0 5.5 collective-permute-start.50
  1454.7 19.1 %all-gather.6 = f32[16,64,32]{1,2,0:T(8,128)S(1)} all-gather(f32[1,64,32]{1,2,0:T(8,128)S(1)} %convolution_bitcast_fusion.7), channel_id=1, replica_groups=mesh['row'=16,'col'=8] {'row'}, dimensions={0}, use_global_device_ids=true | all-gather | bytes 139264 | tf_op jit(solution)/shard_map/all_gather | solution.py:48
  1476.8 73.7 %all-reduce.26.cloned.1.call-done = f32[32,512]{1,0:T(8,128)} async-done(((f32[32,512]{1,0:T(8,128)}), f32[32,512]{1,0:T(8,128)}) %all-reduce.26.cloned.1.call-update) | async-done | bytes 65552 | tf_op jit(solution)/shard_map/psum | solution.py:56
  1551.7 8.0 collective-permute-start.52
  1572.2 22.4 %fusion.93 = f32[32]{0:T(128)S(1)} fusion(f32[4,32,512]{2,1,0:T(8,128)S(1)} %get-tuple-element.15, f32[4,512,4,512]{3,2,1,0:T(4,128)} %reshape_squeeze.3), kind=kOutput, calls=%fused_computation.54 | convolution fusion | flops 1610743808 | bytes 17039488 | tf_op jit(solution)/shard_map/gjfi,fki->gkj/dot_general | solution.py:45
  1594.6 64.8 %all-reduce = (f32[32]{0:T(128)S(1)}, f32[32]{0:T(128)S(1)}) all-reduce(f32[32]{0:T(128)S(1)} %get-tuple-element.14, f32[32]{0:T(128)S(1)} %fusion.93), channel_id=1, replica_groups=mesh['row'=16,'col'=8] {'row','col'}, use_global_device_ids=true, to_apply=%region_28.29 | all-reduce | flops 64 | bytes 512 | tf_op jit(solution)/shard_map/psum | solution.py:76
  (221 shorter events, 199.3 us)
Async XLA Ops:
  7.2 104.4 %all-reduce.14.cloned.1.call-start = ((), (), s32[]{:S(2)}) async-start(), calls=%async_computation | async-start | bytes 131072 | tf_op jit(solution)/shard_map/psum | solution.py:56
  34.4 272.0 %all-reduce.16.cloned.1.call-start = ((), (), s32[]{:S(2)}) async-start(), calls=%async_computation.1 | async-start | bytes 131072 | tf_op jit(solution)/shard_map/psum | solution.py:56
  113.7 41.8 %collective-permute-start = (f32[1,32,512]{2,1,0:T(8,128)}, f32[1,32,512]{2,1,0:T(8,128)S(1)}, u32[]{:S(2)}, u32[]{:S(2)}) collective-permute-start(f32[1,32,512]{2,1,0:T(8,128)} %get-tuple-element.82), channel_id=1, source_target_pairs={{0,8},{8,16},{16,24},{24,32},{32,40},{40,48},{48,56},{56,64},{64,7... | collective-permute-start | bytes 196616 | tf_op jit(solution)/shard_map/ppermute | solution.py:18
  121.7 35.8 %collective-permute-start.3 = (f32[1,32,512]{2,1,0:T(8,128)}, f32[1,32,512]{2,1,0:T(8,128)S(1)}, u32[]{:S(2)}, u32[]{:S(2)}) collective-permute-start(f32[1,32,512]{2,1,0:T(8,128)} %get-tuple-element.83), channel_id=1, source_target_pairs={{1,0},{2,1},{3,2},{4,3},{5,4},{6,5},{7,6},{9,8},{10,9},{11,10},{12... | collective-permute-start | bytes 196616 | tf_op jit(solution)/shard_map/ppermute | solution.py:21
  123.0 35.9 %collective-permute-start.2 = (f32[1,32,512]{2,1,0:T(8,128)}, f32[1,32,512]{2,1,0:T(8,128)S(1)}, u32[]{:S(2)}, u32[]{:S(2)}) collective-permute-start(f32[1,32,512]{2,1,0:T(8,128)} %get-tuple-element.84), channel_id=1, source_target_pairs={{0,1},{1,2},{2,3},{3,4},{4,5},{5,6},{6,7},{8,9},{9,10},{10,11},{11... | collective-permute-start | bytes 196616 | tf_op jit(solution)/shard_map/ppermute | solution.py:18
  128.5 36.1 %collective-permute-start.1 = (f32[1,32,512]{2,1,0:T(8,128)S(1)}, f32[1,32,512]{2,1,0:T(8,128)S(1)}, u32[]{:S(2)}, u32[]{:S(2)}) collective-permute-start(f32[1,32,512]{2,1,0:T(8,128)S(1)} %get-tuple-element.85), channel_id=1, source_target_pairs={{8,0},{16,8},{24,16},{32,24},{40,32},{48,40},{56,48},{64,56},{72,6... | collective-permute-start | bytes 196616 | tf_op jit(solution)/shard_map/ppermute | solution.py:21
  131.4 62.1 %collective-permute-start.8 = (f32[1,32,512]{2,1,0:T(8,128)S(1)}, f32[1,32,512]{2,1,0:T(8,128)S(1)}, u32[]{:S(2)}, u32[]{:S(2)}) collective-permute-start(f32[1,32,512]{2,1,0:T(8,128)S(1)} %get-tuple-element.74), channel_id=1, source_target_pairs={{0,8},{8,16},{16,24},{24,32},{32,40},{40,48},{48,56},{56,64},{64,7... | collective-permute-start | bytes 196616 | tf_op jit(solution)/shard_map/ppermute | solution.py:18
  155.5 39.3 %collective-permute-start.9 = (f32[1,32,512]{2,1,0:T(8,128)S(1)}, f32[1,32,512]{2,1,0:T(8,128)S(1)}, u32[]{:S(2)}, u32[]{:S(2)}) collective-permute-start(f32[1,32,512]{2,1,0:T(8,128)S(1)} %get-tuple-element.75), channel_id=1, source_target_pairs={{8,0},{16,8},{24,16},{32,24},{40,32},{48,40},{56,48},{64,56},{72,6... | collective-permute-start | bytes 196616 | tf_op jit(solution)/shard_map/ppermute | solution.py:21
  157.6 42.7 %collective-permute-start.11 = (f32[1,32,512]{2,1,0:T(8,128)S(1)}, f32[1,32,512]{2,1,0:T(8,128)S(1)}, u32[]{:S(2)}, u32[]{:S(2)}) collective-permute-start(f32[1,32,512]{2,1,0:T(8,128)S(1)} %get-tuple-element.76), channel_id=1, source_target_pairs={{1,0},{2,1},{3,2},{4,3},{5,4},{6,5},{7,6},{9,8},{10,9},{11,10},{12... | collective-permute-start | bytes 196616 | tf_op jit(solution)/shard_map/ppermute | solution.py:21
  158.9 44.0 %collective-permute-start.10 = (f32[1,32,512]{2,1,0:T(8,128)S(1)}, f32[1,32,512]{2,1,0:T(8,128)S(1)}, u32[]{:S(2)}, u32[]{:S(2)}) collective-permute-start(f32[1,32,512]{2,1,0:T(8,128)S(1)} %get-tuple-element.77), channel_id=1, source_target_pairs={{0,1},{1,2},{2,3},{3,4},{4,5},{5,6},{6,7},{8,9},{9,10},{10,11},{11... | collective-permute-start | bytes 196616 | tf_op jit(solution)/shard_map/ppermute | solution.py:18
  189.3 13.6 collective-permute-start.4
  193.5 9.4 collective-permute-start.7
  194.8 8.1 collective-permute-start.6
  230.5 324.2 %all-reduce.18.cloned.1.call-start = ((), (), s32[]{:S(2)}) async-start(), calls=%async_computation.2 | async-start | bytes 131072 | tf_op jit(solution)/shard_map/psum | solution.py:56
  307.6 17.4 %collective-permute-start.12 = (f32[1,32,512]{2,1,0:T(8,128)S(1)}, f32[1,32,512]{2,1,0:T(8,128)S(1)}, u32[]{:S(2)}, u32[]{:S(2)}) collective-permute-start(f32[1,32,512]{2,1,0:T(8,128)S(1)} %get-tuple-element.70), channel_id=1, source_target_pairs={{0,8},{8,16},{16,24},{24,32},{32,40},{40,48},{48,56},{56,64},{64,7... | collective-permute-start | bytes 196616 | tf_op jit(solution)/shard_map/ppermute | solution.py:18
  315.6 9.4 collective-permute-start.15
  316.9 8.1 collective-permute-start.14
  442.3 11.9 collective-permute-start.16
  445.4 8.7 collective-permute-start.19
  446.7 7.5 collective-permute-start.18
  481.0 321.8 %all-reduce.20.cloned.1.call-start = ((), (), s32[]{:S(2)}) async-start(), calls=%async_computation.3 | async-start | bytes 131072 | tf_op jit(solution)/shard_map/psum | solution.py:56
  555.9 16.7 %collective-permute-start.20 = (f32[1,32,512]{2,1,0:T(8,128)S(1)}, f32[1,32,512]{2,1,0:T(8,128)S(1)}, u32[]{:S(2)}, u32[]{:S(2)}) collective-permute-start(f32[1,32,512]{2,1,0:T(8,128)S(1)} %get-tuple-element.62), channel_id=1, source_target_pairs={{0,8},{8,16},{16,24},{24,32},{32,40},{40,48},{48,56},{56,64},{64,7... | collective-permute-start | bytes 196616 | tf_op jit(solution)/shard_map/ppermute | solution.py:18
  563.9 8.7 collective-permute-start.23
  565.2 7.5 collective-permute-start.22
  689.2 11.9 collective-permute-start.24
  692.3 8.7 collective-permute-start.27
  693.6 7.5 collective-permute-start.26
  729.1 324.1 %all-reduce.22.cloned.1.call-start = ((), (), s32[]{:S(2)}) async-start(), calls=%async_computation.4 | async-start | bytes 131072 | tf_op jit(solution)/shard_map/psum | solution.py:56
  804.0 16.7 %collective-permute-start.28 = (f32[1,32,512]{2,1,0:T(8,128)S(1)}, f32[1,32,512]{2,1,0:T(8,128)S(1)}, u32[]{:S(2)}, u32[]{:S(2)}) collective-permute-start(f32[1,32,512]{2,1,0:T(8,128)S(1)} %get-tuple-element.54), channel_id=1, source_target_pairs={{0,8},{8,16},{16,24},{24,32},{32,40},{40,48},{48,56},{56,64},{64,7... | collective-permute-start | bytes 196616 | tf_op jit(solution)/shard_map/ppermute | solution.py:18
  812.0 8.7 collective-permute-start.31
  813.3 7.5 collective-permute-start.30
  940.6 11.9 collective-permute-start.32
  943.8 8.7 collective-permute-start.35
  945.1 7.5 collective-permute-start.34
  979.4 322.5 %all-reduce.24.cloned.1.call-start = ((), (), s32[]{:S(2)}) async-start(), calls=%async_computation.5 | async-start | bytes 131072 | tf_op jit(solution)/shard_map/psum | solution.py:56
  1054.4 16.7 %collective-permute-start.36 = (f32[1,32,512]{2,1,0:T(8,128)S(1)}, f32[1,32,512]{2,1,0:T(8,128)S(1)}, u32[]{:S(2)}, u32[]{:S(2)}) collective-permute-start(f32[1,32,512]{2,1,0:T(8,128)S(1)} %get-tuple-element.46), channel_id=1, source_target_pairs={{0,8},{8,16},{16,24},{24,32},{32,40},{40,48},{48,56},{56,64},{64,7... | collective-permute-start | bytes 196616 | tf_op jit(solution)/shard_map/ppermute | solution.py:18
  1062.4 8.7 collective-permute-start.39
  1063.7 7.5 collective-permute-start.38
  1187.8 11.9 collective-permute-start.40
  1191.0 8.7 collective-permute-start.43
  1228.2 322.2 %all-reduce.26.cloned.1.call-start = ((), (), s32[]{:S(2)}) async-start(), calls=%async_computation.6 | async-start | bytes 131072 | tf_op jit(solution)/shard_map/psum | solution.py:56
  1303.1 16.7 %collective-permute-start.44 = (f32[1,32,512]{2,1,0:T(8,128)S(1)}, f32[1,32,512]{2,1,0:T(8,128)S(1)}, u32[]{:S(2)}, u32[]{:S(2)}) collective-permute-start(f32[1,32,512]{2,1,0:T(8,128)S(1)} %get-tuple-element.38), channel_id=1, source_target_pairs={{0,8},{8,16},{16,24},{24,32},{32,40},{40,48},{48,56},{56,64},{64,7... | collective-permute-start | bytes 196616 | tf_op jit(solution)/shard_map/ppermute | solution.py:18
  1311.1 8.7 collective-permute-start.47
  1438.5 11.9 collective-permute-start.48
  1441.7 8.7 collective-permute-start.51
  1443.0 7.5 collective-permute-start.50
  1551.7 16.7 %collective-permute-start.52 = (f32[1,32,512]{2,1,0:T(8,128)S(1)}, f32[1,32,512]{2,1,0:T(8,128)S(1)}, u32[]{:S(2)}, u32[]{:S(2)}) collective-permute-start(f32[1,32,512]{2,1,0:T(8,128)S(1)} %get-tuple-element.30), channel_id=1, source_target_pairs={{0,8},{8,16},{16,24},{24,32},{32,40},{40,48},{48,56},{56,64},{64,7... | collective-permute-start | bytes 196616 | tf_op jit(solution)/shard_map/ppermute | solution.py:18
  1559.6 8.7 collective-permute-start.55
  (34 other events, 1422.9 us)
Sparse Core Ops, SparseCore 0:
  34.6 77.0 all-reduce.13
  230.6 75.7 all-reduce.15
  481.1 73.5 all-reduce.17
  729.2 73.5 all-reduce.19
  979.5 73.6 all-reduce.21
  1228.4 73.5 all-reduce.23
  1476.9 73.5 all-reduce.25
where the time goes:
time: 1670 us
  waiting for transfers between devices  564 us (34%)
  blocking collectives  527 us (32%)
  matrix products  314 us (19%)
  starting transfers between devices  202 us (12%)
  local copies, waits for them, and re-layouts  33.4 us (2%)
    psum x7, waiting for transfers between devices, coarse(): summed = lax.psum(partial_amps, 'col')  521 us
    psum x6, blocking collectives, shards(): numer_all, denom_all = lax.psum((numer, denom), ('row', 'col'))  390 us
    dot_general x12, matrix products, apply_dual(): return jnp.einsum('gjfi,fki->gkj', blocks, vector, precision=HIGH)  283 us
    ppermute x28, starting transfers between devices, padded(): lax.ppermute(lax.slice_in_dim(block, block.shape[dim] - width, None, axis...  157 us
    all_gather x7, blocking collectives, coarse(): gathered = lax.all_gather(coef, 'row', axis=1, tiled=True)  137 us
    ppermute x28, starting transfers between devices, padded(): lax.ppermute(lax.slice_in_dim(block, 0, width, axis=dim), axis, backward)  45.1 us
    ppermute x28, waiting for transfers between devices, padded(): lax.ppermute(lax.slice_in_dim(block, 0, width, axis=dim), axis, backward)  42.8 us
  transfers between devices with their start and end apart: 63, of which 19 were waited for; matrix products, arithmetic and copies ran while one was open for 3% of the time, Pallas kernels for 0%

commit v1 on v0

v1 whole, which is shorter than its diff:
```python
import functools

import jax
import jax.numpy as jnp
from jax import lax
from jax.experimental import pallas as pl
from jax.experimental.pallas import tpu as pltpu
from jax.sharding import PartitionSpec as P

MDEV = 64
ITERS = 6
K = 32
FACE = 512
M = 4 * FACE
VMEM_LIMIT = 20 << 20

F32 = jnp.float32
BF16 = jnp.bfloat16


def split(x):
    hi = x.astype(BF16)
    return hi, (x - hi.astype(F32)).astype(BF16)


def call(kernel, outs, *args, scratch=(), smem=()):
    specs = [
        pl.BlockSpec(memory_space=pltpu.SMEM if i in smem else pltpu.VMEM)
        for i in range(len(args))
    ]
    return pl.pallas_call(
        kernel,
        out_shape=[jax.ShapeDtypeStruct(shape, dtype) for shape, dtype in outs],
        in_specs=specs,
        out_specs=[pl.BlockSpec(memory_space=pltpu.VMEM)] * len(outs),
        scratch_shapes=[pltpu.VMEM(shape, dtype) for shape, dtype in scratch],
        compiler_params=pltpu.CompilerParams(vmem_limit_bytes=VMEM_LIMIT),
    )(*args)


def split_kernel(x_ref, hi_ref, lo_ref):
    hi_ref[...], lo_ref[...] = split(x_ref[...])


def split_operator(dual):
    rows = 256
    return pl.pallas_call(
        split_kernel,
        grid=(M // rows,),
        out_shape=[jax.ShapeDtypeStruct((M, M), BF16)] * 2,
        in_specs=[pl.BlockSpec((rows, M), lambda i: (i, 0))],
        out_specs=[pl.BlockSpec((rows, M), lambda i: (i, 0))] * 2,
        compiler_params=pltpu.CompilerParams(vmem_limit_bytes=VMEM_LIMIT),
    )(dual)


def split_t_kernel(x_ref, hi_ref, lo_ref):
    hi_ref[...], lo_ref[...] = split(x_ref[...].T)


def split_tile(tile):
    rows, cols = tile.shape
    step = 256
    return pl.pallas_call(
        split_t_kernel,
        grid=(cols // step,),
        out_shape=[jax.ShapeDtypeStruct((cols, rows), BF16)] * 2,
        in_specs=[pl.BlockSpec((rows, step), lambda i: (0, i))],
        out_specs=[pl.BlockSpec((step, rows), lambda i: (i, 0))] * 2,
        compiler_params=pltpu.CompilerParams(vmem_limit_bytes=VMEM_LIMIT),
    )(tile)


def weights_kernel(has_ref, basis_ref, gap_ref, n0, n1, n2, n3, exp_ref, res_ref, dvec_ref):
    for f, n_ref in enumerate((n0, n1, n2, n3)):
        own = basis_ref[f]
        there = has_ref[f] != 0
        nb = jnp.where(there, n_ref[0:MDEV, :], 0.0)
        both = jnp.concatenate([own, nb] if f < 2 else [nb, own], axis=0)
        hi, lo = split(both)
        exp_ref[f, 0:128, :] = hi
        exp_ref[f, 128:256, :] = lo
        hi, lo = split(own)
        pair = jnp.concatenate([hi.astype(F32), lo.astype(F32)], axis=0)
        res_ref[f * FACE : (f + 1) * FACE, :] = pair.T.astype(BF16)
        dvec_ref[f] = gap_ref[f] + jnp.where(there, n_ref[MDEV : MDEV + K, :], 0.0)


def low_lanes(shape):
    return lax.broadcasted_iota(jnp.int32, shape, len(shape) - 1) < MDEV


def expand_faces(amps_ref, exp_ref):
    total = amps_ref[0]
    for s in range(1, amps_ref.shape[0]):
        total = total + amps_ref[s]
    own_up, left_down, right = total[0:K], total[K : 2 * K], total[2 * K : 3 * K]
    low = low_lanes((K, 128))
    own_high = pltpu.roll(own_up, MDEV, 1)
    sides = (
        own_up,
        jnp.where(low, own_up, left_down),
        jnp.where(low, left_down, own_high),
        jnp.where(low, right, own_high),
    )
    out = []
    for f, side in enumerate(sides):
        hi, lo = split(side)
        lhs = jnp.concatenate(
            [jnp.concatenate([hi, hi], axis=1), jnp.concatenate([lo, lo], axis=1)], axis=0
        )
        res = jnp.dot(lhs, exp_ref[f], preferred_element_type=F32)
        out.append(res[0:K] + res[K : 2 * K])
    return out


def put(lhs, f, value):
    hi, lo = split(value)
    lhs[0:K, f * FACE : (f + 1) * FACE] = hi
    lhs[K : 2 * K, f * FACE : (f + 1) * FACE] = lo


def apply_face(lhs, hi_ref, lo_ref, f):
    cols = slice(f * FACE, (f + 1) * FACE)
    a = jnp.dot(lhs[...], hi_ref[:, cols], preferred_element_type=F32)
    b = jnp.dot(lhs[0:K, :], lo_ref[:, cols], preferred_element_type=F32)
    return a[0:K] + a[K : 2 * K] + b


def first_kernel(amps_ref, exp_ref, hi_ref, lo_ref, m_ref, a0, a1, a2, a3, lhs):
    for f, face in enumerate(expand_faces(amps_ref, exp_ref)):
        m_ref[f] = face
        put(lhs, f, face)
    for f, a_ref in enumerate((a0, a1, a2, a3)):
        a_ref[...] = apply_face(lhs, hi_ref, lo_ref, f)


def step_face(sums_ref, contact_ref, m_ref, p_ref):
    sums = jnp.sum(sums_ref[...], axis=0)
    quot = sums / pltpu.roll(sums, 128 - K, 1)
    rows = lax.broadcasted_iota(jnp.int32, (K, 128), 0)
    lanes = lax.broadcasted_iota(jnp.int32, (K, 128), 1)
    ratio = jnp.sum(jnp.where(rows == lanes, quot, 0.0), axis=1, keepdims=True)
    for f in range(4):
        new = m_ref[f] - ratio * p_ref[f]
        yield f, jnp.where(contact_ref[f : f + 1, :] != 0, jnp.maximum(new, 0.0), new)


def step_kernel(
    sums_ref, contact_ref, m_ref, p_ref, hi_ref, lo_ref, new_ref, a0, a1, a2, a3, lhs
):
    for f, new in step_face(sums_ref, contact_ref, m_ref, p_ref):
        new_ref[f] = new
        put(lhs, f, new)
    for f, a_ref in enumerate((a0, a1, a2, a3)):
        a_ref[...] = apply_face(lhs, hi_ref, lo_ref, f)


def last_kernel(sums_ref, contact_ref, m_ref, p_ref, new_ref):
    for f, new in step_face(sums_ref, contact_ref, m_ref, p_ref):
        new_ref[f] = new


def grad_kernel(
    has_ref, a0, a1, a2, a3, n0, n1, n2, n3, dvec_ref, res_ref, grad_ref, e_ref, lhs
):
    for f, (a_ref, n_ref) in enumerate(((a0, n0), (a1, n1), (a2, n2), (a3, n3))):
        nb = jnp.where(has_ref[f] != 0, n_ref[...], 0.0)
        grad = a_ref[...] + nb - dvec_ref[f]
        grad_ref[f] = grad
        put(lhs, f, grad)
    both = jnp.dot(lhs[...], res_ref[...], preferred_element_type=F32)
    both = both[0:K] + both[K : 2 * K]
    e = both + pltpu.roll(both, MDEV, 1)
    packed = jnp.where(low_lanes((K // 2, 128)), e[0 : K // 2], e[K // 2 : K])
    for s in range(e_ref.shape[0]):
        e_ref[s] = packed


def coarse_kernel(x_ref, uh, ul, oh, ol, dh, dl, out_ref, lhs):
    half = K // 2
    low = low_lanes((half, 128))
    for t in range(x_ref.shape[0] // 2):
        xa, xb = x_ref[2 * t], x_ref[2 * t + 1]
        cols = slice(t * 128, (t + 1) * 128)
        top = jnp.where(low, xa, pltpu.roll(xb, MDEV, 1))
        bottom = jnp.where(low, pltpu.roll(xa, MDEV, 1), xb)
        lhs[0:half, cols], lhs[K : K + half, cols] = split(top)
        lhs[half:K, cols], lhs[K + half : 2 * K, cols] = split(bottom)

    def product(h_ref, l_ref):
        a = jnp.dot(lhs[...], h_ref[...], preferred_element_type=F32)
        b = jnp.dot(lhs[0:K, :], l_ref[...], preferred_element_type=F32)
        full = a[0:K] + a[K : 2 * K] + b
        blocks = [full[:, q * 128 : (q + 1) * 128] for q in range(full.shape[1] // 128)]
        return blocks, [pltpu.roll(b, MDEV, 1) for b in blocks]

    up, up_r = product(uh, ul)
    own, own_r = product(oh, ol)
    down, down_r = product(dh, dl)
    low = low_lanes((K, 128))
    zero = jnp.zeros((K, 128), F32)
    n = len(own)
    for q in range(n):
        even, odd = 2 * q, 2 * q + 1
        out_ref[even, 0:K, :] = jnp.where(low, own[q], up_r[q])
        out_ref[even, K : 2 * K, :] = jnp.where(low, own_r[q - 1] if q > 0 else zero, down_r[q])
        out_ref[even, 2 * K : 3 * K, :] = own_r[q]
        out_ref[odd, 0:K, :] = jnp.where(low, own_r[q], up[q])
        out_ref[odd, K : 2 * K, :] = jnp.where(low, own[q], down[q])
        out_ref[odd, 2 * K : 3 * K, :] = own[q + 1] if q + 1 < n else zero


def image_kernel(has_ref, amps_ref, grad_ref, exp_ref, hi_ref, lo_ref, p_ref, s_ref, lhs):
    numer = jnp.zeros((K, 1), F32)
    for f, face in enumerate(expand_faces(amps_ref, exp_ref)):
        grad = grad_ref[f]
        p = grad - face
        p_ref[f] = p
        put(lhs, f, p)
        weight = jnp.where(has_ref[f] != 0, 0.5, 1.0)
        numer = numer + weight * jnp.sum(grad * p, axis=1, keepdims=True)
    denom = jnp.zeros((K, 1), F32)
    for f in range(4):
        image = apply_face(lhs, hi_ref, lo_ref, f)
        denom = denom + jnp.sum(p_ref[f] * image, axis=1, keepdims=True)
    rows = lax.broadcasted_iota(jnp.int32, (K, 128), 0)
    lanes = lax.broadcasted_iota(jnp.int32, (K, 128), 1)
    placed = jnp.where(rows == lanes, numer, 0.0) + jnp.where(rows + K == lanes, denom, 0.0)
    line = jnp.sum(placed, axis=0, keepdims=True)
    s_ref[...] = jnp.broadcast_to(line[None], s_ref.shape)


def exchange(faces):
    def ring(axis, step):
        n = lax.axis_size(axis)
        return [(i, (i + step) % n) for i in range(n)]

    return (
        lax.ppermute(faces[1], "row", ring("row", 1)),
        lax.ppermute(faces[0], "row", ring("row", -1)),
        lax.ppermute(faces[3], "col", ring("col", 1)),
        lax.ppermute(faces[2], "col", ring("col", -1)),
    )


def shards(dual_ops, basis, coarse_inverse, gap_rhs, coarse_rhs, contact_mask):
    n_rows, n_cols = lax.axis_size("row"), lax.axis_size("col")
    row, col = lax.axis_index("row"), lax.axis_index("col")
    has_nb = jnp.stack([row > 0, row < n_rows - 1, col > 0, col < n_cols - 1]).astype(jnp.int32)
    contact = jnp.where(has_nb[:, None] != 0, 0, (contact_mask[0, 0] == 1).astype(jnp.int32))

    vec = ((4, K, FACE), F32)
    face = ((K, FACE), F32)
    split_lhs = ((2 * K, M), BF16)

    rhs = coarse_rhs[0, 0]
    packed = jnp.concatenate([rhs[: K // 2], rhs[K // 2 :]], axis=1)
    sent = jnp.broadcast_to(packed[None], (n_rows, K // 2, 2 * MDEV))

    both = jnp.concatenate([basis[0, 0], gap_rhs[0, 0]], axis=1)
    nbs = exchange([both[f] for f in range(4)])
    ring = [(i, (i + 1) % n_rows) for i in range(n_rows)]
    up_tile = lax.ppermute(coarse_inverse, "row", ring)
    down_tile = lax.ppermute(coarse_inverse, "row", [(b, a) for a, b in ring])

    hi, lo = split_operator(dual_ops[0, 0])
    exp, res, dvec = call(
        weights_kernel,
        [((4, 256, FACE), BF16), ((M, 128), BF16), vec],
        has_nb, basis[0, 0], gap_rhs[0, 0], *nbs,
        smem=(0,),
    )
    tiles = [*split_tile(up_tile), *split_tile(coarse_inverse), *split_tile(down_tile)]

    def coarse(sent):
        got = lax.all_to_all(sent, "row", 0, 0, tiled=True)
        (parts,) = call(
            coarse_kernel,
            [((n_cols, 3 * K, 128), F32)],
            got, *tiles,
            scratch=[((2 * K, n_rows * MDEV), BF16)],
        )
        return lax.all_to_all(parts, "col", 0, 0, tiled=True)

    amps = coarse(sent)
    multipliers, *applied = call(
        first_kernel, [vec] + [face] * 4, amps, exp, hi, lo, scratch=[split_lhs]
    )
    for step in range(ITERS):
        nbs = exchange(applied)
        grad, sent = call(
            grad_kernel,
            [vec, ((n_rows, K // 2, 128), F32)],
            has_nb, *applied, *nbs, dvec, res,
            scratch=[split_lhs], smem=(0,),
        )
        amps = coarse(sent)
        projected, sums = call(
            image_kernel,
            [vec, ((n_rows * n_cols, 1, 128), F32)],
            has_nb, amps, grad, exp, hi, lo,
            scratch=[split_lhs], smem=(0,),
        )
        sums = lax.all_to_all(sums, ("row", "col"), 0, 0, tiled=True)
        if step + 1 < ITERS:
            multipliers, *applied = call(
                step_kernel, [vec] + [face] * 4, sums, contact, multipliers, projected, hi, lo,
                scratch=[split_lhs],
            )
        else:
            (multipliers,) = call(last_kernel, [vec], sums, contact, multipliers, projected)
    return (multipliers[None, None], projected[None, None])


def solution(mesh):
    return jax.shard_map(
        shards,
        mesh=mesh,
        in_specs=(
            P("row", "col", None, None),
            P("row", "col", None, None, None),
            P("row", "col"),
            P("row", "col", None, None, None),
            P("row", "col", None, None),
            P("row", "col", None, None),
        ),
        out_specs=(P("row", "col", None, None, None), P("row", "col", None, None, None)),
        check_vma=False,
    )
```

time: 1670 us -> 488 us (0.29)
  waiting for transfers between devices: 564 us -> 74.7 us
  blocking collectives: 527 us -> 211 us
  matrix products: 314 us -> 0 us
  starting transfers between devices: 202 us -> 63.2 us
  Pallas kernels: 0 us -> 71.1 us
  local copies, waits for them, and re-layouts: 33.4 us -> 56.2 us
    psum x7 -> x0, waiting for transfers between devices: 521 us -> none  [coarse(): summed = lax.psum(partial_amps, 'col')]
    psum x6 -> x0, blocking collectives: 390 us -> none  [shards(): numer_all, denom_all = lax.psum((numer, denom), ('row', 'col'))]
    dot_general x32 -> x0, matrix products: 314 us -> none  [the longest x12 283 us: apply_dual(): return jnp.einsum('gjfi,fki->gkj', blocks, vector, precision=HIGH)]
    all_to_all x0 -> x17, blocking collectives: none -> 211 us  [the longest x5 73.2 us: shards(): sums = lax.all_to_all(sums, ('row', 'col'), 0, 0, tiled=True)]
    ppermute x56 -> x30, starting transfers between devices: 202 us -> 45 us  [the longest x7 15.2 us: exchange(): lax.ppermute(faces[2], 'col', ring('col', -1))]
    all_gather x7 -> x0, blocking collectives: 137 us -> none  [coarse(): gathered = lax.all_gather(coef, 'row', axis=1, tiled=True)]
    pallas_call x0 -> x31, Pallas kernels: none -> 71.1 us  [the longest x27 62.1 us: call(): pl.pallas_call(kernel, out_shape=[jax.ShapeDtypeStruct(shape, dtype) for...]
    unnamed x45 -> x98, local copies, waits for them, and re-layouts: 8.04 us -> 54.8 us
  transfers between devices with their start and end apart: 63 -> 33, of which waited for: 19 -> 15; matrix products, arithmetic and copies ran while one was open for 3% -> 1% of each run, Pallas kernels for 0% -> 2%
where the time goes in v1:
time: 488 us; the launch traced here: 480 us
  blocking collectives  211 us (43%)
  waiting for transfers between devices  74.7 us (15%)
  Pallas kernels  71.1 us (15%)
  starting transfers between devices  63.2 us (13%)
  local copies, waits for them, and re-layouts  56.2 us (12%)
    all_to_all x5, blocking collectives, shards(): sums = lax.all_to_all(sums, ('row', 'col'), 0, 0, tiled=True)  73.2 us
    all_to_all x6, blocking collectives, coarse(): return lax.all_to_all(parts, 'col', 0, 0, tiled=True)  71.7 us
    all_to_all x6, blocking collectives, coarse(): got = lax.all_to_all(sent, 'row', 0, 0, tiled=True)  65.8 us
    pallas_call x27, Pallas kernels, call(): pl.pallas_call(kernel, out_shape=[jax.ShapeDtypeStruct(shape, dtype) for...  62.1 us
    unnamed x98, local copies, waits for them, and re-layouts  54.8 us
    ppermute x1, waiting for transfers between devices, shards(): up_tile = lax.ppermute(coarse_inverse, 'row', ring)  32.7 us
    ppermute x7, waiting for transfers between devices, exchange(): lax.ppermute(faces[3], 'col', ring('col', 1))  16.4 us
    ppermute x7, starting transfers between devices, exchange(): lax.ppermute(faces[2], 'col', ring('col', -1))  15.2 us
  transfers between devices with their start and end apart: 33, of which 15 were waited for; matrix products, arithmetic and copies ran while one was open for 1% of the time, Pallas kernels for 2%

profile of v1, /device:TPU:1, one launch (start us, length us, event | category | flops | bytes accessed | tf_op | source)
XLA Modules:
  0.0 479.6 jit_solution(11153974910659238850)
XLA Ops:
  4.8 6.1 %all-to-all-start = ((f32[16,16,128]{2,1,0:T(8,128)}), f32[16,16,128]{2,1,0:T(8,128)S(1)}, u32[]{:S(2)}, u32[]{:S(2)}) async-start(f32[16,16,128]{2,1,0:T(8,128)} %broadcast_in_dim.25), calls=%async_computation | async-start | bytes 262144 | tf_op jit(solution)/shard_map/all_to_all | solution.py:277
  13.5 32.7 %collective-permute-done.x_ref = f32[512,1024]{1,0:T(8,128)} collective-permute-done((f32[512,1024]{1,0:T(8,128)}, f32[512,1024]{1,0:T(8,128)}, u32[]{:S(2)}, u32[]{:S(2)}) %collective-permute-start) | collective-permute-done | bytes 2097184 | tf_op jit(solution)/shard_map/ppermute | solution.py:264
  62.2 7.0 %all-to-all-start.1 = ((f32[8,96,128]{2,1,0:T(8,128)}), f32[8,96,128]{2,1,0:T(8,128)}, u32[]{:S(2)}, u32[]{:S(2)}) async-start(f32[8,96,128]{2,1,0:T(8,128)} %shard_map.80), calls=%async_computation.1 | async-start | bytes 786432 | tf_op jit(solution)/shard_map/all_to_all | solution.py:284
  71.2 5.1 %collective-permute-start.5 = (f32[96,512]{1,0:T(8,128)}, f32[96,512]{1,0:T(8,128)S(1)}, u32[]{:S(2)}, u32[]{:S(2)}) collective-permute-start(f32[96,512]{1,0:T(8,128)} %get-tuple-element.134), channel_id=1, source_target_pairs={{0,7},{1,0},{2,1},{3,2},{4,3},{5,4},{6,5},{7,6},{8,15},{9,8},{10,9... | collective-permute-start | bytes 589832 | tf_op jit(solution)/shard_map/ppermute | solution.py:243
  77.0 3.3 collective-permute-start.3
  80.4 5.8 %copy-done.29 = f32[1,1,2048,2048]{3,2,1,0:T(8,128)S(1)} copy-done((f32[1,1,2048,2048]{3,2,1,0:T(8,128)S(1)}, f32[1,1,2048,2048]{3,2,1,0:T(8,128)}, u32[]{:S(2)}) %copy-start.29) | copy-done | bytes 16777240
  88.6 3.3 copy-done
  91.9 3.3 copy-done.5
  101.7 3.4 copy-done.1
  105.1 3.4 copy-done.6
  109.7 4.4 shard_map.83
  114.1 3.9 collective-permute-start.7
  118.0 5.4 %collective-permute-start.9 = (f32[32,512]{1,0:T(8,128)S(1)}, f32[32,512]{1,0:T(8,128)S(1)}, u32[]{:S(2)}, u32[]{:S(2)}) collective-permute-start(f32[32,512]{1,0:T(8,128)S(1)} %get-tuple-element.78.a2), channel_id=1, source_target_pairs={{0,7},{1,0},{2,1},{3,2},{4,3},{5,4},{6,5},{7,6},{8,15},{9,8},{10,9... | collective-permute-start | bytes 196616 | tf_op jit(solution)/shard_map/ppermute | solution.py:243
  124.7 5.4 %collective-permute-done.8.n2 = f32[32,512]{1,0:T(8,128)S(1)} collective-permute-done((f32[32,512]{1,0:T(8,128)S(1)}, f32[32,512]{1,0:T(8,128)S(1)}, u32[]{:S(2)}, u32[]{:S(2)}) %collective-permute-start.8) | collective-permute-done | bytes 65568 | tf_op jit(solution)/shard_map/ppermute | solution.py:242
  131.0 11.4 %all_to_all.100.x_ref = f32[16,16,128]{2,1,0:T(8,128)S(1)} all-to-all(f32[16,16,128]{2,1,0:T(8,128)S(1)} %get-tuple-element.82), channel_id=1, replica_groups=mesh['row'=16,'col'=8] {'row'}, dimensions={0} | all-to-all | bytes 262144 | tf_op jit(solution)/shard_map/all_to_all | solution.py:277
  143.8 12.2 %all_to_all.101.amps_ref = f32[8,96,128]{2,1,0:T(8,128)S(1)} all-to-all(f32[8,96,128]{2,1,0:T(8,128)S(1)} %shard_map.85), channel_id=1, replica_groups=mesh['row'=16,'col'=8] {'col'}, dimensions={0} | all-to-all | bytes 786432 | tf_op jit(solution)/shard_map/all_to_all | solution.py:284
  156.0 3.9 shard_map.86
  161.2 5.2 %all-to-all-start.4 = ((f32[128,1,128]{2,1,0:T(1,128)}), f32[128,1,128]{2,1,0:T(1,128)S(1)}, u32[]{:S(2)}, u32[]{:S(2)}) async-start(f32[128,1,128]{2,1,0:T(1,128)} %copy-done.43), calls=%async_computation.4 | async-start | bytes 131072 | tf_op jit(solution)/shard_map/all_to_all | solution.py:305
  166.5 9.9 %all-to-all-done.4.sums_ref = f32[128,1,128]{2,1,0:T(1,128)S(1)} async-done(((f32[128,1,128]{2,1,0:T(1,128)}), f32[128,1,128]{2,1,0:T(1,128)S(1)}, u32[]{:S(2)}, u32[]{:S(2)}) %all-to-all-start.4) | async-done | bytes 65568 | tf_op jit(solution)/shard_map/all_to_all | solution.py:305
  176.4 3.4 copy-done.3
  179.8 3.4 copy-done.7
  198.7 10.9 %all_to_all.102.x_ref = f32[16,16,128]{2,1,0:T(8,128)S(1)} all-to-all(f32[16,16,128]{2,1,0:T(8,128)S(1)} %get-tuple-element.91), channel_id=1, replica_groups=mesh['row'=16,'col'=8] {'row'}, dimensions={0} | all-to-all | bytes 262144 | tf_op jit(solution)/shard_map/all_to_all | solution.py:277
  211.0 11.9 %all_to_all.103.amps_ref = f32[8,96,128]{2,1,0:T(8,128)S(1)} all-to-all(f32[8,96,128]{2,1,0:T(8,128)S(1)} %shard_map.89), channel_id=1, replica_groups=mesh['row'=16,'col'=8] {'col'}, dimensions={0} | all-to-all | bytes 786432 | tf_op jit(solution)/shard_map/all_to_all | solution.py:284
  222.8 3.4 copy-done.4
  226.2 3.4 copy-done.8
  229.6 3.9 shard_map.90
  233.5 14.8 %all_to_all.104.sums_ref = f32[128,1,128]{2,1,0:T(1,128)S(1)} all-to-all(f32[128,1,128]{2,1,0:T(1,128)S(1)} %get-tuple-element.93), channel_id=1, replica_groups=mesh['row'=16,'col'=8] {'row','col'}, dimensions={0} | all-to-all | bytes 131072 | tf_op jit(solution)/shard_map/all_to_all | solution.py:305
  248.4 3.4 copy-done.9
  251.7 3.3 shard_map.91
  265.3 10.9 %all_to_all.105.x_ref = f32[16,16,128]{2,1,0:T(8,128)S(1)} all-to-all(f32[16,16,128]{2,1,0:T(8,128)S(1)} %get-tuple-element.100), channel_id=1, replica_groups=mesh['row'=16,'col'=8] {'row'}, dimensions={0} | all-to-all | bytes 262144 | tf_op jit(solution)/shard_map/all_to_all | solution.py:277
  277.6 11.9 %all_to_all.106.amps_ref = f32[8,96,128]{2,1,0:T(8,128)S(1)} all-to-all(f32[8,96,128]{2,1,0:T(8,128)S(1)} %shard_map.93), channel_id=1, replica_groups=mesh['row'=16,'col'=8] {'col'}, dimensions={0} | all-to-all | bytes 786432 | tf_op jit(solution)/shard_map/all_to_all | solution.py:284
  289.4 3.9 shard_map.94
  293.3 14.6 %all_to_all.107.sums_ref = f32[128,1,128]{2,1,0:T(1,128)S(1)} all-to-all(f32[128,1,128]{2,1,0:T(1,128)S(1)} %get-tuple-element.102), channel_id=1, replica_groups=mesh['row'=16,'col'=8] {'row','col'}, dimensions={0} | all-to-all | bytes 131072 | tf_op jit(solution)/shard_map/all_to_all | solution.py:305
  307.9 3.3 shard_map.95
  321.7 10.9 %all_to_all.108.x_ref = f32[16,16,128]{2,1,0:T(8,128)S(1)} all-to-all(f32[16,16,128]{2,1,0:T(8,128)S(1)} %get-tuple-element.109), channel_id=1, replica_groups=mesh['row'=16,'col'=8] {'row'}, dimensions={0} | all-to-all | bytes 262144 | tf_op jit(solution)/shard_map/all_to_all | solution.py:277
  333.9 11.7 %all_to_all.109.amps_ref = f32[8,96,128]{2,1,0:T(8,128)S(1)} all-to-all(f32[8,96,128]{2,1,0:T(8,128)S(1)} %shard_map.97), channel_id=1, replica_groups=mesh['row'=16,'col'=8] {'col'}, dimensions={0} | all-to-all | bytes 786432 | tf_op jit(solution)/shard_map/all_to_all | solution.py:284
  345.6 3.9 shard_map.98
  349.5 14.7 %all_to_all.110.sums_ref = f32[128,1,128]{2,1,0:T(1,128)S(1)} all-to-all(f32[128,1,128]{2,1,0:T(1,128)S(1)} %get-tuple-element.111), channel_id=1, replica_groups=mesh['row'=16,'col'=8] {'row','col'}, dimensions={0} | all-to-all | bytes 131072 | tf_op jit(solution)/shard_map/all_to_all | solution.py:305
  364.2 3.3 shard_map.99
  377.8 10.9 %all_to_all.111.x_ref = f32[16,16,128]{2,1,0:T(8,128)S(1)} all-to-all(f32[16,16,128]{2,1,0:T(8,128)S(1)} %get-tuple-element.118), channel_id=1, replica_groups=mesh['row'=16,'col'=8] {'row'}, dimensions={0} | all-to-all | bytes 262144 | tf_op jit(solution)/shard_map/all_to_all | solution.py:277
  390.0 12.1 %all_to_all.112.amps_ref = f32[8,96,128]{2,1,0:T(8,128)S(1)} all-to-all(f32[8,96,128]{2,1,0:T(8,128)S(1)} %shard_map.101), channel_id=1, replica_groups=mesh['row'=16,'col'=8] {'col'}, dimensions={0} | all-to-all | bytes 786432 | tf_op jit(solution)/shard_map/all_to_all | solution.py:284
  402.1 3.9 shard_map.102
  406.0 14.6 %all_to_all.113.sums_ref = f32[128,1,128]{2,1,0:T(1,128)S(1)} all-to-all(f32[128,1,128]{2,1,0:T(1,128)S(1)} %get-tuple-element.120), channel_id=1, replica_groups=mesh['row'=16,'col'=8] {'row','col'}, dimensions={0} | all-to-all | bytes 131072 | tf_op jit(solution)/shard_map/all_to_all | solution.py:305
  420.6 3.3 shard_map.103
  434.2 10.9 %all_to_all.114.x_ref = f32[16,16,128]{2,1,0:T(8,128)S(1)} all-to-all(f32[16,16,128]{2,1,0:T(8,128)S(1)} %get-tuple-element.127), channel_id=1, replica_groups=mesh['row'=16,'col'=8] {'row'}, dimensions={0} | all-to-all | bytes 262144 | tf_op jit(solution)/shard_map/all_to_all | solution.py:277
  446.4 11.9 %all_to_all.115.amps_ref = f32[8,96,128]{2,1,0:T(8,128)S(1)} all-to-all(f32[8,96,128]{2,1,0:T(8,128)S(1)} %shard_map.105), channel_id=1, replica_groups=mesh['row'=16,'col'=8] {'col'}, dimensions={0} | all-to-all | bytes 786432 | tf_op jit(solution)/shard_map/all_to_all | solution.py:284
  458.3 4.3 shard_map.106
  462.6 14.5 %all_to_all.116.sums_ref = f32[128,1,128]{2,1,0:T(1,128)S(1)} all-to-all(f32[128,1,128]{2,1,0:T(1,128)S(1)} %get-tuple-element.129), channel_id=1, replica_groups=mesh['row'=16,'col'=8] {'row','col'}, dimensions={0} | all-to-all | bytes 131072 | tf_op jit(solution)/shard_map/all_to_all | solution.py:305
  (172 shorter events, 106.0 us)
Async XLA Ops:
  0.6 68.5 %copy-start.32 = (f32[1,1,4,32,512]{4,3,2,1,0:T(8,128)S(1)}, f32[1,1,4,32,512]{4,3,2,1,0:T(8,128)}, u32[]{:S(2)}) copy-start(f32[1,1,4,32,512]{4,3,2,1,0:T(8,128)} %param.9) | copy-start | bytes 786436
  0.6 45.5 %collective-permute-start = (f32[512,1024]{1,0:T(8,128)}, f32[512,1024]{1,0:T(8,128)}, u32[]{:S(2)}, u32[]{:S(2)}) collective-permute-start(f32[512,1024]{1,0:T(8,128)} %x_ref.1), channel_id=1, source_target_pairs={{0,8},{8,16},{16,24},{24,32},{32,40},{40,48},{48,56},{56,64},{64,7... | collective-permute-start | bytes 6291464 | tf_op jit(solution)/shard_map/ppermute | solution.py:264
  3.3 48.4 %collective-permute-start.1 = (f32[512,1024]{1,0:T(8,128)}, f32[512,1024]{1,0:T(8,128)}, u32[]{:S(2)}, u32[]{:S(2)}) collective-permute-start(f32[512,1024]{1,0:T(8,128)} %x_ref.1), channel_id=1, source_target_pairs={{8,0},{16,8},{24,16},{32,24},{40,32},{48,40},{56,48},{64,56},{72,6... | collective-permute-start | bytes 6291464 | tf_op jit(solution)/shard_map/ppermute | solution.py:265
  4.8 51.6 %all-to-all-start = ((f32[16,16,128]{2,1,0:T(8,128)}), f32[16,16,128]{2,1,0:T(8,128)S(1)}, u32[]{:S(2)}, u32[]{:S(2)}) async-start(f32[16,16,128]{2,1,0:T(8,128)} %broadcast_in_dim.25), calls=%async_computation | async-start | bytes 262144 | tf_op jit(solution)/shard_map/all_to_all | solution.py:277
  62.2 39.6 %all-to-all-start.1 = ((f32[8,96,128]{2,1,0:T(8,128)}), f32[8,96,128]{2,1,0:T(8,128)}, u32[]{:S(2)}, u32[]{:S(2)}) async-start(f32[8,96,128]{2,1,0:T(8,128)} %shard_map.80), calls=%async_computation.1 | async-start | bytes 786432 | tf_op jit(solution)/shard_map/all_to_all | solution.py:284
  71.2 24.2 %collective-permute-start.5 = (f32[96,512]{1,0:T(8,128)}, f32[96,512]{1,0:T(8,128)S(1)}, u32[]{:S(2)}, u32[]{:S(2)}) collective-permute-start(f32[96,512]{1,0:T(8,128)} %get-tuple-element.134), channel_id=1, source_target_pairs={{0,7},{1,0},{2,1},{3,2},{4,3},{5,4},{6,5},{7,6},{8,15},{9,8},{10,9... | collective-permute-start | bytes 589832 | tf_op jit(solution)/shard_map/ppermute | solution.py:243
  76.2 19.8 %collective-permute-start.2 = (f32[96,512]{1,0:T(8,128)}, f32[96,512]{1,0:T(8,128)S(1)}, u32[]{:S(2)}, u32[]{:S(2)}) collective-permute-start(f32[96,512]{1,0:T(8,128)} %get-tuple-element.135), channel_id=1, source_target_pairs={{0,8},{8,16},{16,24},{24,32},{32,40},{40,48},{48,56},{56,64},{64,7... | collective-permute-start | bytes 589832 | tf_op jit(solution)/shard_map/ppermute | solution.py:240
  77.0 19.7 %collective-permute-start.3 = (f32[96,512]{1,0:T(8,128)}, f32[96,512]{1,0:T(8,128)}, u32[]{:S(2)}, u32[]{:S(2)}) collective-permute-start(f32[96,512]{1,0:T(8,128)} %get-tuple-element.136), channel_id=1, source_target_pairs={{0,120},{8,0},{16,8},{24,16},{32,24},{40,32},{48,40},{56,48},{64,5... | collective-permute-start | bytes 589832 | tf_op jit(solution)/shard_map/ppermute | solution.py:241
  80.4 16.4 %collective-permute-start.4 = (f32[96,512]{1,0:T(8,128)}, f32[96,512]{1,0:T(8,128)}, u32[]{:S(2)}, u32[]{:S(2)}) collective-permute-start(f32[96,512]{1,0:T(8,128)} %get-tuple-element.137), channel_id=1, source_target_pairs={{0,1},{1,2},{2,3},{3,4},{4,5},{5,6},{6,7},{7,0},{8,9},{9,10},{10,1... | collective-permute-start | bytes 589832 | tf_op jit(solution)/shard_map/ppermute | solution.py:242
  109.7 20.4 %copy-start.27 = (bf16[2048,128]{1,0:T(8,128)(2,1)S(1)}, bf16[2048,128]{1,0:T(8,128)(2,1)}, u32[]{:S(2)}) copy-start(bf16[2048,128]{1,0:T(8,128)(2,1)} %copy-done.26) | copy-start | bytes 1572868
  109.7 32.7 %copy-start.12 = (bf16[1024,512]{1,0:T(8,128)(2,1)S(1)}, bf16[1024,512]{1,0:T(8,128)(2,1)}, u32[]{:S(2)}) copy-start(bf16[1024,512]{1,0:T(8,128)(2,1)} %copy-done.10) | copy-start | bytes 3145732
  109.7 32.7 %copy-start.16 = (bf16[1024,512]{1,0:T(8,128)(2,1)S(1)}, bf16[1024,512]{1,0:T(8,128)(2,1)}, u32[]{:S(2)}) copy-start(bf16[1024,512]{1,0:T(8,128)(2,1)} %copy-done.14) | copy-start | bytes 3145732
  109.7 32.7 %copy-start.20 = (bf16[1024,512]{1,0:T(8,128)(2,1)S(1)}, bf16[1024,512]{1,0:T(8,128)(2,1)}, u32[]{:S(2)}) copy-start(bf16[1024,512]{1,0:T(8,128)(2,1)} %copy-done.18) | copy-start | bytes 3145732
  109.7 46.2 %copy-start.24 = (bf16[4,256,512]{2,1,0:T(8,128)(2,1)S(1)}, bf16[4,256,512]{2,1,0:T(8,128)(2,1)}, u32[]{:S(2)}) copy-start(bf16[4,256,512]{2,1,0:T(8,128)(2,1)} %copy-done.22) | copy-start | bytes 3145732
  114.1 28.3 %copy-start.34 = (f32[4,32,512]{2,1,0:T(8,128)}, f32[4,32,512]{2,1,0:T(8,128)S(1)}, u32[]{:S(2)}) copy-start(f32[4,32,512]{2,1,0:T(8,128)S(1)} %get-tuple-element.85.m_ref) | copy-start | bytes 786436
  114.1 41.9 %copy-start.2 = (bf16[2048,2048]{1,0:T(8,128)(2,1)S(1)}, bf16[2048,2048]{1,0:T(8,128)(2,1)}, u32[]{:S(2)}) copy-start(bf16[2048,2048]{1,0:T(8,128)(2,1)} %copy-done) | copy-start | bytes 25165828
  114.1 9.3 %collective-permute-start.7 = (f32[32,512]{1,0:T(8,128)S(1)}, f32[32,512]{1,0:T(8,128)S(1)}, u32[]{:S(2)}, u32[]{:S(2)}) collective-permute-start(f32[32,512]{1,0:T(8,128)S(1)} %get-tuple-element.76.a0), channel_id=1, source_target_pairs={{0,120},{8,0},{16,8},{24,16},{32,24},{40,32},{48,40},{56,48},{64,5... | collective-permute-start | bytes 196616 | tf_op jit(solution)/shard_map/ppermute | solution.py:241
  118.0 5.4 %collective-permute-start.6 = (f32[32,512]{1,0:T(8,128)S(1)}, f32[32,512]{1,0:T(8,128)S(1)}, u32[]{:S(2)}, u32[]{:S(2)}) collective-permute-start(f32[32,512]{1,0:T(8,128)S(1)} %get-tuple-element.77.a1), channel_id=1, source_target_pairs={{0,8},{8,16},{16,24},{24,32},{32,40},{40,48},{48,56},{56,64},{64,7... | collective-permute-start | bytes 196616 | tf_op jit(solution)/shard_map/ppermute | solution.py:240
  118.0 6.7 %collective-permute-start.9 = (f32[32,512]{1,0:T(8,128)S(1)}, f32[32,512]{1,0:T(8,128)S(1)}, u32[]{:S(2)}, u32[]{:S(2)}) collective-permute-start(f32[32,512]{1,0:T(8,128)S(1)} %get-tuple-element.78.a2), channel_id=1, source_target_pairs={{0,7},{1,0},{2,1},{3,2},{4,3},{5,4},{6,5},{7,6},{8,15},{9,8},{10,9... | collective-permute-start | bytes 196616 | tf_op jit(solution)/shard_map/ppermute | solution.py:243
  123.4 6.7 %collective-permute-start.8 = (f32[32,512]{1,0:T(8,128)S(1)}, f32[32,512]{1,0:T(8,128)S(1)}, u32[]{:S(2)}, u32[]{:S(2)}) collective-permute-start(f32[32,512]{1,0:T(8,128)S(1)} %get-tuple-element.79.a3), channel_id=1, source_target_pairs={{0,1},{1,2},{2,3},{3,4},{4,5},{5,6},{6,7},{7,0},{8,9},{9,10},{10,1... | collective-permute-start | bytes 196616 | tf_op jit(solution)/shard_map/ppermute | solution.py:242
  161.2 15.2 %all-to-all-start.4 = ((f32[128,1,128]{2,1,0:T(1,128)}), f32[128,1,128]{2,1,0:T(1,128)S(1)}, u32[]{:S(2)}, u32[]{:S(2)}) async-start(f32[128,1,128]{2,1,0:T(1,128)} %copy-done.43), calls=%async_computation.4 | async-start | bytes 131072 | tf_op jit(solution)/shard_map/all_to_all | solution.py:305
  185.1 24.5 %copy-start.13 = (bf16[1024,512]{1,0:T(8,128)(2,1)S(1)}, bf16[1024,512]{1,0:T(8,128)(2,1)}, u32[]{:S(2)}) copy-start(bf16[1024,512]{1,0:T(8,128)(2,1)} %copy-done.10) | copy-start | bytes 3145732
  185.1 24.5 %copy-start.17 = (bf16[1024,512]{1,0:T(8,128)(2,1)S(1)}, bf16[1024,512]{1,0:T(8,128)(2,1)}, u32[]{:S(2)}) copy-start(bf16[1024,512]{1,0:T(8,128)(2,1)} %copy-done.14) | copy-start | bytes 3145732
  185.1 24.5 %copy-start.21 = (bf16[1024,512]{1,0:T(8,128)(2,1)S(1)}, bf16[1024,512]{1,0:T(8,128)(2,1)}, u32[]{:S(2)}) copy-start(bf16[1024,512]{1,0:T(8,128)(2,1)} %copy-done.18) | copy-start | bytes 3145732
  188.4 34.4 %copy-start.25 = (bf16[4,256,512]{2,1,0:T(8,128)(2,1)S(1)}, bf16[4,256,512]{2,1,0:T(8,128)(2,1)}, u32[]{:S(2)}) copy-start(bf16[4,256,512]{2,1,0:T(8,128)(2,1)} %copy-done.22) | copy-start | bytes 3145732
  188.4 4.7 collective-permute-start.11
  188.8 4.4 collective-permute-start.10
  190.2 5.6 %collective-permute-start.13 = (f32[32,512]{1,0:T(8,128)S(1)}, f32[32,512]{1,0:T(8,128)S(1)}, u32[]{:S(2)}, u32[]{:S(2)}) collective-permute-start(f32[32,512]{1,0:T(8,128)S(1)} %get-tuple-element.89.a2), channel_id=1, source_target_pairs={{0,7},{1,0},{2,1},{3,2},{4,3},{5,4},{6,5},{7,6},{8,15},{9,8},{10,9... | collective-permute-start | bytes 196616 | tf_op jit(solution)/shard_map/ppermute | solution.py:243
  191.2 6.7 %collective-permute-start.12 = (f32[32,512]{1,0:T(8,128)S(1)}, f32[32,512]{1,0:T(8,128)S(1)}, u32[]{:S(2)}, u32[]{:S(2)}) collective-permute-start(f32[32,512]{1,0:T(8,128)S(1)} %get-tuple-element.90.a3), channel_id=1, source_target_pairs={{0,1},{1,2},{2,3},{3,4},{4,5},{5,6},{6,7},{7,0},{8,9},{9,10},{10,1... | collective-permute-start | bytes 196616 | tf_op jit(solution)/shard_map/ppermute | solution.py:242
  209.6 38.7 %slice-start = ((s8[8388608]{0:T(1024)(128)(4,1)}), s8[4194304]{0:T(1024)(128)(4,1)S(1)}, s32[]{:S(2)}) async-start(s8[8388608]{0:T(1024)(128)(4,1)} %bitcast.23), calls=%async_computation.20 | async-start | bytes 8388608
  229.6 59.8 %slice-start.2 = ((s8[8388608]{0:T(1024)(128)(4,1)}), s8[4194304]{0:T(1024)(128)(4,1)S(1)}, s32[]{:S(2)}) async-start(s8[8388608]{0:T(1024)(128)(4,1)} %bitcast.25), calls=%async_computation.22 | async-start | bytes 8388608
  251.7 37.7 %slice-start.3 = ((s8[8388608]{0:T(1024)(128)(4,1)}), s8[4194304]{0:T(1024)(128)(4,1)S(1)}, s32[]{:S(2)}) async-start(s8[8388608]{0:T(1024)(128)(4,1)} %bitcast.25), calls=%async_computation.23 | async-start | bytes 8388608
  255.0 4.7 collective-permute-start.15
  255.4 4.4 collective-permute-start.14
  256.8 5.5 %collective-permute-start.17 = (f32[32,512]{1,0:T(8,128)S(1)}, f32[32,512]{1,0:T(8,128)S(1)}, u32[]{:S(2)}, u32[]{:S(2)}) collective-permute-start(f32[32,512]{1,0:T(8,128)S(1)} %get-tuple-element.98.a2), channel_id=1, source_target_pairs={{0,7},{1,0},{2,1},{3,2},{4,3},{5,4},{6,5},{7,6},{8,15},{9,8},{10,9... | collective-permute-start | bytes 196616 | tf_op jit(solution)/shard_map/ppermute | solution.py:243
  257.7 6.7 %collective-permute-start.16 = (f32[32,512]{1,0:T(8,128)S(1)}, f32[32,512]{1,0:T(8,128)S(1)}, u32[]{:S(2)}, u32[]{:S(2)}) collective-permute-start(f32[32,512]{1,0:T(8,128)S(1)} %get-tuple-element.99.a3), channel_id=1, source_target_pairs={{0,1},{1,2},{2,3},{3,4},{4,5},{5,6},{6,7},{7,0},{8,9},{9,10},{10,1... | collective-permute-start | bytes 196616 | tf_op jit(solution)/shard_map/ppermute | solution.py:242
  311.2 4.9 %collective-permute-start.19 = (f32[32,512]{1,0:T(8,128)S(1)}, f32[32,512]{1,0:T(8,128)S(1)}, u32[]{:S(2)}, u32[]{:S(2)}) collective-permute-start(f32[32,512]{1,0:T(8,128)S(1)} %get-tuple-element.105.a0), channel_id=1, source_target_pairs={{0,120},{8,0},{16,8},{24,16},{32,24},{40,32},{48,40},{56,48},{64,5... | collective-permute-start | bytes 196616 | tf_op jit(solution)/shard_map/ppermute | solution.py:241
  311.5 4.6 collective-permute-start.18
  312.9 5.5 %collective-permute-start.21 = (f32[32,512]{1,0:T(8,128)S(1)}, f32[32,512]{1,0:T(8,128)S(1)}, u32[]{:S(2)}, u32[]{:S(2)}) collective-permute-start(f32[32,512]{1,0:T(8,128)S(1)} %get-tuple-element.107.a2), channel_id=1, source_target_pairs={{0,7},{1,0},{2,1},{3,2},{4,3},{5,4},{6,5},{7,6},{8,15},{9,8},{10,9... | collective-permute-start | bytes 196616 | tf_op jit(solution)/shard_map/ppermute | solution.py:243
  313.9 6.9 %collective-permute-start.20 = (f32[32,512]{1,0:T(8,128)S(1)}, f32[32,512]{1,0:T(8,128)S(1)}, u32[]{:S(2)}, u32[]{:S(2)}) collective-permute-start(f32[32,512]{1,0:T(8,128)S(1)} %get-tuple-element.108.a3), channel_id=1, source_target_pairs={{0,1},{1,2},{2,3},{3,4},{4,5},{5,6},{6,7},{7,0},{8,9},{9,10},{10,1... | collective-permute-start | bytes 196616 | tf_op jit(solution)/shard_map/ppermute | solution.py:242
  367.5 4.7 collective-permute-start.23
  367.9 4.4 collective-permute-start.22
  369.3 5.5 %collective-permute-start.25 = (f32[32,512]{1,0:T(8,128)S(1)}, f32[32,512]{1,0:T(8,128)S(1)}, u32[]{:S(2)}, u32[]{:S(2)}) collective-permute-start(f32[32,512]{1,0:T(8,128)S(1)} %get-tuple-element.116.a2), channel_id=1, source_target_pairs={{0,7},{1,0},{2,1},{3,2},{4,3},{5,4},{6,5},{7,6},{8,15},{9,8},{10,9... | collective-permute-start | bytes 196616 | tf_op jit(solution)/shard_map/ppermute | solution.py:243
  370.2 6.7 %collective-permute-start.24 = (f32[32,512]{1,0:T(8,128)S(1)}, f32[32,512]{1,0:T(8,128)S(1)}, u32[]{:S(2)}, u32[]{:S(2)}) collective-permute-start(f32[32,512]{1,0:T(8,128)S(1)} %get-tuple-element.117.a3), channel_id=1, source_target_pairs={{0,1},{1,2},{2,3},{3,4},{4,5},{5,6},{6,7},{7,0},{8,9},{9,10},{10,1... | collective-permute-start | bytes 196616 | tf_op jit(solution)/shard_map/ppermute | solution.py:242
  423.9 4.7 collective-permute-start.27
  424.3 4.4 collective-permute-start.26
  425.7 5.5 %collective-permute-start.29 = (f32[32,512]{1,0:T(8,128)S(1)}, f32[32,512]{1,0:T(8,128)S(1)}, u32[]{:S(2)}, u32[]{:S(2)}) collective-permute-start(f32[32,512]{1,0:T(8,128)S(1)} %get-tuple-element.125.a2), channel_id=1, source_target_pairs={{0,7},{1,0},{2,1},{3,2},{4,3},{5,4},{6,5},{7,6},{8,15},{9,8},{10,9... | collective-permute-start | bytes 196616 | tf_op jit(solution)/shard_map/ppermute | solution.py:243
  426.6 6.7 %collective-permute-start.28 = (f32[32,512]{1,0:T(8,128)S(1)}, f32[32,512]{1,0:T(8,128)S(1)}, u32[]{:S(2)}, u32[]{:S(2)}) collective-permute-start(f32[32,512]{1,0:T(8,128)S(1)} %get-tuple-element.126.a3), channel_id=1, source_target_pairs={{0,1},{1,2},{2,3},{3,4},{4,5},{5,6},{6,7},{7,0},{8,9},{9,10},{10,1... | collective-permute-start | bytes 196616 | tf_op jit(solution)/shard_map/ppermute | solution.py:242
  (34 other events, 118.0 us)

commit v2 on v1

v2 whole, which is shorter than its diff:
```python
import functools

import jax
import jax.numpy as jnp
from jax import lax
from jax.experimental import pallas as pl
from jax.experimental.pallas import tpu as pltpu
from jax.sharding import PartitionSpec as P

MDEV = 64
ITERS = 6
K = 32
FACE = 512
M = 4 * FACE
DEPTH = 256
VMEM_LIMIT = 24 << 20

F32 = jnp.float32
BF16 = jnp.bfloat16


def split(x):
    hi = x.astype(BF16)
    return hi, (x - hi.astype(F32)).astype(BF16)


def call(kernel, outs, *args, scratch=(), smem=()):
    return pl.pallas_call(
        kernel,
        out_shape=[jax.ShapeDtypeStruct(shape, dtype) for shape, dtype in outs],
        in_specs=[
            pl.BlockSpec(memory_space=pltpu.SMEM if i in smem else pltpu.VMEM)
            for i in range(len(args))
        ],
        out_specs=[pl.BlockSpec(memory_space=pltpu.VMEM)] * len(outs),
        scratch_shapes=[pltpu.VMEM(shape, dtype) for shape, dtype in scratch],
        compiler_params=pltpu.CompilerParams(vmem_limit_bytes=VMEM_LIMIT),
    )(*args)


def split_t_kernel(x_ref, hi_ref, lo_ref):
    hi_ref[...], lo_ref[...] = split(x_ref[...].T)


def split_tile(tile):
    rows, cols = tile.shape
    step = 256
    return pl.pallas_call(
        split_t_kernel,
        grid=(cols // step,),
        out_shape=[jax.ShapeDtypeStruct((cols, rows), BF16)] * 2,
        in_specs=[pl.BlockSpec((rows, step), lambda i: (0, i))],
        out_specs=[pl.BlockSpec((step, rows), lambda i: (i, 0))] * 2,
        compiler_params=pltpu.CompilerParams(vmem_limit_bytes=VMEM_LIMIT),
    )(tile)


def weights_kernel(
    has_ref, mask_ref, basis_ref, gap_ref, n0, n1, n2, n3, exp_ref, res_ref, dvec_ref, contact_ref
):
    for f, n_ref in enumerate((n0, n1, n2, n3)):
        own = basis_ref[f]
        there = has_ref[f] != 0
        nb = jnp.where(there, n_ref[0:MDEV, :], 0.0)
        both = jnp.concatenate([nb, own] if f == 2 else [own, nb], axis=0)
        hi, lo = split(both)
        exp_ref[f, 0:128, :] = hi
        exp_ref[f, 128:256, :] = lo
        hi, lo = split(own)
        pair = jnp.concatenate([hi.astype(F32), lo.astype(F32)], axis=0)
        res_ref[f * FACE : (f + 1) * FACE, :] = pair.T.astype(BF16)
        dvec_ref[f] = gap_ref[f] + jnp.where(there, n_ref[MDEV : MDEV + K, :], 0.0)
        touch = jnp.where(mask_ref[f : f + 1, :] == 1, 1, 0)
        contact_ref[f : f + 1, :] = jnp.where(there, 0, touch)


def low_lanes(shape):
    return lax.broadcasted_iota(jnp.int32, shape, len(shape) - 1) < MDEV


def put(lhs, f, value):
    hi, lo = split(value)
    lhs[0:K, f * FACE : (f + 1) * FACE] = hi
    lhs[K : 2 * K, f * FACE : (f + 1) * FACE] = lo


def expand_face(side, weights):
    hi, lo = split(side)
    lhs = jnp.concatenate(
        [jnp.concatenate([hi, hi], axis=1), jnp.concatenate([lo, lo], axis=1)], axis=0
    )
    res = jnp.dot(lhs, weights, preferred_element_type=F32)
    return res[0:K] + res[K : 2 * K]


def product(lhs, first, block):
    last = first + block.shape[0]
    hi, lo = split(block)
    a = jnp.dot(lhs[:, first:last], hi, preferred_element_type=F32)
    b = jnp.dot(lhs[0:K, first:last], lo, preferred_element_type=F32)
    return a[0:K] + a[K : 2 * K] + b


def apply_face(lhs, dual, f):
    cols = slice(f * FACE, (f + 1) * FACE)
    total = jnp.zeros((K, FACE), F32)
    for first in range(0, M, DEPTH):
        total = total + product(lhs, first, dual[first : first + DEPTH, cols])
    return total


def amps_sides(own, pair, up, down):
    low = low_lanes((K, 128))
    return (
        jnp.where(low, own, up),
        jnp.where(low, own, down),
        jnp.where(low, pair, own),
        jnp.where(low, own, pair),
    )


def amps_kernel(parts_ref, own_ref, pair_ref):
    half = K // 2
    total = parts_ref[0]
    for s in range(1, parts_ref.shape[0]):
        total = total + parts_ref[s]
    pair_ref[...] = total[0:K]
    packed = total[K : K + half]
    turned = pltpu.roll(packed, MDEV, 1)
    low = low_lanes((half, 128))
    own_ref[0:half, :] = jnp.where(low, packed, turned)
    own_ref[half:K, :] = jnp.where(low, turned, packed)


def first_kernel(
    own_ref, pair_ref, up_ref, down_ref, exp_ref, dual, m_ref, a0, a1, a2, a3, lhs
):
    sides = amps_sides(own_ref[...], pair_ref[...], up_ref[...], down_ref[...])
    for f, side in enumerate(sides):
        face = expand_face(side, exp_ref[f])
        m_ref[f] = face
        put(lhs, f, face)
    for f, a_ref in enumerate((a0, a1, a2, a3)):
        a_ref[...] = apply_face(lhs, dual, f)


def ratio_of(sums_ref):
    sums = jnp.sum(sums_ref[...], axis=0)
    quot = sums / pltpu.roll(sums, 128 - K, 1)
    rows = lax.broadcasted_iota(jnp.int32, (K, 128), 0)
    lanes = lax.broadcasted_iota(jnp.int32, (K, 128), 1)
    return jnp.sum(jnp.where(rows == lanes, quot, 0.0), axis=1, keepdims=True)


def step_kernel(
    has_ref, sums_ref, contact_ref, m_ref, p_ref, image_ref, o0, o1, o2, o3, dual,
    new_ref, a0, a1, a2, a3, lhs, corr,
):
    ratio = ratio_of(sums_ref)
    for f in range(4):
        plain = m_ref[f] - ratio * p_ref[f]
        new = jnp.where(contact_ref[f : f + 1, :] != 0, jnp.maximum(plain, 0.0), plain)
        new_ref[f] = new
        corr[f] = new - plain
    faces = ((o0, a0), (o1, a1), (o2, a2), (o3, a3))
    for f, (o_ref, a_ref) in enumerate(faces):
        a_ref[...] = o_ref[...] - ratio * image_ref[f]
    for face in range(4):

        @pl.when(has_ref[face] == 0)
        def _():
            hi, lo = split(corr[face])
            lhs[0:K, :] = hi
            lhs[K : 2 * K, :] = lo
            for f, (_, a_ref) in enumerate(faces):
                total = a_ref[...]
                for first in range(0, FACE, DEPTH):
                    row = face * FACE + first
                    cols = slice(f * FACE, (f + 1) * FACE)
                    total = total + product(lhs, first, dual[row : row + DEPTH, cols])
                a_ref[...] = total


def last_kernel(sums_ref, contact_ref, m_ref, p_ref, new_ref):
    ratio = ratio_of(sums_ref)
    for f in range(4):
        new = m_ref[f] - ratio * p_ref[f]
        new_ref[f] = jnp.where(contact_ref[f : f + 1, :] != 0, jnp.maximum(new, 0.0), new)


def grad_kernel(
    has_ref, a0, a1, a2, a3, n0, n1, n2, n3, dvec_ref, res_ref, grad_ref, e_ref, lhs
):
    for f, (a_ref, n_ref) in enumerate(((a0, n0), (a1, n1), (a2, n2), (a3, n3))):
        nb = jnp.where(has_ref[f] != 0, n_ref[...], 0.0)
        grad = a_ref[...] + nb - dvec_ref[f]
        grad_ref[f] = grad
        put(lhs, f, grad)
    both = jnp.dot(lhs[...], res_ref[...], preferred_element_type=F32)
    both = both[0:K] + both[K : 2 * K]
    e = both + pltpu.roll(both, MDEV, 1)
    packed = jnp.where(low_lanes((K // 2, 128)), e[0 : K // 2], e[K // 2 : K])
    for s in range(e_ref.shape[0]):
        e_ref[s] = packed


def unpack_residuals(x_ref, lhs):
    half = K // 2
    low = low_lanes((half, 128))
    for t in range(x_ref.shape[0] // 2):
        xa, xb = x_ref[2 * t], x_ref[2 * t + 1]
        cols = slice(t * 128, (t + 1) * 128)
        top = jnp.where(low, xa, pltpu.roll(xb, MDEV, 1))
        bottom = jnp.where(low, pltpu.roll(xa, MDEV, 1), xb)
        lhs[0:half, cols], lhs[K : K + half, cols] = split(top)
        lhs[half:K, cols], lhs[K + half : 2 * K, cols] = split(bottom)


def coarse_kernel(x_ref, hi_ref, lo_ref, out_ref, lhs):
    unpack_residuals(x_ref, lhs)
    a = jnp.dot(lhs[...], hi_ref[...], preferred_element_type=F32)
    b = jnp.dot(lhs[0:K, :], lo_ref[...], preferred_element_type=F32)
    full = a[0:K] + a[K : 2 * K] + b
    own = [full[:, q : q + 128] for q in range(0, full.shape[1], 128)]
    turned = [pltpu.roll(b, MDEV, 1) for b in own]
    half, n = K // 2, len(own)
    low = low_lanes((K, 128))
    low_half = low_lanes((half, 128))
    zero = jnp.zeros((K, 128), F32)
    for q in range(n):
        even, odd = 2 * q, 2 * q + 1
        out_ref[even, 0:K, :] = jnp.where(low, turned[q - 1] if q > 0 else zero, own[q])
        out_ref[even, K : K + half, :] = jnp.where(low_half, own[q][0:half], turned[q][half:K])
        out_ref[odd, 0:K, :] = jnp.where(low, own[q], turned[q + 1] if q + 1 < n else zero)
        out_ref[odd, K : K + half, :] = jnp.where(low_half, turned[q][0:half], own[q][half:K])


def image_kernel(
    has_ref, own_ref, pair_ref, up_ref, down_ref, grad_ref, exp_ref, dual, p_ref, image_ref, s_ref, lhs
):
    sides = amps_sides(own_ref[...], pair_ref[...], up_ref[...], down_ref[...])
    numer = jnp.zeros((K, 1), F32)
    for f, side in enumerate(sides):
        grad = grad_ref[f]
        p = grad - expand_face(side, exp_ref[f])
        p_ref[f] = p
        put(lhs, f, p)
        weight = jnp.where(has_ref[f] != 0, 0.5, 1.0)
        numer = numer + weight * jnp.sum(grad * p, axis=1, keepdims=True)
    denom = jnp.zeros((K, 1), F32)
    for f in range(4):
        image = apply_face(lhs, dual, f)
        image_ref[f] = image
        denom = denom + jnp.sum(p_ref[f] * image, axis=1, keepdims=True)
    rows = lax.broadcasted_iota(jnp.int32, (K, 128), 0)
    lanes = lax.broadcasted_iota(jnp.int32, (K, 128), 1)
    placed = jnp.where(rows == lanes, numer, 0.0) + jnp.where(rows + K == lanes, denom, 0.0)
    line = jnp.sum(placed, axis=0, keepdims=True)
    s_ref[...] = jnp.broadcast_to(line[None], s_ref.shape)


def along(value, axis, step):
    n = lax.axis_size(axis)
    return lax.ppermute(value, axis, [(i, (i + step) % n) for i in range(n)])


def exchange(faces):
    return (
        along(faces[1], "row", 1),
        along(faces[0], "row", -1),
        along(faces[3], "col", 1),
        along(faces[2], "col", -1),
    )


def shards(dual_ops, basis, coarse_inverse, gap_rhs, coarse_rhs, contact_mask):
    n_rows, n_cols = lax.axis_size("row"), lax.axis_size("col")
    row, col = lax.axis_index("row"), lax.axis_index("col")
    has_nb = jnp.stack([row > 0, row < n_rows - 1, col > 0, col < n_cols - 1]).astype(jnp.int32)
    dual = dual_ops[0, 0]

    vec = ((4, K, FACE), F32)
    face = ((K, FACE), F32)
    amps = ((K, 128), F32)
    split_lhs = ((2 * K, M), BF16)

    tile = split_tile(coarse_inverse)

    def coarse(sent):
        got = lax.all_to_all(sent, "row", 0, 0, tiled=True)
        (parts,) = call(
            coarse_kernel, [((n_cols, K + K // 2, 128), F32)], got, *tile,
            scratch=[((2 * K, n_rows * MDEV), BF16)],
        )
        parts = lax.all_to_all(parts, "col", 0, 0, tiled=True)
        own, pair = call(amps_kernel, [amps, amps], parts)
        return own, pair, along(own, "row", 1), along(own, "row", -1)

    rhs = coarse_rhs[0, 0]
    packed = jnp.concatenate([rhs[: K // 2], rhs[K // 2 :]], axis=1)
    sent = jnp.broadcast_to(packed[None], (n_rows, K // 2, 2 * MDEV))

    both = jnp.concatenate([basis[0, 0], gap_rhs[0, 0]], axis=1)
    nbs = exchange([both[f] for f in range(4)])
    exp, res, dvec, contact = call(
        weights_kernel,
        [((4, 256, FACE), BF16), ((M, 128), BF16), vec, ((4, FACE), jnp.int32)],
        has_nb, contact_mask[0, 0], basis[0, 0], gap_rhs[0, 0], *nbs,
        smem=(0,),
    )

    sides = coarse(sent)
    exp, res, dvec, contact, sides = lax.optimization_barrier((exp, res, dvec, contact, sides))
    multipliers, *faces = call(
        first_kernel, [vec] + [face] * 4, *sides, exp, dual, scratch=[split_lhs]
    )
    for step in range(ITERS):
        grad, sent = call(
            grad_kernel,
            [vec, ((n_rows, K // 2, 128), F32)],
            has_nb, *faces, *exchange(faces), dvec, res,
            scratch=[split_lhs], smem=(0,),
        )
        projected, image, sums = call(
            image_kernel,
            [vec, vec, ((n_rows * n_cols, 1, 128), F32)],
            has_nb, *coarse(sent), grad, exp, dual,
            scratch=[split_lhs], smem=(0,),
        )
        sums = lax.all_to_all(sums, ("row", "col"), 0, 0, tiled=True)
        if step + 1 < ITERS:
            multipliers, *faces = call(
                step_kernel, [vec] + [face] * 4,
                has_nb, sums, contact, multipliers, projected, image, *faces, dual,
                scratch=[((2 * K, FACE), BF16), vec], smem=(0,),
            )
        else:
            (multipliers,) = call(last_kernel, [vec], sums, contact, multipliers, projected)
    return (multipliers[None, None], projected[None, None])


def solution(mesh):
    return jax.shard_map(
        shards,
        mesh=mesh,
        in_specs=(
            P("row", "col", None, None),
            P("row", "col", None, None, None),
            P("row", "col"),
            P("row", "col", None, None, None),
            P("row", "col", None, None),
            P("row", "col", None, None),
        ),
        out_specs=(P("row", "col", None, None, None), P("row", "col", None, None, None)),
        check_vma=False,
    )
```

time: 488 us -> 416 us (0.85)
  local copies, waits for them, and re-layouts: 56.2 us -> 12.4 us
  waiting for transfers between devices: 74.7 us -> 41.9 us
  Pallas kernels: 71.1 us -> 52 us
  blocking collectives: 211 us -> 229 us
  starting transfers between devices: 63.2 us -> 69.2 us
    unnamed x98 -> x14, local copies, waits for them, and re-layouts: 54.8 us -> 11 us
    all_to_all x5 -> x6, blocking collectives: 73.2 us -> 100 us  [shards(): sums = lax.all_to_all(sums, ('row', 'col'), 0, 0, tiled=True)]
    ppermute x30 -> x42, waiting for transfers between devices: 64.7 us -> 39.4 us  [along(): return lax.ppermute(value, axis, [(i, (i + step) % n) for i in range(n)])]
    ppermute x30 -> x42, starting transfers between devices: 45 us -> 58.9 us  [along(): return lax.ppermute(value, axis, [(i, (i + step) % n) for i in range(n)])]
    all_to_all x6, blocking collectives: 71.7 us -> 58.3 us  [coarse(): parts = lax.all_to_all(parts, 'col', 0, 0, tiled=True)]
    pallas_call x27 -> x34, Pallas kernels: 62.1 us -> 50.9 us  [call(): pl.pallas_call(kernel, out_shape=[jax.ShapeDtypeStruct(shape, dtype) for...]
    all_to_all x2 -> x1, starting transfers between devices: 12.2 us -> 3.39 us  [coarse(): parts = lax.all_to_all(parts, 'col', 0, 0, tiled=True)]
    all_to_all x2 -> x1, waiting for transfers between devices: 9.93 us -> 2.45 us  [coarse(): parts = lax.all_to_all(parts, 'col', 0, 0, tiled=True)]
  transfers between devices with their start and end apart: 33 -> 44, of which waited for: 15 -> 20; matrix products, arithmetic and copies ran while one was open for 1% -> 1% of each run, Pallas kernels for 2% -> 1%
where the time goes in v2:
time: 416 us; the launch traced here: 408 us
  blocking collectives  229 us (55%)
  starting transfers between devices  69.2 us (17%)
  Pallas kernels  52 us (12%)
  waiting for transfers between devices  41.9 us (10%)
  local copies, waits for them, and re-layouts  12.4 us (3%)
    all_to_all x6, blocking collectives, shards(): sums = lax.all_to_all(sums, ('row', 'col'), 0, 0, tiled=True)  100 us
    all_to_all x6, blocking collectives, coarse(): got = lax.all_to_all(sent, 'row', 0, 0, tiled=True)  70.6 us
    ppermute x42, starting transfers between devices, along(): return lax.ppermute(value, axis, [(i, (i + step) % n) for i in range(n)])  58.9 us
    all_to_all x6, blocking collectives, coarse(): parts = lax.all_to_all(parts, 'col', 0, 0, tiled=True)  58.3 us
    pallas_call x34, Pallas kernels, call(): pl.pallas_call(kernel, out_shape=[jax.ShapeDtypeStruct(shape, dtype) for...  50.9 us
    ppermute x42, waiting for transfers between devices, along(): return lax.ppermute(value, axis, [(i, (i + step) % n) for i in range(n)])  39.4 us
    unnamed x14, local copies, waits for them, and re-layouts  11 us
  transfers between devices with their start and end apart: 44, of which 20 were waited for; matrix products, arithmetic and copies ran while one was open for 1% of the time, Pallas kernels for 1%

profile of v2, /device:TPU:1, one launch (start us, length us, event | category | flops | bytes accessed | tf_op | source)
XLA Modules:
  0.0 408.0 jit_solution(8024897669389974081)
XLA Ops:
  2.1 6.9 %all-to-all-start = ((f32[16,16,128]{2,1,0:T(8,128)}), f32[16,16,128]{2,1,0:T(8,128)S(1)}, u32[]{:S(2)}, u32[]{:S(2)}) async-start(f32[16,16,128]{2,1,0:T(8,128)} %broadcast_in_dim.12), calls=%async_computation | async-start | bytes 262144 | tf_op jit(solution)/shard_map/all_to_all | solution.py:290
  9.0 2.0 fusion.6
  11.0 5.9 %collective-permute-start.3 = (f32[96,512]{1,0:T(8,128)}, f32[96,512]{1,0:T(8,128)S(1)}, u32[]{:S(2)}, u32[]{:S(2)}) collective-permute-start(f32[96,512]{1,0:T(8,128)} %get-tuple-element.176), channel_id=1, source_target_pairs={{0,7},{1,0},{2,1},{3,2},{4,3},{5,4},{6,5},{7,6},{8,15},{9,8},{10,9... | collective-permute-start | bytes 589832 | tf_op jit(solution)/shard_map/ppermute | solution.py:264
  20.9 3.4 all-to-all-start.1
  25.7 3.7 collective-permute-start.2
  29.3 2.4 all-to-all-done.1.parts_ref
  34.4 4.3 %collective-permute-done.2.n2 = f32[96,512]{1,0:T(8,128)S(1)} collective-permute-done((f32[96,512]{1,0:T(8,128)S(1)}, f32[96,512]{1,0:T(8,128)S(1)}, u32[]{:S(2)}, u32[]{:S(2)}) %collective-permute-start.2) | collective-permute-done | bytes 196640 | tf_op jit(solution)/shard_map/ppermute | solution.py:264
  42.2 5.8 %copy-done = f32[1,1,2048,2048]{3,2,1,0:T(8,128)S(1)} copy-done((f32[1,1,2048,2048]{3,2,1,0:T(8,128)S(1)}, f32[1,1,2048,2048]{3,2,1,0:T(8,128)}, u32[]{:S(2)}) %copy-start) | copy-done | bytes 16777240
  48.0 3.4 shard_map.81
  51.4 3.2 collective-permute-start.7
  59.9 3.3 collective-permute-done.8.n2
  64.1 11.6 %all_to_all.100.x_ref = f32[16,16,128]{2,1,0:T(8,128)S(1)} all-to-all(f32[16,16,128]{2,1,0:T(8,128)S(1)} %get-tuple-element.108), channel_id=1, replica_groups=mesh['row'=16,'col'=8] {'row'}, dimensions={0} | all-to-all | bytes 262144 | tf_op jit(solution)/shard_map/all_to_all | solution.py:290
  76.3 9.7 %all_to_all.101.parts_ref = f32[8,48,128]{2,1,0:T(8,128)S(1)} all-to-all(f32[8,48,128]{2,1,0:T(8,128)S(1)} %shard_map.83), channel_id=1, replica_groups=mesh['row'=16,'col'=8] {'col'}, dimensions={0} | all-to-all | bytes 393216 | tf_op jit(solution)/shard_map/all_to_all | solution.py:295
  86.1 2.0 collective-permute-start.11
  89.7 4.2 %shard_map.85 = (f32[4,32,512]{2,1,0:T(8,128)S(1)}, f32[4,32,512]{2,1,0:T(8,128)S(1)}, f32[128,1,128]{2,1,0:T(1,128)S(1)}) custom-call(s32[4]{0:T(128)S(1)} %add_convert_fusion.has_ref, f32[32,128]{1,0:T(8,128)S(1)} %get-tuple-element.109.own_ref, f32[32,128]{1,0:T(8,128)S(1)} %get-tuple-element.110.pair_ref, f32[32,128]{1,0:T(8,128)S(1)} %collective-permute-done.10.up_ref, ...), custom_call_target="tpu_custom_call" | custom-call | tf_op jit(solution)/shard_map/pallas_call | solution.py:28
  93.9 16.8 %all_to_all.102.sums_ref = f32[128,1,128]{2,1,0:T(1,128)S(1)} all-to-all(f32[128,1,128]{2,1,0:T(1,128)S(1)} %get-tuple-element.112), channel_id=1, replica_groups=mesh['row'=16,'col'=8] {'row','col'}, dimensions={0} | all-to-all | bytes 131072 | tf_op jit(solution)/shard_map/all_to_all | solution.py:330
  115.3 2.0 collective-permute-start.14
  119.0 3.1 collective-permute-done.14.n2
  122.9 11.8 %all_to_all.103.x_ref = f32[16,16,128]{2,1,0:T(8,128)S(1)} all-to-all(f32[16,16,128]{2,1,0:T(8,128)S(1)} %get-tuple-element.121), channel_id=1, replica_groups=mesh['row'=16,'col'=8] {'row'}, dimensions={0} | all-to-all | bytes 262144 | tf_op jit(solution)/shard_map/all_to_all | solution.py:290
  135.3 9.7 %all_to_all.104.parts_ref = f32[8,48,128]{2,1,0:T(8,128)S(1)} all-to-all(f32[8,48,128]{2,1,0:T(8,128)S(1)} %shard_map.88), channel_id=1, replica_groups=mesh['row'=16,'col'=8] {'col'}, dimensions={0} | all-to-all | bytes 393216 | tf_op jit(solution)/shard_map/all_to_all | solution.py:295
  148.6 4.2 %shard_map.90 = (f32[4,32,512]{2,1,0:T(8,128)S(1)}, f32[4,32,512]{2,1,0:T(8,128)S(1)}, f32[128,1,128]{2,1,0:T(1,128)S(1)}) custom-call(s32[4]{0:T(128)S(1)} %add_convert_fusion.has_ref, f32[32,128]{1,0:T(8,128)S(1)} %get-tuple-element.122.own_ref, f32[32,128]{1,0:T(8,128)S(1)} %get-tuple-element.123.pair_ref, f32[32,128]{1,0:T(8,128)S(1)} %collective-permute-done.16.up_ref, ...), custom_call_target="tpu_custom_call" | custom-call | tf_op jit(solution)/shard_map/pallas_call | solution.py:28
  152.9 16.8 %all_to_all.105.sums_ref = f32[128,1,128]{2,1,0:T(1,128)S(1)} all-to-all(f32[128,1,128]{2,1,0:T(1,128)S(1)} %get-tuple-element.125), channel_id=1, replica_groups=mesh['row'=16,'col'=8] {'row','col'}, dimensions={0} | all-to-all | bytes 131072 | tf_op jit(solution)/shard_map/all_to_all | solution.py:330
  169.7 1.9 shard_map.91
  174.3 2.0 collective-permute-start.20
  178.0 3.1 collective-permute-done.20.n2
  181.9 11.8 %all_to_all.106.x_ref = f32[16,16,128]{2,1,0:T(8,128)S(1)} all-to-all(f32[16,16,128]{2,1,0:T(8,128)S(1)} %get-tuple-element.133), channel_id=1, replica_groups=mesh['row'=16,'col'=8] {'row'}, dimensions={0} | all-to-all | bytes 262144 | tf_op jit(solution)/shard_map/all_to_all | solution.py:290
  194.3 9.7 %all_to_all.107.parts_ref = f32[8,48,128]{2,1,0:T(8,128)S(1)} all-to-all(f32[8,48,128]{2,1,0:T(8,128)S(1)} %shard_map.93), channel_id=1, replica_groups=mesh['row'=16,'col'=8] {'col'}, dimensions={0} | all-to-all | bytes 393216 | tf_op jit(solution)/shard_map/all_to_all | solution.py:295
  207.7 4.2 %shard_map.95 = (f32[4,32,512]{2,1,0:T(8,128)S(1)}, f32[4,32,512]{2,1,0:T(8,128)S(1)}, f32[128,1,128]{2,1,0:T(1,128)S(1)}) custom-call(s32[4]{0:T(128)S(1)} %add_convert_fusion.has_ref, f32[32,128]{1,0:T(8,128)S(1)} %get-tuple-element.134.own_ref, f32[32,128]{1,0:T(8,128)S(1)} %get-tuple-element.135.pair_ref, f32[32,128]{1,0:T(8,128)S(1)} %collective-permute-done.22.up_ref, ...), custom_call_target="tpu_custom_call" | custom-call | tf_op jit(solution)/shard_map/pallas_call | solution.py:28
  211.9 16.6 %all_to_all.108.sums_ref = f32[128,1,128]{2,1,0:T(1,128)S(1)} all-to-all(f32[128,1,128]{2,1,0:T(1,128)S(1)} %get-tuple-element.137), channel_id=1, replica_groups=mesh['row'=16,'col'=8] {'row','col'}, dimensions={0} | all-to-all | bytes 131072 | tf_op jit(solution)/shard_map/all_to_all | solution.py:330
  233.1 2.0 collective-permute-start.26
  236.7 3.1 collective-permute-done.26.n2
  240.7 11.8 %all_to_all.109.x_ref = f32[16,16,128]{2,1,0:T(8,128)S(1)} all-to-all(f32[16,16,128]{2,1,0:T(8,128)S(1)} %get-tuple-element.145), channel_id=1, replica_groups=mesh['row'=16,'col'=8] {'row'}, dimensions={0} | all-to-all | bytes 262144 | tf_op jit(solution)/shard_map/all_to_all | solution.py:290
  253.1 9.7 %all_to_all.110.parts_ref = f32[8,48,128]{2,1,0:T(8,128)S(1)} all-to-all(f32[8,48,128]{2,1,0:T(8,128)S(1)} %shard_map.98), channel_id=1, replica_groups=mesh['row'=16,'col'=8] {'col'}, dimensions={0} | all-to-all | bytes 393216 | tf_op jit(solution)/shard_map/all_to_all | solution.py:295
  266.4 4.2 %shard_map.100 = (f32[4,32,512]{2,1,0:T(8,128)S(1)}, f32[4,32,512]{2,1,0:T(8,128)S(1)}, f32[128,1,128]{2,1,0:T(1,128)S(1)}) custom-call(s32[4]{0:T(128)S(1)} %add_convert_fusion.has_ref, f32[32,128]{1,0:T(8,128)S(1)} %get-tuple-element.146.own_ref, f32[32,128]{1,0:T(8,128)S(1)} %get-tuple-element.147.pair_ref, f32[32,128]{1,0:T(8,128)S(1)} %collective-permute-done.28.up_ref, ...), custom_call_target="tpu_custom_call" | custom-call | tf_op jit(solution)/shard_map/pallas_call | solution.py:28
  270.7 16.6 %all_to_all.111.sums_ref = f32[128,1,128]{2,1,0:T(1,128)S(1)} all-to-all(f32[128,1,128]{2,1,0:T(1,128)S(1)} %get-tuple-element.149), channel_id=1, replica_groups=mesh['row'=16,'col'=8] {'row','col'}, dimensions={0} | all-to-all | bytes 131072 | tf_op jit(solution)/shard_map/all_to_all | solution.py:330
  287.3 1.9 shard_map.101
  291.9 2.0 collective-permute-start.32
  295.5 3.1 collective-permute-done.32.n2
  299.5 11.8 %all_to_all.112.x_ref = f32[16,16,128]{2,1,0:T(8,128)S(1)} all-to-all(f32[16,16,128]{2,1,0:T(8,128)S(1)} %get-tuple-element.157), channel_id=1, replica_groups=mesh['row'=16,'col'=8] {'row'}, dimensions={0} | all-to-all | bytes 262144 | tf_op jit(solution)/shard_map/all_to_all | solution.py:290
  311.9 9.7 %all_to_all.113.parts_ref = f32[8,48,128]{2,1,0:T(8,128)S(1)} all-to-all(f32[8,48,128]{2,1,0:T(8,128)S(1)} %shard_map.103), channel_id=1, replica_groups=mesh['row'=16,'col'=8] {'col'}, dimensions={0} | all-to-all | bytes 393216 | tf_op jit(solution)/shard_map/all_to_all | solution.py:295
  325.2 4.2 %shard_map.105 = (f32[4,32,512]{2,1,0:T(8,128)S(1)}, f32[4,32,512]{2,1,0:T(8,128)S(1)}, f32[128,1,128]{2,1,0:T(1,128)S(1)}) custom-call(s32[4]{0:T(128)S(1)} %add_convert_fusion.has_ref, f32[32,128]{1,0:T(8,128)S(1)} %get-tuple-element.158.own_ref, f32[32,128]{1,0:T(8,128)S(1)} %get-tuple-element.159.pair_ref, f32[32,128]{1,0:T(8,128)S(1)} %collective-permute-done.34.up_ref, ...), custom_call_target="tpu_custom_call" | custom-call | tf_op jit(solution)/shard_map/pallas_call | solution.py:28
  329.5 16.7 %all_to_all.114.sums_ref = f32[128,1,128]{2,1,0:T(1,128)S(1)} all-to-all(f32[128,1,128]{2,1,0:T(1,128)S(1)} %get-tuple-element.161), channel_id=1, replica_groups=mesh['row'=16,'col'=8] {'row','col'}, dimensions={0} | all-to-all | bytes 131072 | tf_op jit(solution)/shard_map/all_to_all | solution.py:330
  350.7 2.0 collective-permute-start.38
  354.4 3.1 collective-permute-done.38.n2
  358.3 11.8 %all_to_all.115.x_ref = f32[16,16,128]{2,1,0:T(8,128)S(1)} all-to-all(f32[16,16,128]{2,1,0:T(8,128)S(1)} %get-tuple-element.169), channel_id=1, replica_groups=mesh['row'=16,'col'=8] {'row'}, dimensions={0} | all-to-all | bytes 262144 | tf_op jit(solution)/shard_map/all_to_all | solution.py:290
  370.7 9.7 %all_to_all.116.parts_ref = f32[8,48,128]{2,1,0:T(8,128)S(1)} all-to-all(f32[8,48,128]{2,1,0:T(8,128)S(1)} %shard_map.108), channel_id=1, replica_groups=mesh['row'=16,'col'=8] {'col'}, dimensions={0} | all-to-all | bytes 393216 | tf_op jit(solution)/shard_map/all_to_all | solution.py:295
  384.1 4.8 %shard_map.110 = (f32[4,32,512]{2,1,0:T(8,128)}, f32[4,32,512]{2,1,0:T(8,128)}, f32[128,1,128]{2,1,0:T(1,128)S(1)}) custom-call(s32[4]{0:T(128)S(1)} %add_convert_fusion.has_ref, f32[32,128]{1,0:T(8,128)S(1)} %get-tuple-element.170.own_ref, f32[32,128]{1,0:T(8,128)S(1)} %get-tuple-element.171.pair_ref, f32[32,128]{1,0:T(8,128)S(1)} %collective-permute-done.40.up_ref, ...), custom_call_target="tpu_custom_call" | custom-call | tf_op jit(solution)/shard_map/pallas_call | solution.py:28
  388.9 16.7 %all_to_all.117.sums_ref = f32[128,1,128]{2,1,0:T(1,128)S(1)} all-to-all(f32[128,1,128]{2,1,0:T(1,128)S(1)} %get-tuple-element.173), channel_id=1, replica_groups=mesh['row'=16,'col'=8] {'row','col'}, dimensions={0} | all-to-all | bytes 131072 | tf_op jit(solution)/shard_map/all_to_all | solution.py:330
  (112 shorter events, 76.1 us)
Async XLA Ops:
  2.1 17.5 %all-to-all-start = ((f32[16,16,128]{2,1,0:T(8,128)}), f32[16,16,128]{2,1,0:T(8,128)S(1)}, u32[]{:S(2)}, u32[]{:S(2)}) async-start(f32[16,16,128]{2,1,0:T(8,128)} %broadcast_in_dim.12), calls=%async_computation | async-start | bytes 262144 | tf_op jit(solution)/shard_map/all_to_all | solution.py:290
  11.0 22.3 %collective-permute-start.3 = (f32[96,512]{1,0:T(8,128)}, f32[96,512]{1,0:T(8,128)S(1)}, u32[]{:S(2)}, u32[]{:S(2)}) collective-permute-start(f32[96,512]{1,0:T(8,128)} %get-tuple-element.176), channel_id=1, source_target_pairs={{0,7},{1,0},{2,1},{3,2},{4,3},{5,4},{6,5},{7,6},{8,15},{9,8},{10,9... | collective-permute-start | bytes 589832 | tf_op jit(solution)/shard_map/ppermute | solution.py:264
  17.0 1.6 copy-start.3
  20.9 10.9 %all-to-all-start.1 = ((f32[8,48,128]{2,1,0:T(8,128)}), f32[8,48,128]{2,1,0:T(8,128)S(1)}, u32[]{:S(2)}, u32[]{:S(2)}) async-start(f32[8,48,128]{2,1,0:T(8,128)} %shard_map.79), calls=%async_computation.1 | async-start | bytes 393216 | tf_op jit(solution)/shard_map/all_to_all | solution.py:295
  24.3 10.1 %collective-permute-start = (f32[96,512]{1,0:T(8,128)}, f32[96,512]{1,0:T(8,128)S(1)}, u32[]{:S(2)}, u32[]{:S(2)}) collective-permute-start(f32[96,512]{1,0:T(8,128)} %get-tuple-element.177), channel_id=1, source_target_pairs={{0,8},{8,16},{16,24},{24,32},{32,40},{40,48},{48,56},{56,64},{64,7... | collective-permute-start | bytes 589832 | tf_op jit(solution)/shard_map/ppermute | solution.py:264
  25.7 8.7 %collective-permute-start.1 = (f32[96,512]{1,0:T(8,128)S(1)}, f32[96,512]{1,0:T(8,128)S(1)}, u32[]{:S(2)}, u32[]{:S(2)}) collective-permute-start(f32[96,512]{1,0:T(8,128)S(1)} %get-tuple-element.178), channel_id=1, source_target_pairs={{0,120},{8,0},{16,8},{24,16},{32,24},{40,32},{48,40},{56,48},{64,5... | collective-permute-start | bytes 589832 | tf_op jit(solution)/shard_map/ppermute | solution.py:264
  25.7 13.0 %collective-permute-start.2 = (f32[96,512]{1,0:T(8,128)S(1)}, f32[96,512]{1,0:T(8,128)S(1)}, u32[]{:S(2)}, u32[]{:S(2)}) collective-permute-start(f32[96,512]{1,0:T(8,128)S(1)} %get-tuple-element.179), channel_id=1, source_target_pairs={{0,1},{1,2},{2,3},{3,4},{4,5},{5,6},{6,7},{7,0},{8,9},{9,10},{10,1... | collective-permute-start | bytes 589832 | tf_op jit(solution)/shard_map/ppermute | solution.py:264
  31.9 10.4 %collective-permute-start.5 = (f32[32,128]{1,0:T(8,128)S(1)}, f32[32,128]{1,0:T(8,128)S(1)}, u32[]{:S(2)}, u32[]{:S(2)}) collective-permute-start(f32[32,128]{1,0:T(8,128)S(1)} %get-tuple-element.97.own_ref), channel_id=1, source_target_pairs={{0,120},{8,0},{16,8},{24,16},{32,24},{40,32},{48,40},{56,48},{64,5... | collective-permute-start | bytes 49160 | tf_op jit(solution)/shard_map/ppermute | solution.py:264
  33.4 8.8 %collective-permute-start.4 = (f32[32,128]{1,0:T(8,128)S(1)}, f32[32,128]{1,0:T(8,128)S(1)}, u32[]{:S(2)}, u32[]{:S(2)}) collective-permute-start(f32[32,128]{1,0:T(8,128)S(1)} %get-tuple-element.97.own_ref), channel_id=1, source_target_pairs={{0,8},{8,16},{16,24},{24,32},{32,40},{40,48},{48,56},{56,64},{64,7... | collective-permute-start | bytes 49160 | tf_op jit(solution)/shard_map/ppermute | solution.py:264
  38.7 1.0 copy-start.2
  42.2 5.8 %copy-start = (f32[1,1,2048,2048]{3,2,1,0:T(8,128)S(1)}, f32[1,1,2048,2048]{3,2,1,0:T(8,128)}, u32[]{:S(2)}) copy-start(f32[1,1,2048,2048]{3,2,1,0:T(8,128)} %param.6) | copy-start | bytes 50331652
  48.0 41.6 %copy-start.1 = (f32[1,1,2048,2048]{3,2,1,0:T(8,128)S(1)}, f32[1,1,2048,2048]{3,2,1,0:T(8,128)}, u32[]{:S(2)}) copy-start(f32[1,1,2048,2048]{3,2,1,0:T(8,128)} %param.6) | copy-start | bytes 50331652
  51.4 6.9 %collective-permute-start.7 = (f32[32,512]{1,0:T(8,128)S(1)}, f32[32,512]{1,0:T(8,128)S(1)}, u32[]{:S(2)}, u32[]{:S(2)}) collective-permute-start(f32[32,512]{1,0:T(8,128)S(1)} %get-tuple-element.102.a0.o0), channel_id=1, source_target_pairs={{0,120},{8,0},{16,8},{24,16},{32,24},{40,32},{48,40},{56,48},{64,5... | collective-permute-start | bytes 196616 | tf_op jit(solution)/shard_map/ppermute | solution.py:264
  54.6 3.7 collective-permute-start.6
  55.3 4.6 %collective-permute-start.9 = (f32[32,512]{1,0:T(8,128)S(1)}, f32[32,512]{1,0:T(8,128)S(1)}, u32[]{:S(2)}, u32[]{:S(2)}) collective-permute-start(f32[32,512]{1,0:T(8,128)S(1)} %get-tuple-element.104.a2.o2), channel_id=1, source_target_pairs={{0,7},{1,0},{2,1},{3,2},{4,3},{5,4},{6,5},{7,6},{8,15},{9,8},{10,9... | collective-permute-start | bytes 196616 | tf_op jit(solution)/shard_map/ppermute | solution.py:264
  56.5 6.7 %collective-permute-start.8 = (f32[32,512]{1,0:T(8,128)S(1)}, f32[32,512]{1,0:T(8,128)S(1)}, u32[]{:S(2)}, u32[]{:S(2)}) collective-permute-start(f32[32,512]{1,0:T(8,128)S(1)} %get-tuple-element.105.a3.o3), channel_id=1, source_target_pairs={{0,1},{1,2},{2,3},{3,4},{4,5},{5,6},{6,7},{7,0},{8,9},{9,10},{10,1... | collective-permute-start | bytes 196616 | tf_op jit(solution)/shard_map/ppermute | solution.py:264
  86.1 3.5 collective-permute-start.11
  88.1 1.5 collective-permute-start.10
  112.5 4.8 %collective-permute-start.13 = (f32[32,512]{1,0:T(8,128)S(1)}, f32[32,512]{1,0:T(8,128)S(1)}, u32[]{:S(2)}, u32[]{:S(2)}) collective-permute-start(f32[32,512]{1,0:T(8,128)S(1)} %get-tuple-element.117.a0.o0), channel_id=1, source_target_pairs={{0,120},{8,0},{16,8},{24,16},{32,24},{40,32},{48,40},{56,48},{64,5... | collective-permute-start | bytes 196616 | tf_op jit(solution)/shard_map/ppermute | solution.py:264
  113.9 3.5 collective-permute-start.12
  114.3 4.6 %collective-permute-start.15 = (f32[32,512]{1,0:T(8,128)S(1)}, f32[32,512]{1,0:T(8,128)S(1)}, u32[]{:S(2)}, u32[]{:S(2)}) collective-permute-start(f32[32,512]{1,0:T(8,128)S(1)} %get-tuple-element.119.a2.o2), channel_id=1, source_target_pairs={{0,7},{1,0},{2,1},{3,2},{4,3},{5,4},{6,5},{7,6},{8,15},{9,8},{10,9... | collective-permute-start | bytes 196616 | tf_op jit(solution)/shard_map/ppermute | solution.py:264
  115.3 6.7 %collective-permute-start.14 = (f32[32,512]{1,0:T(8,128)S(1)}, f32[32,512]{1,0:T(8,128)S(1)}, u32[]{:S(2)}, u32[]{:S(2)}) collective-permute-start(f32[32,512]{1,0:T(8,128)S(1)} %get-tuple-element.120.a3.o3), channel_id=1, source_target_pairs={{0,1},{1,2},{2,3},{3,4},{4,5},{5,6},{6,7},{7,0},{8,9},{9,10},{10,1... | collective-permute-start | bytes 196616 | tf_op jit(solution)/shard_map/ppermute | solution.py:264
  145.1 3.5 collective-permute-start.17
  146.9 1.7 collective-permute-start.16
  171.6 4.8 %collective-permute-start.19 = (f32[32,512]{1,0:T(8,128)S(1)}, f32[32,512]{1,0:T(8,128)S(1)}, u32[]{:S(2)}, u32[]{:S(2)}) collective-permute-start(f32[32,512]{1,0:T(8,128)S(1)} %get-tuple-element.129.a0.o0), channel_id=1, source_target_pairs={{0,120},{8,0},{16,8},{24,16},{32,24},{40,32},{48,40},{56,48},{64,5... | collective-permute-start | bytes 196616 | tf_op jit(solution)/shard_map/ppermute | solution.py:264
  172.9 3.4 collective-permute-start.18
  173.3 4.6 %collective-permute-start.21 = (f32[32,512]{1,0:T(8,128)S(1)}, f32[32,512]{1,0:T(8,128)S(1)}, u32[]{:S(2)}, u32[]{:S(2)}) collective-permute-start(f32[32,512]{1,0:T(8,128)S(1)} %get-tuple-element.131.a2.o2), channel_id=1, source_target_pairs={{0,7},{1,0},{2,1},{3,2},{4,3},{5,4},{6,5},{7,6},{8,15},{9,8},{10,9... | collective-permute-start | bytes 196616 | tf_op jit(solution)/shard_map/ppermute | solution.py:264
  174.3 6.7 %collective-permute-start.20 = (f32[32,512]{1,0:T(8,128)S(1)}, f32[32,512]{1,0:T(8,128)S(1)}, u32[]{:S(2)}, u32[]{:S(2)}) collective-permute-start(f32[32,512]{1,0:T(8,128)S(1)} %get-tuple-element.132.a3.o3), channel_id=1, source_target_pairs={{0,1},{1,2},{2,3},{3,4},{4,5},{5,6},{6,7},{7,0},{8,9},{9,10},{10,1... | collective-permute-start | bytes 196616 | tf_op jit(solution)/shard_map/ppermute | solution.py:264
  204.1 3.5 collective-permute-start.23
  205.9 1.7 collective-permute-start.22
  230.3 4.8 %collective-permute-start.25 = (f32[32,512]{1,0:T(8,128)S(1)}, f32[32,512]{1,0:T(8,128)S(1)}, u32[]{:S(2)}, u32[]{:S(2)}) collective-permute-start(f32[32,512]{1,0:T(8,128)S(1)} %get-tuple-element.141.a0.o0), channel_id=1, source_target_pairs={{0,120},{8,0},{16,8},{24,16},{32,24},{40,32},{48,40},{56,48},{64,5... | collective-permute-start | bytes 196616 | tf_op jit(solution)/shard_map/ppermute | solution.py:264
  231.6 3.5 collective-permute-start.24
  232.1 4.6 %collective-permute-start.27 = (f32[32,512]{1,0:T(8,128)S(1)}, f32[32,512]{1,0:T(8,128)S(1)}, u32[]{:S(2)}, u32[]{:S(2)}) collective-permute-start(f32[32,512]{1,0:T(8,128)S(1)} %get-tuple-element.143.a2.o2), channel_id=1, source_target_pairs={{0,7},{1,0},{2,1},{3,2},{4,3},{5,4},{6,5},{7,6},{8,15},{9,8},{10,9... | collective-permute-start | bytes 196616 | tf_op jit(solution)/shard_map/ppermute | solution.py:264
  233.1 6.7 %collective-permute-start.26 = (f32[32,512]{1,0:T(8,128)S(1)}, f32[32,512]{1,0:T(8,128)S(1)}, u32[]{:S(2)}, u32[]{:S(2)}) collective-permute-start(f32[32,512]{1,0:T(8,128)S(1)} %get-tuple-element.144.a3.o3), channel_id=1, source_target_pairs={{0,1},{1,2},{2,3},{3,4},{4,5},{5,6},{6,7},{7,0},{8,9},{9,10},{10,1... | collective-permute-start | bytes 196616 | tf_op jit(solution)/shard_map/ppermute | solution.py:264
  262.9 3.5 collective-permute-start.29
  264.7 1.7 collective-permute-start.28
  289.1 4.8 %collective-permute-start.31 = (f32[32,512]{1,0:T(8,128)S(1)}, f32[32,512]{1,0:T(8,128)S(1)}, u32[]{:S(2)}, u32[]{:S(2)}) collective-permute-start(f32[32,512]{1,0:T(8,128)S(1)} %get-tuple-element.153.a0.o0), channel_id=1, source_target_pairs={{0,120},{8,0},{16,8},{24,16},{32,24},{40,32},{48,40},{56,48},{64,5... | collective-permute-start | bytes 196616 | tf_op jit(solution)/shard_map/ppermute | solution.py:264
  290.4 3.4 collective-permute-start.30
  290.9 4.6 %collective-permute-start.33 = (f32[32,512]{1,0:T(8,128)S(1)}, f32[32,512]{1,0:T(8,128)S(1)}, u32[]{:S(2)}, u32[]{:S(2)}) collective-permute-start(f32[32,512]{1,0:T(8,128)S(1)} %get-tuple-element.155.a2.o2), channel_id=1, source_target_pairs={{0,7},{1,0},{2,1},{3,2},{4,3},{5,4},{6,5},{7,6},{8,15},{9,8},{10,9... | collective-permute-start | bytes 196616 | tf_op jit(solution)/shard_map/ppermute | solution.py:264
  291.9 6.7 %collective-permute-start.32 = (f32[32,512]{1,0:T(8,128)S(1)}, f32[32,512]{1,0:T(8,128)S(1)}, u32[]{:S(2)}, u32[]{:S(2)}) collective-permute-start(f32[32,512]{1,0:T(8,128)S(1)} %get-tuple-element.156.a3.o3), channel_id=1, source_target_pairs={{0,1},{1,2},{2,3},{3,4},{4,5},{5,6},{6,7},{7,0},{8,9},{9,10},{10,1... | collective-permute-start | bytes 196616 | tf_op jit(solution)/shard_map/ppermute | solution.py:264
  321.7 3.5 collective-permute-start.35
  323.5 1.7 collective-permute-start.34
  348.0 4.8 %collective-permute-start.37 = (f32[32,512]{1,0:T(8,128)S(1)}, f32[32,512]{1,0:T(8,128)S(1)}, u32[]{:S(2)}, u32[]{:S(2)}) collective-permute-start(f32[32,512]{1,0:T(8,128)S(1)} %get-tuple-element.165.a0), channel_id=1, source_target_pairs={{0,120},{8,0},{16,8},{24,16},{32,24},{40,32},{48,40},{56,48},{64,5... | collective-permute-start | bytes 196616 | tf_op jit(solution)/shard_map/ppermute | solution.py:264
  349.3 3.5 collective-permute-start.36
  349.8 4.6 %collective-permute-start.39 = (f32[32,512]{1,0:T(8,128)S(1)}, f32[32,512]{1,0:T(8,128)S(1)}, u32[]{:S(2)}, u32[]{:S(2)}) collective-permute-start(f32[32,512]{1,0:T(8,128)S(1)} %get-tuple-element.167.a2), channel_id=1, source_target_pairs={{0,7},{1,0},{2,1},{3,2},{4,3},{5,4},{6,5},{7,6},{8,15},{9,8},{10,9... | collective-permute-start | bytes 196616 | tf_op jit(solution)/shard_map/ppermute | solution.py:264
  350.7 6.7 %collective-permute-start.38 = (f32[32,512]{1,0:T(8,128)S(1)}, f32[32,512]{1,0:T(8,128)S(1)}, u32[]{:S(2)}, u32[]{:S(2)}) collective-permute-start(f32[32,512]{1,0:T(8,128)S(1)} %get-tuple-element.168.a3), channel_id=1, source_target_pairs={{0,1},{1,2},{2,3},{3,4},{4,5},{5,6},{6,7},{7,0},{8,9},{9,10},{10,1... | collective-permute-start | bytes 196616 | tf_op jit(solution)/shard_map/ppermute | solution.py:264
  380.5 3.5 collective-permute-start.41
  382.3 1.7 collective-permute-start.40
  (3 other events, 2.6 us)

commit v3 on v2

--- a/solution.py
+++ b/solution.py
@@ -24,7 +24,7 @@
     return hi, (x - hi.astype(F32)).astype(BF16)
 
 
-def call(kernel, outs, *args, scratch=(), smem=()):
+def call(kernel, outs, *args, scratch=(), smem=(), cost=None):
     return pl.pallas_call(
         kernel,
         out_shape=[jax.ShapeDtypeStruct(shape, dtype) for shape, dtype in outs],
@@ -34,6 +34,7 @@
         ],
         out_specs=[pl.BlockSpec(memory_space=pltpu.VMEM)] * len(outs),
         scratch_shapes=[pltpu.VMEM(shape, dtype) for shape, dtype in scratch],
+        cost_estimate=cost and pl.CostEstimate(flops=0, bytes_accessed=cost, transcendentals=0),
         compiler_params=pltpu.CompilerParams(vmem_limit_bytes=VMEM_LIMIT),
     )(*args)
 
@@ -56,10 +57,10 @@
 
 
 def weights_kernel(
-    has_ref, mask_ref, basis_ref, gap_ref, n0, n1, n2, n3, exp_ref, res_ref, dvec_ref, contact_ref
-):
-    for f, n_ref in enumerate((n0, n1, n2, n3)):
-        own = basis_ref[f]
+    has_ref, o0, o1, o2, o3, n0, n1, n2, n3, exp_ref, res_ref, dvec_ref, contact_ref
+):
+    for f, (o_ref, n_ref) in enumerate(((o0, n0), (o1, n1), (o2, n2), (o3, n3))):
+        own = o_ref[0:MDEV, :]
         there = has_ref[f] != 0
         nb = jnp.where(there, n_ref[0:MDEV, :], 0.0)
         both = jnp.concatenate([nb, own] if f == 2 else [own, nb], axis=0)
@@ -69,8 +70,9 @@
         hi, lo = split(own)
         pair = jnp.concatenate([hi.astype(F32), lo.astype(F32)], axis=0)
         res_ref[f * FACE : (f + 1) * FACE, :] = pair.T.astype(BF16)
-        dvec_ref[f] = gap_ref[f] + jnp.where(there, n_ref[MDEV : MDEV + K, :], 0.0)
-        touch = jnp.where(mask_ref[f : f + 1, :] == 1, 1, 0)
+        gap = slice(MDEV, MDEV + K)
+        dvec_ref[f] = o_ref[gap, :] + jnp.where(there, n_ref[gap, :], 0.0)
+        touch = jnp.where(o_ref[MDEV + K : MDEV + K + 1, :] == 1.0, 1, 0)
         contact_ref[f : f + 1, :] = jnp.where(there, 0, touch)
 
 
@@ -101,22 +103,11 @@
     return a[0:K] + a[K : 2 * K] + b
 
 
-def apply_face(lhs, dual, f):
+def apply_rows(lhs, dual, f, total, first):
     cols = slice(f * FACE, (f + 1) * FACE)
-    total = jnp.zeros((K, FACE), F32)
-    for first in range(0, M, DEPTH):
-        total = total + product(lhs, first, dual[first : first + DEPTH, cols])
+    for k in range(0, lhs.shape[1], DEPTH):
+        total = total + product(lhs, k, dual[first + k : first + k + DEPTH, cols])
     return total
-
-
-def amps_sides(own, pair, up, down):
-    low = low_lanes((K, 128))
-    return (
-        jnp.where(low, own, up),
-        jnp.where(low, own, down),
-        jnp.where(low, pair, own),
-        jnp.where(low, own, pair),
-    )
 
 
 def amps_kernel(parts_ref, own_ref, pair_ref):
@@ -132,16 +123,47 @@
     own_ref[half:K, :] = jnp.where(low, turned, packed)
 
 
+def col_half_kernel(own_ref, pair_ref, grad_ref, exp_ref, dual, p_ref, part_ref, lhs):
+    low = low_lanes((K, 128))
+    own, pair = own_ref[...], pair_ref[...]
+    for f, side in ((2, jnp.where(low, pair, own)), (3, jnp.where(low, own, pair))):
+        p = grad_ref[f] - expand_face(side, exp_ref[f])
+        p_ref[f - 2] = p
+        put(lhs, f - 2, p)
+    for f in range(4):
+        part_ref[f] = apply_rows(lhs, dual, f, jnp.zeros((K, FACE), F32), M // 2)
+
+
+def row_half(own_ref, up_ref, down_ref, exp_ref):
+    low = low_lanes((K, 128))
+    for f, nb_ref in ((0, up_ref), (1, down_ref)):
+        yield f, expand_face(jnp.where(low, own_ref[...], nb_ref[...]), exp_ref[f])
+
+
 def first_kernel(
-    own_ref, pair_ref, up_ref, down_ref, exp_ref, dual, m_ref, a0, a1, a2, a3, lhs
-):
-    sides = amps_sides(own_ref[...], pair_ref[...], up_ref[...], down_ref[...])
-    for f, side in enumerate(sides):
+    own_ref, pair_ref, up_ref, down_ref, exp_ref, dual, m_ref, a0, a1, a2, a3, buf, lhs, sems
+):
+    rows = buf.shape[1]
+    copies = [
+        pltpu.make_async_copy(dual.at[n * rows : (n + 1) * rows, :], buf.at[n], sems.at[n])
+        for n in range(buf.shape[0])
+    ]
+    for copy in copies:
+        copy.start()
+    low = low_lanes((K, 128))
+    own, pair = own_ref[...], pair_ref[...]
+    for f, face in row_half(own_ref, up_ref, down_ref, exp_ref):
+        m_ref[f] = face
+        put(lhs, f, face)
+    for f, side in ((2, jnp.where(low, pair, own)), (3, jnp.where(low, own, pair))):
         face = expand_face(side, exp_ref[f])
         m_ref[f] = face
         put(lhs, f, face)
-    for f, a_ref in enumerate((a0, a1, a2, a3)):
-        a_ref[...] = apply_face(lhs, dual, f)
+    for n, copy in enumerate(copies):
+        copy.wait()
+        for f, a_ref in enumerate((a0, a1, a2, a3)):
+            part = product(lhs, n * rows, buf[n, :, f * FACE : (f + 1) * FACE])
+            a_ref[...] = part if n == 0 else a_ref[...] + part
 
 
 def ratio_of(sums_ref):
@@ -152,33 +174,31 @@
     return jnp.sum(jnp.where(rows == lanes, quot, 0.0), axis=1, keepdims=True)
 
 
+def add_clamped(has_ref, corr_ref, lhs, dual, faces):
+    for face in range(4):
+
+        @pl.when(has_ref[face] == 0)
+        def _():
+            hi, lo = split(corr_ref[face])
+            lhs[0:K, :] = hi
+            lhs[K : 2 * K, :] = lo
+            for f, a_ref in faces:
+                a_ref[...] = apply_rows(lhs, dual, f, a_ref[...], face * FACE)
+
+
 def step_kernel(
     has_ref, sums_ref, contact_ref, m_ref, p_ref, image_ref, o0, o1, o2, o3, dual,
     new_ref, a0, a1, a2, a3, lhs, corr,
 ):
     ratio = ratio_of(sums_ref)
-    for f in range(4):
+    faces = ((o0, a0), (o1, a1), (o2, a2), (o3, a3))
+    for f, (o_ref, a_ref) in enumerate(faces):
         plain = m_ref[f] - ratio * p_ref[f]
         new = jnp.where(contact_ref[f : f + 1, :] != 0, jnp.maximum(plain, 0.0), plain)
         new_ref[f] = new
         corr[f] = new - plain
-    faces = ((o0, a0), (o1, a1), (o2, a2), (o3, a3))
-    for f, (o_ref, a_ref) in enumerate(faces):
         a_ref[...] = o_ref[...] - ratio * image_ref[f]
-    for face in range(4):
-
-        @pl.when(has_ref[face] == 0)
-        def _():
-            hi, lo = split(corr[face])
-            lhs[0:K, :] = hi
-            lhs[K : 2 * K, :] = lo
-            for f, (_, a_ref) in enumerate(faces):
-                total = a_ref[...]
-                for first in range(0, FACE, DEPTH):
-                    row = face * FACE + first
-                    cols = slice(f * FACE, (f + 1) * FACE)
-                    total = total + product(lhs, first, dual[row : row + DEPTH, cols])
-                a_ref[...] = total
+    add_clamped(has_ref, corr, lhs, dual, [(f, a_ref) for f, (_, a_ref) in enumerate(faces)])
 
 
 def last_kernel(sums_ref, contact_ref, m_ref, p_ref, new_ref):
@@ -236,20 +256,20 @@
 
 
 def image_kernel(
-    has_ref, own_ref, pair_ref, up_ref, down_ref, grad_ref, exp_ref, dual, p_ref, image_ref, s_ref, lhs
-):
-    sides = amps_sides(own_ref[...], pair_ref[...], up_ref[...], down_ref[...])
+    has_ref, own_ref, up_ref, down_ref, grad_ref, half_ref, part_ref, exp_ref, dual,
+    p_ref, image_ref, s_ref, lhs,
+):
+    for f, face in row_half(own_ref, up_ref, down_ref, exp_ref):
+        p = grad_ref[f] - face
+        p_ref[f] = p
+        p_ref[f + 2] = half_ref[f]
+        put(lhs, f, p)
     numer = jnp.zeros((K, 1), F32)
-    for f, side in enumerate(sides):
-        grad = grad_ref[f]
-        p = grad - expand_face(side, exp_ref[f])
-        p_ref[f] = p
-        put(lhs, f, p)
-        weight = jnp.where(has_ref[f] != 0, 0.5, 1.0)
-        numer = numer + weight * jnp.sum(grad * p, axis=1, keepdims=True)
     denom = jnp.zeros((K, 1), F32)
     for f in range(4):
-        image = apply_face(lhs, dual, f)
+        weight = jnp.where(has_ref[f] != 0, 0.5, 1.0)
+        numer = numer + weight * jnp.sum(grad_ref[f] * p_ref[f], axis=1, keepdims=True)
+        image = apply_rows(lhs, dual, f, part_ref[f], 0)
         image_ref[f] = image
         denom = denom + jnp.sum(p_ref[f] * image, axis=1, keepdims=True)
     rows = lax.broadcasted_iota(jnp.int32, (K, 128), 0)
@@ -265,12 +285,9 @@
 
 
 def exchange(faces):
-    return (
-        along(faces[1], "row", 1),
-        along(faces[0], "row", -1),
-        along(faces[3], "col", 1),
-        along(faces[2], "col", -1),
-    )
+    right = along(faces[3], "col", 1)
+    left = along(faces[2], "col", -1)
+    return along(faces[1], "row", 1), along(faces[0], "row", -1), right, left
 
 
 def shards(dual_ops, basis, coarse_inverse, gap_rhs, coarse_rhs, contact_mask):
@@ -282,50 +299,76 @@
     vec = ((4, K, FACE), F32)
     face = ((K, FACE), F32)
     amps = ((K, 128), F32)
-    split_lhs = ((2 * K, M), BF16)
-
-    tile = split_tile(coarse_inverse)
-
-    def coarse(sent):
-        got = lax.all_to_all(sent, "row", 0, 0, tiled=True)
+    half = ((2, K, FACE), F32)
+    half_lhs = ((2 * K, M // 2), BF16)
+
+    def gather(sent):
+        return lax.all_to_all(sent, "row", 0, 0, tiled=True)
+
+    def amplitudes(got):
         (parts,) = call(
             coarse_kernel, [((n_cols, K + K // 2, 128), F32)], got, *tile,
             scratch=[((2 * K, n_rows * MDEV), BF16)],
         )
         parts = lax.all_to_all(parts, "col", 0, 0, tiled=True)
-        own, pair = call(amps_kernel, [amps, amps], parts)
-        return own, pair, along(own, "row", 1), along(own, "row", -1)
+        return call(amps_kernel, [amps, amps], parts)
+
+    def sides(own):
+        return along(own, "row", 1), along(own, "row", -1)
+
+    def col_half(own, pair, grad):
+        return call(
+            col_half_kernel, [half, vec], own, pair, grad, exp, dual,
+            scratch=[half_lhs], cost=8 << 20,
+        )
+
+    def first(*args):
+        slabs = 16
+        return pl.pallas_call(
+            first_kernel,
+            out_shape=[jax.ShapeDtypeStruct(*vec)] + [jax.ShapeDtypeStruct(*face)] * 4,
+            in_specs=[pl.BlockSpec(memory_space=pltpu.VMEM)] * (len(args) - 1)
+            + [pl.BlockSpec(memory_space=pltpu.HBM)],
+            out_specs=[pl.BlockSpec(memory_space=pltpu.VMEM)] * 5,
+            scratch_shapes=[
+                pltpu.VMEM((slabs, M // slabs, M), F32),
+                pltpu.VMEM((2 * K, M), BF16),
+                pltpu.SemaphoreType.DMA((slabs,)),
+            ],
+            compiler_params=pltpu.CompilerParams(vmem_limit_bytes=VMEM_LIMIT),
+        )(*args[:-1], pltpu.with_memory_space_constraint(args[-1], pltpu.HBM))
 
     rhs = coarse_rhs[0, 0]
     packed = jnp.concatenate([rhs[: K // 2], rhs[K // 2 :]], axis=1)
-    sent = jnp.broadcast_to(packed[None], (n_rows, K // 2, 2 * MDEV))
-
-    both = jnp.concatenate([basis[0, 0], gap_rhs[0, 0]], axis=1)
-    nbs = exchange([both[f] for f in range(4)])
+    got = gather(jnp.broadcast_to(packed[None], (n_rows, K // 2, 2 * MDEV)))
+    tile = split_tile(coarse_inverse)
+    mask = jnp.broadcast_to(contact_mask[0, 0, :, None, :].astype(F32), (4, 8, FACE))
+    both = jnp.concatenate([basis[0, 0], gap_rhs[0, 0], mask], axis=1)
+    both = [both[f] for f in range(4)]
+    own, pair = amplitudes(got)
+
+    nbs = exchange(both)
     exp, res, dvec, contact = call(
         weights_kernel,
         [((4, 256, FACE), BF16), ((M, 128), BF16), vec, ((4, FACE), jnp.int32)],
-        has_nb, contact_mask[0, 0], basis[0, 0], gap_rhs[0, 0], *nbs,
+        has_nb, *both, *nbs,
         smem=(0,),
     )
-
-    sides = coarse(sent)
-    exp, res, dvec, contact, sides = lax.optimization_barrier((exp, res, dvec, contact, sides))
-    multipliers, *faces = call(
-        first_kernel, [vec] + [face] * 4, *sides, exp, dual, scratch=[split_lhs]
-    )
+    multipliers, *faces = first(own, pair, *sides(own), exp, dual)
+    faces, res, dvec, contact = lax.optimization_barrier((faces, res, dvec, contact))
     for step in range(ITERS):
         grad, sent = call(
             grad_kernel,
             [vec, ((n_rows, K // 2, 128), F32)],
             has_nb, *faces, *exchange(faces), dvec, res,
-            scratch=[split_lhs], smem=(0,),
+            scratch=[((2 * K, M), BF16)], smem=(0,),
         )
+        own, pair = amplitudes(gather(sent))
         projected, image, sums = call(
             image_kernel,
             [vec, vec, ((n_rows * n_cols, 1, 128), F32)],
-            has_nb, *coarse(sent), grad, exp, dual,
-            scratch=[split_lhs], smem=(0,),
+            has_nb, own, *sides(own), grad, *col_half(own, pair, grad), exp, dual,
+            scratch=[half_lhs], smem=(0,),
         )
         sums = lax.all_to_all(sums, ("row", "col"), 0, 0, tiled=True)
         if step + 1 < ITERS:

time: 416 us -> 402 us (0.966)
  local copies, waits for them, and re-layouts: 12.4 us -> 4 us
  waiting for transfers between devices: 41.9 us -> 35.5 us
  blocking collectives: 229 us -> 224 us
  Pallas kernels: 52 us -> 56.6 us
    unnamed x14 -> x6, local copies, waits for them, and re-layouts: 11 us -> 2.54 us
    pallas_call x0 -> x1, Pallas kernels: none -> 6.27 us  [first(): pl.pallas_call(first_kernel, out_shape=[jax.ShapeDtypeStruct(*vec)] + [ja...]
    all_to_all x6, blocking collectives: 100 us -> 95.2 us  [shards(): sums = lax.all_to_all(sums, ('row', 'col'), 0, 0, tiled=True)]
    pallas_call x34 -> x39, Pallas kernels: 50.9 us -> 49.3 us  [call(): pl.pallas_call(kernel, out_shape=[jax.ShapeDtypeStruct(shape, dtype) for...]
  transfers between devices with their start and end apart: 44 -> 44, of which waited for: 20 -> 14; matrix products, arithmetic and copies ran while one was open for 1% -> 1% of each run, Pallas kernels for 1% -> 4%
where the time goes in v3:
time: 402 us; the launch traced here: 394 us
  blocking collectives  224 us (56%)
  starting transfers between devices  70.8 us (18%)
  Pallas kernels  56.6 us (14%)
  waiting for transfers between devices  35.5 us (9%)
    all_to_all x6, blocking collectives, shards(): sums = lax.all_to_all(sums, ('row', 'col'), 0, 0, tiled=True)  95.2 us
    all_to_all x6, blocking collectives, gather(): return lax.all_to_all(sent, 'row', 0, 0, tiled=True)  70.2 us
    all_to_all x6, blocking collectives, amplitudes(): parts = lax.all_to_all(parts, 'col', 0, 0, tiled=True)  58.3 us
    ppermute x42, starting transfers between devices, along(): return lax.ppermute(value, axis, [(i, (i + step) % n) for i in range(n)])  57.7 us
    pallas_call x39, Pallas kernels, call(): pl.pallas_call(kernel, out_shape=[jax.ShapeDtypeStruct(shape, dtype) for...  49.3 us
    ppermute x42, waiting for transfers between devices, along(): return lax.ppermute(value, axis, [(i, (i + step) % n) for i in range(n)])  35.5 us
  transfers between devices with their start and end apart: 44, of which 14 were waited for; matrix products, arithmetic and copies ran while one was open for 1% of the time, Pallas kernels for 4%

profile of v3, /device:TPU:1, one launch (start us, length us, event | category | flops | bytes accessed | tf_op | source)
XLA Modules:
  0.0 394.1 jit_solution(5315787191493897043)
XLA Ops:
  2.1 6.9 %all-to-all-start = ((f32[16,16,128]{2,1,0:T(8,128)}), f32[16,16,128]{2,1,0:T(8,128)S(1)}, u32[]{:S(2)}, u32[]{:S(2)}) async-start(f32[16,16,128]{2,1,0:T(8,128)} %broadcast_in_dim.8), calls=%async_computation | async-start | bytes 262144 | tf_op jit(solution)/shard_map/all_to_all | solution.py:306
  11.0 2.5 collective-permute-start.4
  17.4 6.2 %all-to-all-start.1 = ((f32[8,48,128]{2,1,0:T(8,128)}), f32[8,48,128]{2,1,0:T(8,128)S(1)}, u32[]{:S(2)}, u32[]{:S(2)}) async-start(f32[8,48,128]{2,1,0:T(8,128)} %shard_map.78), calls=%async_computation.1 | async-start | bytes 393216 | tf_op jit(solution)/shard_map/all_to_all | solution.py:313
  23.6 5.1 %collective-permute-start.5 = (f32[104,512]{1,0:T(8,128)S(1)}, f32[104,512]{1,0:T(8,128)}, u32[]{:S(2)}, u32[]{:S(2)}) collective-permute-start(f32[104,512]{1,0:T(8,128)S(1)} %get-tuple-element.199.o2), channel_id=1, source_target_pairs={{0,7},{1,0},{2,1},{3,2},{4,3},{5,4},{6,5},{7,6},{8,15},{9,8},{10,9... | collective-permute-start | bytes 638984 | tf_op jit(solution)/shard_map/ppermute | solution.py:284
  28.7 2.7 collective-permute-start.2
  31.5 2.7 collective-permute-start.1
  36.6 4.1 %collective-permute-done.3.n1 = f32[104,512]{1,0:T(8,128)} collective-permute-done((f32[104,512]{1,0:T(8,128)S(1)}, f32[104,512]{1,0:T(8,128)}, u32[]{:S(2)}, u32[]{:S(2)}) %collective-permute-start.3) | collective-permute-done | bytes 213024 | tf_op jit(solution)/shard_map/ppermute | solution.py:284
  42.1 6.3 %shard_map.81 = (f32[4,32,512]{2,1,0:T(8,128)S(1)}, f32[32,512]{1,0:T(8,128)S(1)}, f32[32,512]{1,0:T(8,128)S(1)}, f32[32,512]{1,0:T(8,128)S(1)}, f32[32,512]{1,0:T(8,128)S(1)}) custom-call(f32[32,128]{1,0:T(8,128)S(1)} %get-tuple-element.102.own_ref, f32[32,128]{1,0:T(8,128)S(1)} %get-tuple-element.103.pair_ref, f32[32,128]{1,0:T(8,128)S(1)} %collective-permute-done.up_ref, ...), custom_call_target="tpu_custom_call" | custom-call | tf_op jit(solution)/shard_map/pallas_call | solution.py:327
  50.2 2.9 collective-permute-start.9
  54.9 5.0 %collective-permute-done.8.n2 = f32[32,512]{1,0:T(8,128)S(1)} collective-permute-done((f32[32,512]{1,0:T(8,128)S(1)}, f32[32,512]{1,0:T(8,128)S(1)}, u32[]{:S(2)}, u32[]{:S(2)}) %collective-permute-start.8) | collective-permute-done | bytes 65568 | tf_op jit(solution)/shard_map/ppermute | solution.py:284
  60.7 11.2 %all_to_all.100.x_ref = f32[16,16,128]{2,1,0:T(8,128)S(1)} all-to-all(f32[16,16,128]{2,1,0:T(8,128)S(1)} %get-tuple-element.118), channel_id=1, replica_groups=mesh['row'=16,'col'=8] {'row'}, dimensions={0} | all-to-all | bytes 262144 | tf_op jit(solution)/shard_map/all_to_all | solution.py:306
  72.6 9.7 %all_to_all.101.parts_ref = f32[8,48,128]{2,1,0:T(8,128)S(1)} all-to-all(f32[8,48,128]{2,1,0:T(8,128)S(1)} %shard_map.83), channel_id=1, replica_groups=mesh['row'=16,'col'=8] {'col'}, dimensions={0} | all-to-all | bytes 393216 | tf_op jit(solution)/shard_map/all_to_all | solution.py:313
  84.8 1.9 shard_map.85
  86.7 2.6 shard_map.86
  89.2 15.9 %all_to_all.102.sums_ref = f32[128,1,128]{2,1,0:T(1,128)S(1)} all-to-all(f32[128,1,128]{2,1,0:T(1,128)S(1)} %get-tuple-element.124), channel_id=1, replica_groups=mesh['row'=16,'col'=8] {'row','col'}, dimensions={0} | all-to-all | bytes 131072 | tf_op jit(solution)/shard_map/all_to_all | solution.py:373
  109.7 2.0 collective-permute-start.14
  113.4 3.1 collective-permute-done.14.n2
  117.3 11.8 %all_to_all.103.x_ref = f32[16,16,128]{2,1,0:T(8,128)S(1)} all-to-all(f32[16,16,128]{2,1,0:T(8,128)S(1)} %get-tuple-element.133), channel_id=1, replica_groups=mesh['row'=16,'col'=8] {'row'}, dimensions={0} | all-to-all | bytes 262144 | tf_op jit(solution)/shard_map/all_to_all | solution.py:306
  129.7 9.7 %all_to_all.104.parts_ref = f32[8,48,128]{2,1,0:T(8,128)S(1)} all-to-all(f32[8,48,128]{2,1,0:T(8,128)S(1)} %shard_map.89), channel_id=1, replica_groups=mesh['row'=16,'col'=8] {'col'}, dimensions={0} | all-to-all | bytes 393216 | tf_op jit(solution)/shard_map/all_to_all | solution.py:313
  142.1 1.9 shard_map.91
  144.0 2.6 shard_map.92
  146.6 15.9 %all_to_all.105.sums_ref = f32[128,1,128]{2,1,0:T(1,128)S(1)} all-to-all(f32[128,1,128]{2,1,0:T(1,128)S(1)} %get-tuple-element.139), channel_id=1, replica_groups=mesh['row'=16,'col'=8] {'row','col'}, dimensions={0} | all-to-all | bytes 131072 | tf_op jit(solution)/shard_map/all_to_all | solution.py:373
  167.1 2.0 collective-permute-start.20
  170.7 3.1 collective-permute-done.20.n2
  174.6 11.8 %all_to_all.106.x_ref = f32[16,16,128]{2,1,0:T(8,128)S(1)} all-to-all(f32[16,16,128]{2,1,0:T(8,128)S(1)} %get-tuple-element.147), channel_id=1, replica_groups=mesh['row'=16,'col'=8] {'row'}, dimensions={0} | all-to-all | bytes 262144 | tf_op jit(solution)/shard_map/all_to_all | solution.py:306
  187.0 9.7 %all_to_all.107.parts_ref = f32[8,48,128]{2,1,0:T(8,128)S(1)} all-to-all(f32[8,48,128]{2,1,0:T(8,128)S(1)} %shard_map.95), channel_id=1, replica_groups=mesh['row'=16,'col'=8] {'col'}, dimensions={0} | all-to-all | bytes 393216 | tf_op jit(solution)/shard_map/all_to_all | solution.py:313
  199.2 1.9 shard_map.97
  201.1 2.6 shard_map.98
  203.7 15.9 %all_to_all.108.sums_ref = f32[128,1,128]{2,1,0:T(1,128)S(1)} all-to-all(f32[128,1,128]{2,1,0:T(1,128)S(1)} %get-tuple-element.153), channel_id=1, replica_groups=mesh['row'=16,'col'=8] {'row','col'}, dimensions={0} | all-to-all | bytes 131072 | tf_op jit(solution)/shard_map/all_to_all | solution.py:373
  224.2 2.0 collective-permute-start.26
  227.8 3.1 collective-permute-done.26.n2
  231.7 11.8 %all_to_all.109.x_ref = f32[16,16,128]{2,1,0:T(8,128)S(1)} all-to-all(f32[16,16,128]{2,1,0:T(8,128)S(1)} %get-tuple-element.161), channel_id=1, replica_groups=mesh['row'=16,'col'=8] {'row'}, dimensions={0} | all-to-all | bytes 262144 | tf_op jit(solution)/shard_map/all_to_all | solution.py:306
  244.1 9.7 %all_to_all.110.parts_ref = f32[8,48,128]{2,1,0:T(8,128)S(1)} all-to-all(f32[8,48,128]{2,1,0:T(8,128)S(1)} %shard_map.101), channel_id=1, replica_groups=mesh['row'=16,'col'=8] {'col'}, dimensions={0} | all-to-all | bytes 393216 | tf_op jit(solution)/shard_map/all_to_all | solution.py:313
  258.2 2.6 shard_map.104
  260.8 15.9 %all_to_all.111.sums_ref = f32[128,1,128]{2,1,0:T(1,128)S(1)} all-to-all(f32[128,1,128]{2,1,0:T(1,128)S(1)} %get-tuple-element.167), channel_id=1, replica_groups=mesh['row'=16,'col'=8] {'row','col'}, dimensions={0} | all-to-all | bytes 131072 | tf_op jit(solution)/shard_map/all_to_all | solution.py:373
  281.3 2.0 collective-permute-start.32
  284.9 3.1 collective-permute-done.32.n2
  288.9 11.8 %all_to_all.112.x_ref = f32[16,16,128]{2,1,0:T(8,128)S(1)} all-to-all(f32[16,16,128]{2,1,0:T(8,128)S(1)} %get-tuple-element.175), channel_id=1, replica_groups=mesh['row'=16,'col'=8] {'row'}, dimensions={0} | all-to-all | bytes 262144 | tf_op jit(solution)/shard_map/all_to_all | solution.py:306
  301.3 9.7 %all_to_all.113.parts_ref = f32[8,48,128]{2,1,0:T(8,128)S(1)} all-to-all(f32[8,48,128]{2,1,0:T(8,128)S(1)} %shard_map.107), channel_id=1, replica_groups=mesh['row'=16,'col'=8] {'col'}, dimensions={0} | all-to-all | bytes 393216 | tf_op jit(solution)/shard_map/all_to_all | solution.py:313
  315.4 2.6 shard_map.110
  318.0 15.9 %all_to_all.114.sums_ref = f32[128,1,128]{2,1,0:T(1,128)S(1)} all-to-all(f32[128,1,128]{2,1,0:T(1,128)S(1)} %get-tuple-element.181), channel_id=1, replica_groups=mesh['row'=16,'col'=8] {'row','col'}, dimensions={0} | all-to-all | bytes 131072 | tf_op jit(solution)/shard_map/all_to_all | solution.py:373
  338.5 2.0 collective-permute-start.38
  342.1 3.1 collective-permute-done.38.n2
  346.0 11.8 %all_to_all.115.x_ref = f32[16,16,128]{2,1,0:T(8,128)S(1)} all-to-all(f32[16,16,128]{2,1,0:T(8,128)S(1)} %get-tuple-element.189), channel_id=1, replica_groups=mesh['row'=16,'col'=8] {'row'}, dimensions={0} | all-to-all | bytes 262144 | tf_op jit(solution)/shard_map/all_to_all | solution.py:306
  358.4 9.7 %all_to_all.116.parts_ref = f32[8,48,128]{2,1,0:T(8,128)S(1)} all-to-all(f32[8,48,128]{2,1,0:T(8,128)S(1)} %shard_map.113), channel_id=1, replica_groups=mesh['row'=16,'col'=8] {'col'}, dimensions={0} | all-to-all | bytes 393216 | tf_op jit(solution)/shard_map/all_to_all | solution.py:313
  370.7 1.9 shard_map.115
  372.6 3.2 shard_map.116
  375.8 15.9 %all_to_all.117.sums_ref = f32[128,1,128]{2,1,0:T(1,128)S(1)} all-to-all(f32[128,1,128]{2,1,0:T(1,128)S(1)} %get-tuple-element.195), channel_id=1, replica_groups=mesh['row'=16,'col'=8] {'row','col'}, dimensions={0} | all-to-all | bytes 131072 | tf_op jit(solution)/shard_map/all_to_all | solution.py:373
  (113 shorter events, 75.6 us)
Async XLA Ops:
  2.1 14.1 %all-to-all-start = ((f32[16,16,128]{2,1,0:T(8,128)}), f32[16,16,128]{2,1,0:T(8,128)S(1)}, u32[]{:S(2)}, u32[]{:S(2)}) async-start(f32[16,16,128]{2,1,0:T(8,128)} %broadcast_in_dim.8), calls=%async_computation | async-start | bytes 262144 | tf_op jit(solution)/shard_map/all_to_all | solution.py:306
  11.0 23.2 %collective-permute-start.4 = (f32[104,512]{1,0:T(8,128)S(1)}, f32[104,512]{1,0:T(8,128)S(1)}, u32[]{:S(2)}, u32[]{:S(2)}) collective-permute-start(f32[104,512]{1,0:T(8,128)S(1)} %get-tuple-element.198.o3), channel_id=1, source_target_pairs={{0,1},{1,2},{2,3},{3,4},{4,5},{5,6},{6,7},{7,0},{8,9},{9,10},{10,1... | collective-permute-start | bytes 638984 | tf_op jit(solution)/shard_map/ppermute | solution.py:284
  13.5 1.6 copy-start.1
  17.4 14.0 %all-to-all-start.1 = ((f32[8,48,128]{2,1,0:T(8,128)}), f32[8,48,128]{2,1,0:T(8,128)S(1)}, u32[]{:S(2)}, u32[]{:S(2)}) async-start(f32[8,48,128]{2,1,0:T(8,128)} %shard_map.78), calls=%async_computation.1 | async-start | bytes 393216 | tf_op jit(solution)/shard_map/all_to_all | solution.py:313
  23.6 11.9 %collective-permute-start.5 = (f32[104,512]{1,0:T(8,128)S(1)}, f32[104,512]{1,0:T(8,128)}, u32[]{:S(2)}, u32[]{:S(2)}) collective-permute-start(f32[104,512]{1,0:T(8,128)S(1)} %get-tuple-element.199.o2), channel_id=1, source_target_pairs={{0,7},{1,0},{2,1},{3,2},{4,3},{5,4},{6,5},{7,6},{8,15},{9,8},{10,9... | collective-permute-start | bytes 638984 | tf_op jit(solution)/shard_map/ppermute | solution.py:284
  28.7 7.9 %collective-permute-start.2 = (f32[104,512]{1,0:T(8,128)S(1)}, f32[104,512]{1,0:T(8,128)}, u32[]{:S(2)}, u32[]{:S(2)}) collective-permute-start(f32[104,512]{1,0:T(8,128)S(1)} %get-tuple-element.200.o1), channel_id=1, source_target_pairs={{0,8},{8,16},{16,24},{24,32},{32,40},{40,48},{48,56},{56,64},{64,7... | collective-permute-start | bytes 638984 | tf_op jit(solution)/shard_map/ppermute | solution.py:284
  31.4 9.3 %collective-permute-start.3 = (f32[104,512]{1,0:T(8,128)S(1)}, f32[104,512]{1,0:T(8,128)}, u32[]{:S(2)}, u32[]{:S(2)}) collective-permute-start(f32[104,512]{1,0:T(8,128)S(1)} %get-tuple-element.201.o0), channel_id=1, source_target_pairs={{0,120},{8,0},{16,8},{24,16},{32,24},{40,32},{48,40},{56,48},{64,5... | collective-permute-start | bytes 638984 | tf_op jit(solution)/shard_map/ppermute | solution.py:284
  31.4 53.4 %copy-start = (f32[1,1,2048,2048]{3,2,1,0:T(8,128)S(1)}, f32[1,1,2048,2048]{3,2,1,0:T(8,128)}, u32[]{:S(2)}) copy-start(f32[1,1,2048,2048]{3,2,1,0:T(8,128)} %param.6) | copy-start | bytes 50331652
  31.5 10.6 %collective-permute-start.1 = (f32[32,128]{1,0:T(8,128)S(1)}, f32[32,128]{1,0:T(8,128)S(1)}, u32[]{:S(2)}, u32[]{:S(2)}) collective-permute-start(f32[32,128]{1,0:T(8,128)S(1)} %get-tuple-element.102.own_ref), channel_id=1, source_target_pairs={{0,120},{8,0},{16,8},{24,16},{32,24},{40,32},{48,40},{56,48},{64,5... | collective-permute-start | bytes 49160 | tf_op jit(solution)/shard_map/ppermute | solution.py:284
  34.2 7.9 %collective-permute-start = (f32[32,128]{1,0:T(8,128)S(1)}, f32[32,128]{1,0:T(8,128)S(1)}, u32[]{:S(2)}, u32[]{:S(2)}) collective-permute-start(f32[32,128]{1,0:T(8,128)S(1)} %get-tuple-element.102.own_ref), channel_id=1, source_target_pairs={{0,8},{8,16},{16,24},{24,32},{32,40},{40,48},{48,56},{56,64},{64,7... | collective-permute-start | bytes 49160 | tf_op jit(solution)/shard_map/ppermute | solution.py:284
  48.4 4.8 %collective-permute-start.7 = (f32[32,512]{1,0:T(8,128)S(1)}, f32[32,512]{1,0:T(8,128)S(1)}, u32[]{:S(2)}, u32[]{:S(2)}) collective-permute-start(f32[32,512]{1,0:T(8,128)S(1)} %get-tuple-element.112.a0.o0), channel_id=1, source_target_pairs={{0,120},{8,0},{16,8},{24,16},{32,24},{40,32},{48,40},{56,48},{64,5... | collective-permute-start | bytes 196616 | tf_op jit(solution)/shard_map/ppermute | solution.py:284
  49.1 4.1 %collective-permute-start.6 = (f32[32,512]{1,0:T(8,128)S(1)}, f32[32,512]{1,0:T(8,128)S(1)}, u32[]{:S(2)}, u32[]{:S(2)}) collective-permute-start(f32[32,512]{1,0:T(8,128)S(1)} %get-tuple-element.113.a1.o1), channel_id=1, source_target_pairs={{0,8},{8,16},{16,24},{24,32},{32,40},{40,48},{48,56},{56,64},{64,7... | collective-permute-start | bytes 196616 | tf_op jit(solution)/shard_map/ppermute | solution.py:284
  50.2 4.6 %collective-permute-start.9 = (f32[32,512]{1,0:T(8,128)S(1)}, f32[32,512]{1,0:T(8,128)S(1)}, u32[]{:S(2)}, u32[]{:S(2)}) collective-permute-start(f32[32,512]{1,0:T(8,128)S(1)} %get-tuple-element.114.a2.o2), channel_id=1, source_target_pairs={{0,7},{1,0},{2,1},{3,2},{4,3},{5,4},{6,5},{7,6},{8,15},{9,8},{10,9... | collective-permute-start | bytes 196616 | tf_op jit(solution)/shard_map/ppermute | solution.py:284
  53.2 6.7 %collective-permute-start.8 = (f32[32,512]{1,0:T(8,128)S(1)}, f32[32,512]{1,0:T(8,128)S(1)}, u32[]{:S(2)}, u32[]{:S(2)}) collective-permute-start(f32[32,512]{1,0:T(8,128)S(1)} %get-tuple-element.115.a3.o3), channel_id=1, source_target_pairs={{0,1},{1,2},{2,3},{3,4},{4,5},{5,6},{6,7},{7,0},{8,9},{9,10},{10,1... | collective-permute-start | bytes 196616 | tf_op jit(solution)/shard_map/ppermute | solution.py:284
  82.4 4.3 %collective-permute-start.11 = (f32[32,128]{1,0:T(8,128)S(1)}, f32[32,128]{1,0:T(8,128)S(1)}, u32[]{:S(2)}, u32[]{:S(2)}) collective-permute-start(f32[32,128]{1,0:T(8,128)S(1)} %get-tuple-element.119.own_ref), channel_id=1, source_target_pairs={{0,120},{8,0},{16,8},{24,16},{32,24},{40,32},{48,40},{56,48},{64,5... | collective-permute-start | bytes 49160 | tf_op jit(solution)/shard_map/ppermute | solution.py:284
  84.2 2.5 collective-permute-start.10
  107.0 4.8 %collective-permute-start.13 = (f32[32,512]{1,0:T(8,128)S(1)}, f32[32,512]{1,0:T(8,128)S(1)}, u32[]{:S(2)}, u32[]{:S(2)}) collective-permute-start(f32[32,512]{1,0:T(8,128)S(1)} %get-tuple-element.129.a0.o0), channel_id=1, source_target_pairs={{0,120},{8,0},{16,8},{24,16},{32,24},{40,32},{48,40},{56,48},{64,5... | collective-permute-start | bytes 196616 | tf_op jit(solution)/shard_map/ppermute | solution.py:284
  108.3 3.5 collective-permute-start.12
  108.8 4.6 %collective-permute-start.15 = (f32[32,512]{1,0:T(8,128)S(1)}, f32[32,512]{1,0:T(8,128)S(1)}, u32[]{:S(2)}, u32[]{:S(2)}) collective-permute-start(f32[32,512]{1,0:T(8,128)S(1)} %get-tuple-element.131.a2.o2), channel_id=1, source_target_pairs={{0,7},{1,0},{2,1},{3,2},{4,3},{5,4},{6,5},{7,6},{8,15},{9,8},{10,9... | collective-permute-start | bytes 196616 | tf_op jit(solution)/shard_map/ppermute | solution.py:284
  109.7 6.7 %collective-permute-start.14 = (f32[32,512]{1,0:T(8,128)S(1)}, f32[32,512]{1,0:T(8,128)S(1)}, u32[]{:S(2)}, u32[]{:S(2)}) collective-permute-start(f32[32,512]{1,0:T(8,128)S(1)} %get-tuple-element.132.a3.o3), channel_id=1, source_target_pairs={{0,1},{1,2},{2,3},{3,4},{4,5},{5,6},{6,7},{7,0},{8,9},{9,10},{10,1... | collective-permute-start | bytes 196616 | tf_op jit(solution)/shard_map/ppermute | solution.py:284
  139.5 4.5 %collective-permute-start.17 = (f32[32,128]{1,0:T(8,128)S(1)}, f32[32,128]{1,0:T(8,128)S(1)}, u32[]{:S(2)}, u32[]{:S(2)}) collective-permute-start(f32[32,128]{1,0:T(8,128)S(1)} %get-tuple-element.134.own_ref), channel_id=1, source_target_pairs={{0,120},{8,0},{16,8},{24,16},{32,24},{40,32},{48,40},{56,48},{64,5... | collective-permute-start | bytes 49160 | tf_op jit(solution)/shard_map/ppermute | solution.py:284
  141.3 2.7 collective-permute-start.16
  164.3 4.8 %collective-permute-start.19 = (f32[32,512]{1,0:T(8,128)S(1)}, f32[32,512]{1,0:T(8,128)S(1)}, u32[]{:S(2)}, u32[]{:S(2)}) collective-permute-start(f32[32,512]{1,0:T(8,128)S(1)} %get-tuple-element.143.a0.o0), channel_id=1, source_target_pairs={{0,120},{8,0},{16,8},{24,16},{32,24},{40,32},{48,40},{56,48},{64,5... | collective-permute-start | bytes 196616 | tf_op jit(solution)/shard_map/ppermute | solution.py:284
  165.6 3.5 collective-permute-start.18
  166.1 4.6 %collective-permute-start.21 = (f32[32,512]{1,0:T(8,128)S(1)}, f32[32,512]{1,0:T(8,128)S(1)}, u32[]{:S(2)}, u32[]{:S(2)}) collective-permute-start(f32[32,512]{1,0:T(8,128)S(1)} %get-tuple-element.145.a2.o2), channel_id=1, source_target_pairs={{0,7},{1,0},{2,1},{3,2},{4,3},{5,4},{6,5},{7,6},{8,15},{9,8},{10,9... | collective-permute-start | bytes 196616 | tf_op jit(solution)/shard_map/ppermute | solution.py:284
  167.1 6.7 %collective-permute-start.20 = (f32[32,512]{1,0:T(8,128)S(1)}, f32[32,512]{1,0:T(8,128)S(1)}, u32[]{:S(2)}, u32[]{:S(2)}) collective-permute-start(f32[32,512]{1,0:T(8,128)S(1)} %get-tuple-element.146.a3.o3), channel_id=1, source_target_pairs={{0,1},{1,2},{2,3},{3,4},{4,5},{5,6},{6,7},{7,0},{8,9},{9,10},{10,1... | collective-permute-start | bytes 196616 | tf_op jit(solution)/shard_map/ppermute | solution.py:284
  196.8 4.2 %collective-permute-start.23 = (f32[32,128]{1,0:T(8,128)S(1)}, f32[32,128]{1,0:T(8,128)S(1)}, u32[]{:S(2)}, u32[]{:S(2)}) collective-permute-start(f32[32,128]{1,0:T(8,128)S(1)} %get-tuple-element.148.own_ref), channel_id=1, source_target_pairs={{0,120},{8,0},{16,8},{24,16},{32,24},{40,32},{48,40},{56,48},{64,5... | collective-permute-start | bytes 49160 | tf_op jit(solution)/shard_map/ppermute | solution.py:284
  198.6 2.4 collective-permute-start.22
  221.4 4.8 %collective-permute-start.25 = (f32[32,512]{1,0:T(8,128)S(1)}, f32[32,512]{1,0:T(8,128)S(1)}, u32[]{:S(2)}, u32[]{:S(2)}) collective-permute-start(f32[32,512]{1,0:T(8,128)S(1)} %get-tuple-element.157.a0.o0), channel_id=1, source_target_pairs={{0,120},{8,0},{16,8},{24,16},{32,24},{40,32},{48,40},{56,48},{64,5... | collective-permute-start | bytes 196616 | tf_op jit(solution)/shard_map/ppermute | solution.py:284
  222.7 3.5 collective-permute-start.24
  223.2 4.6 %collective-permute-start.27 = (f32[32,512]{1,0:T(8,128)S(1)}, f32[32,512]{1,0:T(8,128)S(1)}, u32[]{:S(2)}, u32[]{:S(2)}) collective-permute-start(f32[32,512]{1,0:T(8,128)S(1)} %get-tuple-element.159.a2.o2), channel_id=1, source_target_pairs={{0,7},{1,0},{2,1},{3,2},{4,3},{5,4},{6,5},{7,6},{8,15},{9,8},{10,9... | collective-permute-start | bytes 196616 | tf_op jit(solution)/shard_map/ppermute | solution.py:284
  224.2 6.7 %collective-permute-start.26 = (f32[32,512]{1,0:T(8,128)S(1)}, f32[32,512]{1,0:T(8,128)S(1)}, u32[]{:S(2)}, u32[]{:S(2)}) collective-permute-start(f32[32,512]{1,0:T(8,128)S(1)} %get-tuple-element.160.a3.o3), channel_id=1, source_target_pairs={{0,1},{1,2},{2,3},{3,4},{4,5},{5,6},{6,7},{7,0},{8,9},{9,10},{10,1... | collective-permute-start | bytes 196616 | tf_op jit(solution)/shard_map/ppermute | solution.py:284
  253.9 4.3 %collective-permute-start.29 = (f32[32,128]{1,0:T(8,128)S(1)}, f32[32,128]{1,0:T(8,128)S(1)}, u32[]{:S(2)}, u32[]{:S(2)}) collective-permute-start(f32[32,128]{1,0:T(8,128)S(1)} %get-tuple-element.162.own_ref), channel_id=1, source_target_pairs={{0,120},{8,0},{16,8},{24,16},{32,24},{40,32},{48,40},{56,48},{64,5... | collective-permute-start | bytes 49160 | tf_op jit(solution)/shard_map/ppermute | solution.py:284
  255.8 2.5 collective-permute-start.28
  278.5 4.8 %collective-permute-start.31 = (f32[32,512]{1,0:T(8,128)S(1)}, f32[32,512]{1,0:T(8,128)S(1)}, u32[]{:S(2)}, u32[]{:S(2)}) collective-permute-start(f32[32,512]{1,0:T(8,128)S(1)} %get-tuple-element.171.a0.o0), channel_id=1, source_target_pairs={{0,120},{8,0},{16,8},{24,16},{32,24},{40,32},{48,40},{56,48},{64,5... | collective-permute-start | bytes 196616 | tf_op jit(solution)/shard_map/ppermute | solution.py:284
  279.8 3.5 collective-permute-start.30
  280.3 4.6 %collective-permute-start.33 = (f32[32,512]{1,0:T(8,128)S(1)}, f32[32,512]{1,0:T(8,128)S(1)}, u32[]{:S(2)}, u32[]{:S(2)}) collective-permute-start(f32[32,512]{1,0:T(8,128)S(1)} %get-tuple-element.173.a2.o2), channel_id=1, source_target_pairs={{0,7},{1,0},{2,1},{3,2},{4,3},{5,4},{6,5},{7,6},{8,15},{9,8},{10,9... | collective-permute-start | bytes 196616 | tf_op jit(solution)/shard_map/ppermute | solution.py:284
  281.3 6.7 %collective-permute-start.32 = (f32[32,512]{1,0:T(8,128)S(1)}, f32[32,512]{1,0:T(8,128)S(1)}, u32[]{:S(2)}, u32[]{:S(2)}) collective-permute-start(f32[32,512]{1,0:T(8,128)S(1)} %get-tuple-element.174.a3.o3), channel_id=1, source_target_pairs={{0,1},{1,2},{2,3},{3,4},{4,5},{5,6},{6,7},{7,0},{8,9},{9,10},{10,1... | collective-permute-start | bytes 196616 | tf_op jit(solution)/shard_map/ppermute | solution.py:284
  311.1 4.3 %collective-permute-start.35 = (f32[32,128]{1,0:T(8,128)S(1)}, f32[32,128]{1,0:T(8,128)S(1)}, u32[]{:S(2)}, u32[]{:S(2)}) collective-permute-start(f32[32,128]{1,0:T(8,128)S(1)} %get-tuple-element.176.own_ref), channel_id=1, source_target_pairs={{0,120},{8,0},{16,8},{24,16},{32,24},{40,32},{48,40},{56,48},{64,5... | collective-permute-start | bytes 49160 | tf_op jit(solution)/shard_map/ppermute | solution.py:284
  312.9 2.5 collective-permute-start.34
  335.7 4.8 %collective-permute-start.37 = (f32[32,512]{1,0:T(8,128)S(1)}, f32[32,512]{1,0:T(8,128)S(1)}, u32[]{:S(2)}, u32[]{:S(2)}) collective-permute-start(f32[32,512]{1,0:T(8,128)S(1)} %get-tuple-element.185.a0), channel_id=1, source_target_pairs={{0,120},{8,0},{16,8},{24,16},{32,24},{40,32},{48,40},{56,48},{64,5... | collective-permute-start | bytes 196616 | tf_op jit(solution)/shard_map/ppermute | solution.py:284
  337.0 3.5 collective-permute-start.36
  337.5 4.6 %collective-permute-start.39 = (f32[32,512]{1,0:T(8,128)S(1)}, f32[32,512]{1,0:T(8,128)S(1)}, u32[]{:S(2)}, u32[]{:S(2)}) collective-permute-start(f32[32,512]{1,0:T(8,128)S(1)} %get-tuple-element.187.a2), channel_id=1, source_target_pairs={{0,7},{1,0},{2,1},{3,2},{4,3},{5,4},{6,5},{7,6},{8,15},{9,8},{10,9... | collective-permute-start | bytes 196616 | tf_op jit(solution)/shard_map/ppermute | solution.py:284
  338.5 6.7 %collective-permute-start.38 = (f32[32,512]{1,0:T(8,128)S(1)}, f32[32,512]{1,0:T(8,128)S(1)}, u32[]{:S(2)}, u32[]{:S(2)}) collective-permute-start(f32[32,512]{1,0:T(8,128)S(1)} %get-tuple-element.188.a3), channel_id=1, source_target_pairs={{0,1},{1,2},{2,3},{3,4},{4,5},{5,6},{6,7},{7,0},{8,9},{9,10},{10,1... | collective-permute-start | bytes 196616 | tf_op jit(solution)/shard_map/ppermute | solution.py:284
  368.2 4.4 %collective-permute-start.41 = (f32[32,128]{1,0:T(8,128)S(1)}, f32[32,128]{1,0:T(8,128)S(1)}, u32[]{:S(2)}, u32[]{:S(2)}) collective-permute-start(f32[32,128]{1,0:T(8,128)S(1)} %get-tuple-element.190.own_ref), channel_id=1, source_target_pairs={{0,120},{8,0},{16,8},{24,16},{32,24},{40,32},{48,40},{56,48},{64,5... | collective-permute-start | bytes 49160 | tf_op jit(solution)/shard_map/ppermute | solution.py:284
  370.1 2.5 collective-permute-start.40
  391.6 1.0 copy-start.2

commit v4 on v3

--- a/solution.py
+++ b/solution.py
@@ -174,7 +174,7 @@
     return jnp.sum(jnp.where(rows == lanes, quot, 0.0), axis=1, keepdims=True)
 
 
-def add_clamped(has_ref, corr_ref, lhs, dual, faces):
+def add_clamped(has_ref, corr_ref, lhs, dual, faces, shared):
     for face in range(4):
 
         @pl.when(has_ref[face] == 0)
@@ -182,13 +182,16 @@
             hi, lo = split(corr_ref[face])
             lhs[0:K, :] = hi
             lhs[K : 2 * K, :] = lo
-            for f, a_ref in faces:
-                a_ref[...] = apply_rows(lhs, dual, f, a_ref[...], face * FACE)
+            for f, a_ref in enumerate(faces):
+
+                @pl.when((has_ref[f] != 0) == shared)
+                def _():
+                    a_ref[...] = apply_rows(lhs, dual, f, a_ref[...], face * FACE)
 
 
 def step_kernel(
     has_ref, sums_ref, contact_ref, m_ref, p_ref, image_ref, o0, o1, o2, o3, dual,
-    new_ref, a0, a1, a2, a3, lhs, corr,
+    new_ref, corr, a0, a1, a2, a3, lhs,
 ):
     ratio = ratio_of(sums_ref)
     faces = ((o0, a0), (o1, a1), (o2, a2), (o3, a3))
@@ -198,7 +201,13 @@
         new_ref[f] = new
         corr[f] = new - plain
         a_ref[...] = o_ref[...] - ratio * image_ref[f]
-    add_clamped(has_ref, corr, lhs, dual, [(f, a_ref) for f, (_, a_ref) in enumerate(faces)])
+    add_clamped(has_ref, corr, lhs, dual, (a0, a1, a2, a3), True)
+
+
+def outer_kernel(has_ref, corr, o0, o1, o2, o3, dual, a0, a1, a2, a3, lhs):
+    for o_ref, a_ref in ((o0, a0), (o1, a1), (o2, a2), (o3, a3)):
+        a_ref[...] = o_ref[...]
+    add_clamped(has_ref, corr, lhs, dual, (a0, a1, a2, a3), False)
 
 
 def last_kernel(sums_ref, contact_ref, m_ref, p_ref, new_ref):
@@ -356,11 +365,12 @@
     )
     multipliers, *faces = first(own, pair, *sides(own), exp, dual)
     faces, res, dvec, contact = lax.optimization_barrier((faces, res, dvec, contact))
+    nbs = exchange(faces)
     for step in range(ITERS):
         grad, sent = call(
             grad_kernel,
             [vec, ((n_rows, K // 2, 128), F32)],
-            has_nb, *faces, *exchange(faces), dvec, res,
+            has_nb, *faces, *nbs, dvec, res,
             scratch=[((2 * K, M), BF16)], smem=(0,),
         )
         own, pair = amplitudes(gather(sent))
@@ -372,10 +382,15 @@
         )
         sums = lax.all_to_all(sums, ("row", "col"), 0, 0, tiled=True)
         if step + 1 < ITERS:
-            multipliers, *faces = call(
-                step_kernel, [vec] + [face] * 4,
+            multipliers, corr, *sent_faces = call(
+                step_kernel, [vec, vec] + [face] * 4,
                 has_nb, sums, contact, multipliers, projected, image, *faces, dual,
-                scratch=[((2 * K, FACE), BF16), vec], smem=(0,),
+                scratch=[((2 * K, FACE), BF16)], smem=(0,),
+            )
+            nbs = exchange(sent_faces)
+            faces = call(
+                outer_kernel, [face] * 4, has_nb, corr, *sent_faces, dual,
+                scratch=[((2 * K, FACE), BF16)], smem=(0,), cost=4 << 20,
             )
         else:
             (multipliers,) = call(last_kernel, [vec], sums, contact, multipliers, projected)

time: 402 us -> 398 us (0.990)
  waiting for transfers between devices: 35.5 us -> 30 us
  Pallas kernels: 56.6 us -> 62 us
    ppermute x42, waiting for transfers between devices: 35.5 us -> 30 us  [along(): return lax.ppermute(value, axis, [(i, (i + step) % n) for i in range(n)])]
    pallas_call x39 -> x44, Pallas kernels: 49.3 us -> 54.7 us  [call(): pl.pallas_call(kernel, out_shape=[jax.ShapeDtypeStruct(shape, dtype) for...]
  transfers between devices with their start and end apart: 44 -> 44, of which waited for: 14 -> 14; matrix products, arithmetic and copies ran while one was open for 1% -> 1% of each run, Pallas kernels for 4% -> 5%
where the time goes in v4:
time: 398 us; the launch traced here: 390 us
  blocking collectives  222 us (56%)
  starting transfers between devices  69.5 us (17%)
  Pallas kernels  62 us (16%)
  waiting for transfers between devices  30 us (8%)
  local copies, waits for them, and re-layouts  4 us (1%)
    all_to_all x6, blocking collectives, shards(): sums = lax.all_to_all(sums, ('row', 'col'), 0, 0, tiled=True)  95.7 us
    all_to_all x6, blocking collectives, gather(): return lax.all_to_all(sent, 'row', 0, 0, tiled=True)  67.1 us
    all_to_all x6, blocking collectives, amplitudes(): parts = lax.all_to_all(parts, 'col', 0, 0, tiled=True)  58.7 us
    ppermute x42, starting transfers between devices, along(): return lax.ppermute(value, axis, [(i, (i + step) % n) for i in range(n)])  56.4 us
    pallas_call x44, Pallas kernels, call(): pl.pallas_call(kernel, out_shape=[jax.ShapeDtypeStruct(shape, dtype) for...  54.7 us
    ppermute x42, waiting for transfers between devices, along(): return lax.ppermute(value, axis, [(i, (i + step) % n) for i in range(n)])  30 us
  transfers between devices with their start and end apart: 44, of which 14 were waited for; matrix products, arithmetic and copies ran while one was open for 1% of the time, Pallas kernels for 5%

profile of v4, /device:TPU:1, one launch (start us, length us, event | category | flops | bytes accessed | tf_op | source)
XLA Modules:
  0.0 390.3 jit_solution(9861140091519912179)
XLA Ops:
  2.1 6.9 %all-to-all-start = ((f32[16,16,128]{2,1,0:T(8,128)}), f32[16,16,128]{2,1,0:T(8,128)S(1)}, u32[]{:S(2)}, u32[]{:S(2)}) async-start(f32[16,16,128]{2,1,0:T(8,128)} %broadcast_in_dim.8), calls=%async_computation | async-start | bytes 262144 | tf_op jit(solution)/shard_map/all_to_all | solution.py:315
  11.0 2.5 collective-permute-start.4
  17.4 6.2 %all-to-all-start.1 = ((f32[8,48,128]{2,1,0:T(8,128)}), f32[8,48,128]{2,1,0:T(8,128)S(1)}, u32[]{:S(2)}, u32[]{:S(2)}) async-start(f32[8,48,128]{2,1,0:T(8,128)} %shard_map.78), calls=%async_computation.1 | async-start | bytes 393216 | tf_op jit(solution)/shard_map/all_to_all | solution.py:322
  23.6 5.1 %collective-permute-start.5 = (f32[104,512]{1,0:T(8,128)S(1)}, f32[104,512]{1,0:T(8,128)}, u32[]{:S(2)}, u32[]{:S(2)}) collective-permute-start(f32[104,512]{1,0:T(8,128)S(1)} %get-tuple-element.249.o2), channel_id=1, source_target_pairs={{0,7},{1,0},{2,1},{3,2},{4,3},{5,4},{6,5},{7,6},{8,15},{9,8},{10,9... | collective-permute-start | bytes 638984 | tf_op jit(solution)/shard_map/ppermute | solution.py:293
  28.7 2.7 collective-permute-start.2
  31.5 2.7 collective-permute-start.1
  36.6 4.1 %collective-permute-done.3.n1 = f32[104,512]{1,0:T(8,128)} collective-permute-done((f32[104,512]{1,0:T(8,128)S(1)}, f32[104,512]{1,0:T(8,128)}, u32[]{:S(2)}, u32[]{:S(2)}) %collective-permute-start.3) | collective-permute-done | bytes 213024 | tf_op jit(solution)/shard_map/ppermute | solution.py:293
  42.1 6.3 %shard_map.81 = (f32[4,32,512]{2,1,0:T(8,128)S(1)}, f32[32,512]{1,0:T(8,128)S(1)}, f32[32,512]{1,0:T(8,128)S(1)}, f32[32,512]{1,0:T(8,128)S(1)}, f32[32,512]{1,0:T(8,128)S(1)}) custom-call(f32[32,128]{1,0:T(8,128)S(1)} %get-tuple-element.127.own_ref, f32[32,128]{1,0:T(8,128)S(1)} %get-tuple-element.128.pair_ref, f32[32,128]{1,0:T(8,128)S(1)} %collective-permute-done.up_ref, ...), custom_call_target="tpu_custom_call" | custom-call | tf_op jit(solution)/shard_map/pallas_call | solution.py:336
  50.2 2.9 collective-permute-start.9
  54.9 5.0 %collective-permute-done.8.n2 = f32[32,512]{1,0:T(8,128)S(1)} collective-permute-done((f32[32,512]{1,0:T(8,128)S(1)}, f32[32,512]{1,0:T(8,128)S(1)}, u32[]{:S(2)}, u32[]{:S(2)}) %collective-permute-start.8) | collective-permute-done | bytes 65568 | tf_op jit(solution)/shard_map/ppermute | solution.py:293
  60.7 11.2 %all_to_all.100.x_ref = f32[16,16,128]{2,1,0:T(8,128)S(1)} all-to-all(f32[16,16,128]{2,1,0:T(8,128)S(1)} %get-tuple-element.143), channel_id=1, replica_groups=mesh['row'=16,'col'=8] {'row'}, dimensions={0} | all-to-all | bytes 262144 | tf_op jit(solution)/shard_map/all_to_all | solution.py:315
  72.6 9.7 %all_to_all.101.parts_ref = f32[8,48,128]{2,1,0:T(8,128)S(1)} all-to-all(f32[8,48,128]{2,1,0:T(8,128)S(1)} %shard_map.83), channel_id=1, replica_groups=mesh['row'=16,'col'=8] {'col'}, dimensions={0} | all-to-all | bytes 393216 | tf_op jit(solution)/shard_map/all_to_all | solution.py:322
  86.6 2.6 shard_map.86
  89.2 15.9 %all_to_all.102.sums_ref = f32[128,1,128]{2,1,0:T(1,128)S(1)} all-to-all(f32[128,1,128]{2,1,0:T(1,128)S(1)} %get-tuple-element.149), channel_id=1, replica_groups=mesh['row'=16,'col'=8] {'row','col'}, dimensions={0} | all-to-all | bytes 131072 | tf_op jit(solution)/shard_map/all_to_all | solution.py:383
  109.7 2.0 collective-permute-start.14
  114.1 2.3 collective-permute-done.14.n2
  117.3 11.2 %all_to_all.103.x_ref = f32[16,16,128]{2,1,0:T(8,128)S(1)} all-to-all(f32[16,16,128]{2,1,0:T(8,128)S(1)} %get-tuple-element.163), channel_id=1, replica_groups=mesh['row'=16,'col'=8] {'row'}, dimensions={0} | all-to-all | bytes 262144 | tf_op jit(solution)/shard_map/all_to_all | solution.py:315
  129.1 10.1 %all_to_all.104.parts_ref = f32[8,48,128]{2,1,0:T(8,128)S(1)} all-to-all(f32[8,48,128]{2,1,0:T(8,128)S(1)} %shard_map.90), channel_id=1, replica_groups=mesh['row'=16,'col'=8] {'col'}, dimensions={0} | all-to-all | bytes 393216 | tf_op jit(solution)/shard_map/all_to_all | solution.py:322
  143.3 2.6 shard_map.93
  145.9 15.9 %all_to_all.105.sums_ref = f32[128,1,128]{2,1,0:T(1,128)S(1)} all-to-all(f32[128,1,128]{2,1,0:T(1,128)S(1)} %get-tuple-element.169), channel_id=1, replica_groups=mesh['row'=16,'col'=8] {'row','col'}, dimensions={0} | all-to-all | bytes 131072 | tf_op jit(solution)/shard_map/all_to_all | solution.py:383
  166.4 2.0 collective-permute-start.20
  170.8 2.3 collective-permute-done.20.n2
  174.0 11.2 %all_to_all.106.x_ref = f32[16,16,128]{2,1,0:T(8,128)S(1)} all-to-all(f32[16,16,128]{2,1,0:T(8,128)S(1)} %get-tuple-element.182), channel_id=1, replica_groups=mesh['row'=16,'col'=8] {'row'}, dimensions={0} | all-to-all | bytes 262144 | tf_op jit(solution)/shard_map/all_to_all | solution.py:315
  185.8 9.7 %all_to_all.107.parts_ref = f32[8,48,128]{2,1,0:T(8,128)S(1)} all-to-all(f32[8,48,128]{2,1,0:T(8,128)S(1)} %shard_map.97), channel_id=1, replica_groups=mesh['row'=16,'col'=8] {'col'}, dimensions={0} | all-to-all | bytes 393216 | tf_op jit(solution)/shard_map/all_to_all | solution.py:322
  195.6 1.9 collective-permute-start.23
  199.7 2.6 shard_map.100
  202.2 16.0 %all_to_all.108.sums_ref = f32[128,1,128]{2,1,0:T(1,128)S(1)} all-to-all(f32[128,1,128]{2,1,0:T(1,128)S(1)} %get-tuple-element.188), channel_id=1, replica_groups=mesh['row'=16,'col'=8] {'row','col'}, dimensions={0} | all-to-all | bytes 131072 | tf_op jit(solution)/shard_map/all_to_all | solution.py:383
  222.8 2.0 collective-permute-start.26
  227.2 2.3 collective-permute-done.26.n2
  230.4 11.2 %all_to_all.109.x_ref = f32[16,16,128]{2,1,0:T(8,128)S(1)} all-to-all(f32[16,16,128]{2,1,0:T(8,128)S(1)} %get-tuple-element.201), channel_id=1, replica_groups=mesh['row'=16,'col'=8] {'row'}, dimensions={0} | all-to-all | bytes 262144 | tf_op jit(solution)/shard_map/all_to_all | solution.py:315
  242.2 9.7 %all_to_all.110.parts_ref = f32[8,48,128]{2,1,0:T(8,128)S(1)} all-to-all(f32[8,48,128]{2,1,0:T(8,128)S(1)} %shard_map.104), channel_id=1, replica_groups=mesh['row'=16,'col'=8] {'col'}, dimensions={0} | all-to-all | bytes 393216 | tf_op jit(solution)/shard_map/all_to_all | solution.py:322
  252.0 2.0 collective-permute-start.29
  256.1 2.6 shard_map.107
  258.6 16.0 %all_to_all.111.sums_ref = f32[128,1,128]{2,1,0:T(1,128)S(1)} all-to-all(f32[128,1,128]{2,1,0:T(1,128)S(1)} %get-tuple-element.207), channel_id=1, replica_groups=mesh['row'=16,'col'=8] {'row','col'}, dimensions={0} | all-to-all | bytes 131072 | tf_op jit(solution)/shard_map/all_to_all | solution.py:383
  279.3 2.0 collective-permute-start.32
  283.7 2.3 collective-permute-done.32.n2
  286.9 11.2 %all_to_all.112.x_ref = f32[16,16,128]{2,1,0:T(8,128)S(1)} all-to-all(f32[16,16,128]{2,1,0:T(8,128)S(1)} %get-tuple-element.220), channel_id=1, replica_groups=mesh['row'=16,'col'=8] {'row'}, dimensions={0} | all-to-all | bytes 262144 | tf_op jit(solution)/shard_map/all_to_all | solution.py:315
  298.7 9.7 %all_to_all.113.parts_ref = f32[8,48,128]{2,1,0:T(8,128)S(1)} all-to-all(f32[8,48,128]{2,1,0:T(8,128)S(1)} %shard_map.111), channel_id=1, replica_groups=mesh['row'=16,'col'=8] {'col'}, dimensions={0} | all-to-all | bytes 393216 | tf_op jit(solution)/shard_map/all_to_all | solution.py:322
  308.5 1.9 collective-permute-start.35
  312.5 2.6 shard_map.114
  315.1 16.0 %all_to_all.114.sums_ref = f32[128,1,128]{2,1,0:T(1,128)S(1)} all-to-all(f32[128,1,128]{2,1,0:T(1,128)S(1)} %get-tuple-element.226), channel_id=1, replica_groups=mesh['row'=16,'col'=8] {'row','col'}, dimensions={0} | all-to-all | bytes 131072 | tf_op jit(solution)/shard_map/all_to_all | solution.py:383
  335.7 2.0 collective-permute-start.38
  340.1 2.3 collective-permute-done.38.n2
  343.3 11.2 %all_to_all.115.x_ref = f32[16,16,128]{2,1,0:T(8,128)S(1)} all-to-all(f32[16,16,128]{2,1,0:T(8,128)S(1)} %get-tuple-element.239), channel_id=1, replica_groups=mesh['row'=16,'col'=8] {'row'}, dimensions={0} | all-to-all | bytes 262144 | tf_op jit(solution)/shard_map/all_to_all | solution.py:315
  355.1 9.7 %all_to_all.116.parts_ref = f32[8,48,128]{2,1,0:T(8,128)S(1)} all-to-all(f32[8,48,128]{2,1,0:T(8,128)S(1)} %shard_map.118), channel_id=1, replica_groups=mesh['row'=16,'col'=8] {'col'}, dimensions={0} | all-to-all | bytes 393216 | tf_op jit(solution)/shard_map/all_to_all | solution.py:322
  364.9 1.9 collective-permute-start.41
  368.9 3.2 shard_map.121
  372.1 16.0 %all_to_all.117.sums_ref = f32[128,1,128]{2,1,0:T(1,128)S(1)} all-to-all(f32[128,1,128]{2,1,0:T(1,128)S(1)} %get-tuple-element.245), channel_id=1, replica_groups=mesh['row'=16,'col'=8] {'row','col'}, dimensions={0} | all-to-all | bytes 131072 | tf_op jit(solution)/shard_map/all_to_all | solution.py:383
  (118 shorter events, 77.5 us)
Async XLA Ops:
  2.1 14.1 %all-to-all-start = ((f32[16,16,128]{2,1,0:T(8,128)}), f32[16,16,128]{2,1,0:T(8,128)S(1)}, u32[]{:S(2)}, u32[]{:S(2)}) async-start(f32[16,16,128]{2,1,0:T(8,128)} %broadcast_in_dim.8), calls=%async_computation | async-start | bytes 262144 | tf_op jit(solution)/shard_map/all_to_all | solution.py:315
  11.0 23.2 %collective-permute-start.4 = (f32[104,512]{1,0:T(8,128)S(1)}, f32[104,512]{1,0:T(8,128)S(1)}, u32[]{:S(2)}, u32[]{:S(2)}) collective-permute-start(f32[104,512]{1,0:T(8,128)S(1)} %get-tuple-element.248.o3), channel_id=1, source_target_pairs={{0,1},{1,2},{2,3},{3,4},{4,5},{5,6},{6,7},{7,0},{8,9},{9,10},{10,1... | collective-permute-start | bytes 638984 | tf_op jit(solution)/shard_map/ppermute | solution.py:293
  13.5 1.6 copy-start.1
  17.4 14.0 %all-to-all-start.1 = ((f32[8,48,128]{2,1,0:T(8,128)}), f32[8,48,128]{2,1,0:T(8,128)S(1)}, u32[]{:S(2)}, u32[]{:S(2)}) async-start(f32[8,48,128]{2,1,0:T(8,128)} %shard_map.78), calls=%async_computation.1 | async-start | bytes 393216 | tf_op jit(solution)/shard_map/all_to_all | solution.py:322
  23.6 11.9 %collective-permute-start.5 = (f32[104,512]{1,0:T(8,128)S(1)}, f32[104,512]{1,0:T(8,128)}, u32[]{:S(2)}, u32[]{:S(2)}) collective-permute-start(f32[104,512]{1,0:T(8,128)S(1)} %get-tuple-element.249.o2), channel_id=1, source_target_pairs={{0,7},{1,0},{2,1},{3,2},{4,3},{5,4},{6,5},{7,6},{8,15},{9,8},{10,9... | collective-permute-start | bytes 638984 | tf_op jit(solution)/shard_map/ppermute | solution.py:293
  28.7 7.9 %collective-permute-start.2 = (f32[104,512]{1,0:T(8,128)S(1)}, f32[104,512]{1,0:T(8,128)}, u32[]{:S(2)}, u32[]{:S(2)}) collective-permute-start(f32[104,512]{1,0:T(8,128)S(1)} %get-tuple-element.250.o1), channel_id=1, source_target_pairs={{0,8},{8,16},{16,24},{24,32},{32,40},{40,48},{48,56},{56,64},{64,7... | collective-permute-start | bytes 638984 | tf_op jit(solution)/shard_map/ppermute | solution.py:293
  31.4 9.3 %collective-permute-start.3 = (f32[104,512]{1,0:T(8,128)S(1)}, f32[104,512]{1,0:T(8,128)}, u32[]{:S(2)}, u32[]{:S(2)}) collective-permute-start(f32[104,512]{1,0:T(8,128)S(1)} %get-tuple-element.251.o0), channel_id=1, source_target_pairs={{0,120},{8,0},{16,8},{24,16},{32,24},{40,32},{48,40},{56,48},{64,5... | collective-permute-start | bytes 638984 | tf_op jit(solution)/shard_map/ppermute | solution.py:293
  31.4 53.3 %copy-start = (f32[1,1,2048,2048]{3,2,1,0:T(8,128)S(1)}, f32[1,1,2048,2048]{3,2,1,0:T(8,128)}, u32[]{:S(2)}) copy-start(f32[1,1,2048,2048]{3,2,1,0:T(8,128)} %param.6) | copy-start | bytes 50331652
  31.5 10.6 %collective-permute-start.1 = (f32[32,128]{1,0:T(8,128)S(1)}, f32[32,128]{1,0:T(8,128)S(1)}, u32[]{:S(2)}, u32[]{:S(2)}) collective-permute-start(f32[32,128]{1,0:T(8,128)S(1)} %get-tuple-element.127.own_ref), channel_id=1, source_target_pairs={{0,120},{8,0},{16,8},{24,16},{32,24},{40,32},{48,40},{56,48},{64,5... | collective-permute-start | bytes 49160 | tf_op jit(solution)/shard_map/ppermute | solution.py:293
  34.2 7.9 %collective-permute-start = (f32[32,128]{1,0:T(8,128)S(1)}, f32[32,128]{1,0:T(8,128)S(1)}, u32[]{:S(2)}, u32[]{:S(2)}) collective-permute-start(f32[32,128]{1,0:T(8,128)S(1)} %get-tuple-element.127.own_ref), channel_id=1, source_target_pairs={{0,8},{8,16},{16,24},{24,32},{32,40},{40,48},{48,56},{56,64},{64,7... | collective-permute-start | bytes 49160 | tf_op jit(solution)/shard_map/ppermute | solution.py:293
  48.4 4.8 %collective-permute-start.7 = (f32[32,512]{1,0:T(8,128)S(1)}, f32[32,512]{1,0:T(8,128)S(1)}, u32[]{:S(2)}, u32[]{:S(2)}) collective-permute-start(f32[32,512]{1,0:T(8,128)S(1)} %get-tuple-element.137.a0.o0), channel_id=1, source_target_pairs={{0,120},{8,0},{16,8},{24,16},{32,24},{40,32},{48,40},{56,48},{64,5... | collective-permute-start | bytes 196616 | tf_op jit(solution)/shard_map/ppermute | solution.py:293
  49.1 4.1 %collective-permute-start.6 = (f32[32,512]{1,0:T(8,128)S(1)}, f32[32,512]{1,0:T(8,128)S(1)}, u32[]{:S(2)}, u32[]{:S(2)}) collective-permute-start(f32[32,512]{1,0:T(8,128)S(1)} %get-tuple-element.138.a1.o1), channel_id=1, source_target_pairs={{0,8},{8,16},{16,24},{24,32},{32,40},{40,48},{48,56},{56,64},{64,7... | collective-permute-start | bytes 196616 | tf_op jit(solution)/shard_map/ppermute | solution.py:293
  50.2 4.6 %collective-permute-start.9 = (f32[32,512]{1,0:T(8,128)S(1)}, f32[32,512]{1,0:T(8,128)S(1)}, u32[]{:S(2)}, u32[]{:S(2)}) collective-permute-start(f32[32,512]{1,0:T(8,128)S(1)} %get-tuple-element.139.a2.o2), channel_id=1, source_target_pairs={{0,7},{1,0},{2,1},{3,2},{4,3},{5,4},{6,5},{7,6},{8,15},{9,8},{10,9... | collective-permute-start | bytes 196616 | tf_op jit(solution)/shard_map/ppermute | solution.py:293
  53.2 6.7 %collective-permute-start.8 = (f32[32,512]{1,0:T(8,128)S(1)}, f32[32,512]{1,0:T(8,128)S(1)}, u32[]{:S(2)}, u32[]{:S(2)}) collective-permute-start(f32[32,512]{1,0:T(8,128)S(1)} %get-tuple-element.140.a3.o3), channel_id=1, source_target_pairs={{0,1},{1,2},{2,3},{3,4},{4,5},{5,6},{6,7},{7,0},{8,9},{9,10},{10,1... | collective-permute-start | bytes 196616 | tf_op jit(solution)/shard_map/ppermute | solution.py:293
  82.4 4.2 %collective-permute-start.11 = (f32[32,128]{1,0:T(8,128)S(1)}, f32[32,128]{1,0:T(8,128)S(1)}, u32[]{:S(2)}, u32[]{:S(2)}) collective-permute-start(f32[32,128]{1,0:T(8,128)S(1)} %get-tuple-element.144.own_ref), channel_id=1, source_target_pairs={{0,120},{8,0},{16,8},{24,16},{32,24},{40,32},{48,40},{56,48},{64,5... | collective-permute-start | bytes 49160 | tf_op jit(solution)/shard_map/ppermute | solution.py:293
  84.2 2.4 collective-permute-start.10
  106.9 5.7 %collective-permute-start.13 = (f32[32,512]{1,0:T(8,128)S(1)}, f32[32,512]{1,0:T(8,128)S(1)}, u32[]{:S(2)}, u32[]{:S(2)}) collective-permute-start(f32[32,512]{1,0:T(8,128)S(1)} %get-tuple-element.155.o0), channel_id=1, source_target_pairs={{0,120},{8,0},{16,8},{24,16},{32,24},{40,32},{48,40},{56,48},{64,5... | collective-permute-start | bytes 196616 | tf_op jit(solution)/shard_map/ppermute | solution.py:293
  107.6 5.0 %collective-permute-start.12 = (f32[32,512]{1,0:T(8,128)S(1)}, f32[32,512]{1,0:T(8,128)S(1)}, u32[]{:S(2)}, u32[]{:S(2)}) collective-permute-start(f32[32,512]{1,0:T(8,128)S(1)} %get-tuple-element.156.o1), channel_id=1, source_target_pairs={{0,8},{8,16},{16,24},{24,32},{32,40},{40,48},{48,56},{56,64},{64,7... | collective-permute-start | bytes 196616 | tf_op jit(solution)/shard_map/ppermute | solution.py:293
  108.7 5.4 %collective-permute-start.15 = (f32[32,512]{1,0:T(8,128)S(1)}, f32[32,512]{1,0:T(8,128)S(1)}, u32[]{:S(2)}, u32[]{:S(2)}) collective-permute-start(f32[32,512]{1,0:T(8,128)S(1)} %get-tuple-element.157.o2), channel_id=1, source_target_pairs={{0,7},{1,0},{2,1},{3,2},{4,3},{5,4},{6,5},{7,6},{8,15},{9,8},{10,9... | collective-permute-start | bytes 196616 | tf_op jit(solution)/shard_map/ppermute | solution.py:293
  109.7 6.7 %collective-permute-start.14 = (f32[32,512]{1,0:T(8,128)S(1)}, f32[32,512]{1,0:T(8,128)S(1)}, u32[]{:S(2)}, u32[]{:S(2)}) collective-permute-start(f32[32,512]{1,0:T(8,128)S(1)} %get-tuple-element.158.o3), channel_id=1, source_target_pairs={{0,1},{1,2},{2,3},{3,4},{4,5},{5,6},{6,7},{7,0},{8,9},{9,10},{10,1... | collective-permute-start | bytes 196616 | tf_op jit(solution)/shard_map/ppermute | solution.py:293
  139.3 4.1 %collective-permute-start.17 = (f32[32,128]{1,0:T(8,128)S(1)}, f32[32,128]{1,0:T(8,128)S(1)}, u32[]{:S(2)}, u32[]{:S(2)}) collective-permute-start(f32[32,128]{1,0:T(8,128)S(1)} %get-tuple-element.164.own_ref), channel_id=1, source_target_pairs={{0,120},{8,0},{16,8},{24,16},{32,24},{40,32},{48,40},{56,48},{64,5... | collective-permute-start | bytes 49160 | tf_op jit(solution)/shard_map/ppermute | solution.py:293
  141.1 2.3 collective-permute-start.16
  163.6 5.8 %collective-permute-start.19 = (f32[32,512]{1,0:T(8,128)S(1)}, f32[32,512]{1,0:T(8,128)S(1)}, u32[]{:S(2)}, u32[]{:S(2)}) collective-permute-start(f32[32,512]{1,0:T(8,128)S(1)} %get-tuple-element.174.o0), channel_id=1, source_target_pairs={{0,120},{8,0},{16,8},{24,16},{32,24},{40,32},{48,40},{56,48},{64,5... | collective-permute-start | bytes 196616 | tf_op jit(solution)/shard_map/ppermute | solution.py:293
  164.3 5.2 %collective-permute-start.18 = (f32[32,512]{1,0:T(8,128)S(1)}, f32[32,512]{1,0:T(8,128)S(1)}, u32[]{:S(2)}, u32[]{:S(2)}) collective-permute-start(f32[32,512]{1,0:T(8,128)S(1)} %get-tuple-element.175.o1), channel_id=1, source_target_pairs={{0,8},{8,16},{16,24},{24,32},{32,40},{40,48},{48,56},{56,64},{64,7... | collective-permute-start | bytes 196616 | tf_op jit(solution)/shard_map/ppermute | solution.py:293
  165.4 5.4 %collective-permute-start.21 = (f32[32,512]{1,0:T(8,128)S(1)}, f32[32,512]{1,0:T(8,128)S(1)}, u32[]{:S(2)}, u32[]{:S(2)}) collective-permute-start(f32[32,512]{1,0:T(8,128)S(1)} %get-tuple-element.176.o2), channel_id=1, source_target_pairs={{0,7},{1,0},{2,1},{3,2},{4,3},{5,4},{6,5},{7,6},{8,15},{9,8},{10,9... | collective-permute-start | bytes 196616 | tf_op jit(solution)/shard_map/ppermute | solution.py:293
  166.4 6.7 %collective-permute-start.20 = (f32[32,512]{1,0:T(8,128)S(1)}, f32[32,512]{1,0:T(8,128)S(1)}, u32[]{:S(2)}, u32[]{:S(2)}) collective-permute-start(f32[32,512]{1,0:T(8,128)S(1)} %get-tuple-element.177.o3), channel_id=1, source_target_pairs={{0,1},{1,2},{2,3},{3,4},{4,5},{5,6},{6,7},{7,0},{8,9},{9,10},{10,1... | collective-permute-start | bytes 196616 | tf_op jit(solution)/shard_map/ppermute | solution.py:293
  195.6 4.1 %collective-permute-start.23 = (f32[32,128]{1,0:T(8,128)S(1)}, f32[32,128]{1,0:T(8,128)S(1)}, u32[]{:S(2)}, u32[]{:S(2)}) collective-permute-start(f32[32,128]{1,0:T(8,128)S(1)} %get-tuple-element.183.own_ref), channel_id=1, source_target_pairs={{0,120},{8,0},{16,8},{24,16},{32,24},{40,32},{48,40},{56,48},{64,5... | collective-permute-start | bytes 49160 | tf_op jit(solution)/shard_map/ppermute | solution.py:293
  197.5 2.2 collective-permute-start.22
  220.1 6.1 %collective-permute-start.25 = (f32[32,512]{1,0:T(8,128)S(1)}, f32[32,512]{1,0:T(8,128)S(1)}, u32[]{:S(2)}, u32[]{:S(2)}) collective-permute-start(f32[32,512]{1,0:T(8,128)S(1)} %get-tuple-element.193.o0), channel_id=1, source_target_pairs={{0,120},{8,0},{16,8},{24,16},{32,24},{40,32},{48,40},{56,48},{64,5... | collective-permute-start | bytes 196616 | tf_op jit(solution)/shard_map/ppermute | solution.py:293
  220.8 5.4 %collective-permute-start.24 = (f32[32,512]{1,0:T(8,128)S(1)}, f32[32,512]{1,0:T(8,128)S(1)}, u32[]{:S(2)}, u32[]{:S(2)}) collective-permute-start(f32[32,512]{1,0:T(8,128)S(1)} %get-tuple-element.194.o1), channel_id=1, source_target_pairs={{0,8},{8,16},{16,24},{24,32},{32,40},{40,48},{48,56},{56,64},{64,7... | collective-permute-start | bytes 196616 | tf_op jit(solution)/shard_map/ppermute | solution.py:293
  221.8 5.4 %collective-permute-start.27 = (f32[32,512]{1,0:T(8,128)S(1)}, f32[32,512]{1,0:T(8,128)S(1)}, u32[]{:S(2)}, u32[]{:S(2)}) collective-permute-start(f32[32,512]{1,0:T(8,128)S(1)} %get-tuple-element.195.o2), channel_id=1, source_target_pairs={{0,7},{1,0},{2,1},{3,2},{4,3},{5,4},{6,5},{7,6},{8,15},{9,8},{10,9... | collective-permute-start | bytes 196616 | tf_op jit(solution)/shard_map/ppermute | solution.py:293
  222.8 6.7 %collective-permute-start.26 = (f32[32,512]{1,0:T(8,128)S(1)}, f32[32,512]{1,0:T(8,128)S(1)}, u32[]{:S(2)}, u32[]{:S(2)}) collective-permute-start(f32[32,512]{1,0:T(8,128)S(1)} %get-tuple-element.196.o3), channel_id=1, source_target_pairs={{0,1},{1,2},{2,3},{3,4},{4,5},{5,6},{6,7},{7,0},{8,9},{9,10},{10,1... | collective-permute-start | bytes 196616 | tf_op jit(solution)/shard_map/ppermute | solution.py:293
  252.0 4.1 %collective-permute-start.29 = (f32[32,128]{1,0:T(8,128)S(1)}, f32[32,128]{1,0:T(8,128)S(1)}, u32[]{:S(2)}, u32[]{:S(2)}) collective-permute-start(f32[32,128]{1,0:T(8,128)S(1)} %get-tuple-element.202.own_ref), channel_id=1, source_target_pairs={{0,120},{8,0},{16,8},{24,16},{32,24},{40,32},{48,40},{56,48},{64,5... | collective-permute-start | bytes 49160 | tf_op jit(solution)/shard_map/ppermute | solution.py:293
  254.0 2.1 collective-permute-start.28
  276.5 5.9 %collective-permute-start.31 = (f32[32,512]{1,0:T(8,128)S(1)}, f32[32,512]{1,0:T(8,128)S(1)}, u32[]{:S(2)}, u32[]{:S(2)}) collective-permute-start(f32[32,512]{1,0:T(8,128)S(1)} %get-tuple-element.212.o0), channel_id=1, source_target_pairs={{0,120},{8,0},{16,8},{24,16},{32,24},{40,32},{48,40},{56,48},{64,5... | collective-permute-start | bytes 196616 | tf_op jit(solution)/shard_map/ppermute | solution.py:293
  277.2 5.2 %collective-permute-start.30 = (f32[32,512]{1,0:T(8,128)S(1)}, f32[32,512]{1,0:T(8,128)S(1)}, u32[]{:S(2)}, u32[]{:S(2)}) collective-permute-start(f32[32,512]{1,0:T(8,128)S(1)} %get-tuple-element.213.o1), channel_id=1, source_target_pairs={{0,8},{8,16},{16,24},{24,32},{32,40},{40,48},{48,56},{56,64},{64,7... | collective-permute-start | bytes 196616 | tf_op jit(solution)/shard_map/ppermute | solution.py:293
  278.3 5.4 %collective-permute-start.33 = (f32[32,512]{1,0:T(8,128)S(1)}, f32[32,512]{1,0:T(8,128)S(1)}, u32[]{:S(2)}, u32[]{:S(2)}) collective-permute-start(f32[32,512]{1,0:T(8,128)S(1)} %get-tuple-element.214.o2), channel_id=1, source_target_pairs={{0,7},{1,0},{2,1},{3,2},{4,3},{5,4},{6,5},{7,6},{8,15},{9,8},{10,9... | collective-permute-start | bytes 196616 | tf_op jit(solution)/shard_map/ppermute | solution.py:293
  279.3 6.7 %collective-permute-start.32 = (f32[32,512]{1,0:T(8,128)S(1)}, f32[32,512]{1,0:T(8,128)S(1)}, u32[]{:S(2)}, u32[]{:S(2)}) collective-permute-start(f32[32,512]{1,0:T(8,128)S(1)} %get-tuple-element.215.o3), channel_id=1, source_target_pairs={{0,1},{1,2},{2,3},{3,4},{4,5},{5,6},{6,7},{7,0},{8,9},{9,10},{10,1... | collective-permute-start | bytes 196616 | tf_op jit(solution)/shard_map/ppermute | solution.py:293
  308.5 4.1 %collective-permute-start.35 = (f32[32,128]{1,0:T(8,128)S(1)}, f32[32,128]{1,0:T(8,128)S(1)}, u32[]{:S(2)}, u32[]{:S(2)}) collective-permute-start(f32[32,128]{1,0:T(8,128)S(1)} %get-tuple-element.221.own_ref), channel_id=1, source_target_pairs={{0,120},{8,0},{16,8},{24,16},{32,24},{40,32},{48,40},{56,48},{64,5... | collective-permute-start | bytes 49160 | tf_op jit(solution)/shard_map/ppermute | solution.py:293
  310.4 2.1 collective-permute-start.34
  332.9 5.9 %collective-permute-start.37 = (f32[32,512]{1,0:T(8,128)S(1)}, f32[32,512]{1,0:T(8,128)S(1)}, u32[]{:S(2)}, u32[]{:S(2)}) collective-permute-start(f32[32,512]{1,0:T(8,128)S(1)} %get-tuple-element.231.o0), channel_id=1, source_target_pairs={{0,120},{8,0},{16,8},{24,16},{32,24},{40,32},{48,40},{56,48},{64,5... | collective-permute-start | bytes 196616 | tf_op jit(solution)/shard_map/ppermute | solution.py:293
  333.6 5.2 %collective-permute-start.36 = (f32[32,512]{1,0:T(8,128)S(1)}, f32[32,512]{1,0:T(8,128)S(1)}, u32[]{:S(2)}, u32[]{:S(2)}) collective-permute-start(f32[32,512]{1,0:T(8,128)S(1)} %get-tuple-element.232.o1), channel_id=1, source_target_pairs={{0,8},{8,16},{16,24},{24,32},{32,40},{40,48},{48,56},{56,64},{64,7... | collective-permute-start | bytes 196616 | tf_op jit(solution)/shard_map/ppermute | solution.py:293
  334.7 5.4 %collective-permute-start.39 = (f32[32,512]{1,0:T(8,128)S(1)}, f32[32,512]{1,0:T(8,128)S(1)}, u32[]{:S(2)}, u32[]{:S(2)}) collective-permute-start(f32[32,512]{1,0:T(8,128)S(1)} %get-tuple-element.233.o2), channel_id=1, source_target_pairs={{0,7},{1,0},{2,1},{3,2},{4,3},{5,4},{6,5},{7,6},{8,15},{9,8},{10,9... | collective-permute-start | bytes 196616 | tf_op jit(solution)/shard_map/ppermute | solution.py:293
  335.7 6.7 %collective-permute-start.38 = (f32[32,512]{1,0:T(8,128)S(1)}, f32[32,512]{1,0:T(8,128)S(1)}, u32[]{:S(2)}, u32[]{:S(2)}) collective-permute-start(f32[32,512]{1,0:T(8,128)S(1)} %get-tuple-element.234.o3), channel_id=1, source_target_pairs={{0,1},{1,2},{2,3},{3,4},{4,5},{5,6},{6,7},{7,0},{8,9},{9,10},{10,1... | collective-permute-start | bytes 196616 | tf_op jit(solution)/shard_map/ppermute | solution.py:293
  364.9 4.1 %collective-permute-start.41 = (f32[32,128]{1,0:T(8,128)S(1)}, f32[32,128]{1,0:T(8,128)S(1)}, u32[]{:S(2)}, u32[]{:S(2)}) collective-permute-start(f32[32,128]{1,0:T(8,128)S(1)} %get-tuple-element.240.own_ref), channel_id=1, source_target_pairs={{0,120},{8,0},{16,8},{24,16},{32,24},{40,32},{48,40},{56,48},{64,5... | collective-permute-start | bytes 49160 | tf_op jit(solution)/shard_map/ppermute | solution.py:293
  366.8 2.2 collective-permute-start.40
  388.1 1.0 copy-start.2

commit v5 on v4

--- a/solution.py
+++ b/solution.py
@@ -123,13 +123,21 @@
     own_ref[half:K, :] = jnp.where(low, turned, packed)
 
 
-def col_half_kernel(own_ref, pair_ref, grad_ref, exp_ref, dual, p_ref, part_ref, lhs):
+def numer_terms(has_ref, f, grad, p):
+    return jnp.where(has_ref[f] != 0, 0.5, 1.0) * grad * p
+
+
+def col_half_kernel(
+    has_ref, own_ref, pair_ref, grad_ref, exp_ref, dual, p_ref, part_ref, numer_ref, lhs
+):
     low = low_lanes((K, 128))
     own, pair = own_ref[...], pair_ref[...]
     for f, side in ((2, jnp.where(low, pair, own)), (3, jnp.where(low, own, pair))):
         p = grad_ref[f] - expand_face(side, exp_ref[f])
         p_ref[f - 2] = p
         put(lhs, f - 2, p)
+        terms = numer_terms(has_ref, f, grad_ref[f], p)
+        numer_ref[...] = terms if f == 2 else numer_ref[...] + terms
     for f in range(4):
         part_ref[f] = apply_rows(lhs, dual, f, jnp.zeros((K, FACE), F32), M // 2)
 
@@ -189,24 +197,35 @@
                     a_ref[...] = apply_rows(lhs, dual, f, a_ref[...], face * FACE)
 
 
+def clamped(contact_ref, f, plain):
+    return jnp.where(contact_ref[f : f + 1, :] != 0, jnp.maximum(plain, 0.0), plain)
+
+
 def step_kernel(
     has_ref, sums_ref, contact_ref, m_ref, p_ref, image_ref, o0, o1, o2, o3, dual,
-    new_ref, corr, a0, a1, a2, a3, lhs,
+    ratio_ref, corr, a0, a1, a2, a3, lhs,
 ):
     ratio = ratio_of(sums_ref)
-    faces = ((o0, a0), (o1, a1), (o2, a2), (o3, a3))
-    for f, (o_ref, a_ref) in enumerate(faces):
-        plain = m_ref[f] - ratio * p_ref[f]
-        new = jnp.where(contact_ref[f : f + 1, :] != 0, jnp.maximum(plain, 0.0), plain)
-        new_ref[f] = new
-        corr[f] = new - plain
+    ratio_ref[...] = jnp.broadcast_to(ratio, ratio_ref.shape)
+    for f, (o_ref, a_ref) in enumerate(((o0, a0), (o1, a1), (o2, a2), (o3, a3))):
         a_ref[...] = o_ref[...] - ratio * image_ref[f]
+
+        @pl.when(has_ref[f] == 0)
+        def _():
+            plain = m_ref[f] - ratio * p_ref[f]
+            corr[f] = clamped(contact_ref, f, plain) - plain
+
     add_clamped(has_ref, corr, lhs, dual, (a0, a1, a2, a3), True)
 
 
-def outer_kernel(has_ref, corr, o0, o1, o2, o3, dual, a0, a1, a2, a3, lhs):
-    for o_ref, a_ref in ((o0, a0), (o1, a1), (o2, a2), (o3, a3)):
+def outer_kernel(
+    has_ref, ratio_ref, contact_ref, m_ref, p_ref, corr, o0, o1, o2, o3, dual,
+    new_ref, a0, a1, a2, a3, lhs,
+):
+    ratio = ratio_ref[:, 0:1]
+    for f, (o_ref, a_ref) in enumerate(((o0, a0), (o1, a1), (o2, a2), (o3, a3))):
         a_ref[...] = o_ref[...]
+        new_ref[f] = clamped(contact_ref, f, m_ref[f] - ratio * p_ref[f])
     add_clamped(has_ref, corr, lhs, dual, (a0, a1, a2, a3), False)
 
 
@@ -265,22 +284,24 @@
 
 
 def image_kernel(
-    has_ref, own_ref, up_ref, down_ref, grad_ref, half_ref, part_ref, exp_ref, dual,
-    p_ref, image_ref, s_ref, lhs,
+    has_ref, own_ref, up_ref, down_ref, grad_ref, half_ref, part_ref, numer_ref,
+    exp_ref, dual, p_ref, image_ref, s_ref, lhs,
 ):
     for f, face in row_half(own_ref, up_ref, down_ref, exp_ref):
         p = grad_ref[f] - face
         p_ref[f] = p
         p_ref[f + 2] = half_ref[f]
         put(lhs, f, p)
-    numer = jnp.zeros((K, 1), F32)
-    denom = jnp.zeros((K, 1), F32)
+    numer = numer_ref[...]
+    for f in range(2):
+        numer = numer + numer_terms(has_ref, f, grad_ref[f], p_ref[f])
+    numer = jnp.sum(numer, axis=1, keepdims=True)
+    denom = jnp.zeros((K, FACE), F32)
     for f in range(4):
-        weight = jnp.where(has_ref[f] != 0, 0.5, 1.0)
-        numer = numer + weight * jnp.sum(grad_ref[f] * p_ref[f], axis=1, keepdims=True)
         image = apply_rows(lhs, dual, f, part_ref[f], 0)
         image_ref[f] = image
-        denom = denom + jnp.sum(p_ref[f] * image, axis=1, keepdims=True)
+        denom = denom + p_ref[f] * image
+    denom = jnp.sum(denom, axis=1, keepdims=True)
     rows = lax.broadcasted_iota(jnp.int32, (K, 128), 0)
     lanes = lax.broadcasted_iota(jnp.int32, (K, 128), 1)
     placed = jnp.where(rows == lanes, numer, 0.0) + jnp.where(rows + K == lanes, denom, 0.0)
@@ -327,8 +348,8 @@
 
     def col_half(own, pair, grad):
         return call(
-            col_half_kernel, [half, vec], own, pair, grad, exp, dual,
-            scratch=[half_lhs], cost=8 << 20,
+            col_half_kernel, [half, vec, face], has_nb, own, pair, grad, exp, dual,
+            scratch=[half_lhs], smem=(0,), cost=8 << 20,
         )
 
     def first(*args):
@@ -382,14 +403,15 @@
         )
         sums = lax.all_to_all(sums, ("row", "col"), 0, 0, tiled=True)
         if step + 1 < ITERS:
-            multipliers, corr, *sent_faces = call(
-                step_kernel, [vec, vec] + [face] * 4,
+            ratio, corr, *sent_faces = call(
+                step_kernel, [amps, vec] + [face] * 4,
                 has_nb, sums, contact, multipliers, projected, image, *faces, dual,
                 scratch=[((2 * K, FACE), BF16)], smem=(0,),
             )
             nbs = exchange(sent_faces)
-            faces = call(
-                outer_kernel, [face] * 4, has_nb, corr, *sent_faces, dual,
+            multipliers, *faces = call(
+                outer_kernel, [vec] + [face] * 4,
+                has_nb, ratio, contact, multipliers, projected, corr, *sent_faces, dual,
                 scratch=[((2 * K, FACE), BF16)], smem=(0,), cost=4 << 20,
             )
         else:

time: 398 us -> 398 us (level)
  blocking collectives: 222 us -> 218 us
  transfers between devices with their start and end apart: 44 -> 44, of which waited for: 14 -> 14; matrix products, arithmetic and copies ran while one was open for 1% -> 1% of each run, Pallas kernels for 5% -> 6%
where the time goes in v5:
time: 398 us; the launch traced here: 391 us
  blocking collectives  218 us (55%)
  starting transfers between devices  69.5 us (17%)
  Pallas kernels  65.9 us (17%)
  waiting for transfers between devices  29.5 us (7%)
  local copies, waits for them, and re-layouts  4 us (1%)
    all_to_all x6, blocking collectives, shards(): sums = lax.all_to_all(sums, ('row', 'col'), 0, 0, tiled=True)  92.5 us
    all_to_all x6, blocking collectives, gather(): return lax.all_to_all(sent, 'row', 0, 0, tiled=True)  67.6 us
    pallas_call x44, Pallas kernels, call(): pl.pallas_call(kernel, out_shape=[jax.ShapeDtypeStruct(shape, dtype) for...  58.6 us
    all_to_all x6, blocking collectives, amplitudes(): parts = lax.all_to_all(parts, 'col', 0, 0, tiled=True)  58.3 us
    ppermute x42, starting transfers between devices, along(): return lax.ppermute(value, axis, [(i, (i + step) % n) for i in range(n)])  56.4 us
    ppermute x42, waiting for transfers between devices, along(): return lax.ppermute(value, axis, [(i, (i + step) % n) for i in range(n)])  29.5 us
  transfers between devices with their start and end apart: 44, of which 14 were waited for; matrix products, arithmetic and copies ran while one was open for 1% of the time, Pallas kernels for 6%

profile of v5, /device:TPU:1, one launch (start us, length us, event | category | flops | bytes accessed | tf_op | source)
XLA Modules:
  0.0 390.5 jit_solution(15407918945661008951)
XLA Ops:
  2.1 6.9 %all-to-all-start = ((f32[16,16,128]{2,1,0:T(8,128)}), f32[16,16,128]{2,1,0:T(8,128)S(1)}, u32[]{:S(2)}, u32[]{:S(2)}) async-start(f32[16,16,128]{2,1,0:T(8,128)} %broadcast_in_dim.8), calls=%async_computation | async-start | bytes 262144 | tf_op jit(solution)/shard_map/all_to_all | solution.py:336
  11.0 2.5 collective-permute-start.4
  17.4 6.2 %all-to-all-start.1 = ((f32[8,48,128]{2,1,0:T(8,128)}), f32[8,48,128]{2,1,0:T(8,128)S(1)}, u32[]{:S(2)}, u32[]{:S(2)}) async-start(f32[8,48,128]{2,1,0:T(8,128)} %shard_map.78), calls=%async_computation.1 | async-start | bytes 393216 | tf_op jit(solution)/shard_map/all_to_all | solution.py:343
  23.6 5.1 %collective-permute-start.5 = (f32[104,512]{1,0:T(8,128)S(1)}, f32[104,512]{1,0:T(8,128)}, u32[]{:S(2)}, u32[]{:S(2)}) collective-permute-start(f32[104,512]{1,0:T(8,128)S(1)} %get-tuple-element.271.o2), channel_id=1, source_target_pairs={{0,7},{1,0},{2,1},{3,2},{4,3},{5,4},{6,5},{7,6},{8,15},{9,8},{10,9... | collective-permute-start | bytes 638984 | tf_op jit(solution)/shard_map/ppermute | solution.py:314
  28.7 2.7 collective-permute-start.2
  31.5 2.7 collective-permute-start.1
  36.6 4.1 %collective-permute-done.3.n1 = f32[104,512]{1,0:T(8,128)} collective-permute-done((f32[104,512]{1,0:T(8,128)S(1)}, f32[104,512]{1,0:T(8,128)}, u32[]{:S(2)}, u32[]{:S(2)}) %collective-permute-start.3) | collective-permute-done | bytes 213024 | tf_op jit(solution)/shard_map/ppermute | solution.py:314
  42.1 6.3 %shard_map.81 = (f32[4,32,512]{2,1,0:T(8,128)S(1)}, f32[32,512]{1,0:T(8,128)S(1)}, f32[32,512]{1,0:T(8,128)S(1)}, f32[32,512]{1,0:T(8,128)S(1)}, f32[32,512]{1,0:T(8,128)S(1)}) custom-call(f32[32,128]{1,0:T(8,128)S(1)} %get-tuple-element.138.own_ref, f32[32,128]{1,0:T(8,128)S(1)} %get-tuple-element.139.pair_ref, f32[32,128]{1,0:T(8,128)S(1)} %collective-permute-done.up_ref, ...), custom_call_target="tpu_custom_call" | custom-call | tf_op jit(solution)/shard_map/pallas_call | solution.py:357
  50.2 2.9 collective-permute-start.9
  54.9 5.0 %collective-permute-done.8.n2 = f32[32,512]{1,0:T(8,128)S(1)} collective-permute-done((f32[32,512]{1,0:T(8,128)S(1)}, f32[32,512]{1,0:T(8,128)S(1)}, u32[]{:S(2)}, u32[]{:S(2)}) %collective-permute-start.8) | collective-permute-done | bytes 65568 | tf_op jit(solution)/shard_map/ppermute | solution.py:314
  60.7 11.2 %all_to_all.100.x_ref = f32[16,16,128]{2,1,0:T(8,128)S(1)} all-to-all(f32[16,16,128]{2,1,0:T(8,128)S(1)} %get-tuple-element.154), channel_id=1, replica_groups=mesh['row'=16,'col'=8] {'row'}, dimensions={0} | all-to-all | bytes 262144 | tf_op jit(solution)/shard_map/all_to_all | solution.py:336
  72.6 9.7 %all_to_all.101.parts_ref = f32[8,48,128]{2,1,0:T(8,128)S(1)} all-to-all(f32[8,48,128]{2,1,0:T(8,128)S(1)} %shard_map.83), channel_id=1, replica_groups=mesh['row'=16,'col'=8] {'col'}, dimensions={0} | all-to-all | bytes 393216 | tf_op jit(solution)/shard_map/all_to_all | solution.py:343
  84.8 2.4 shard_map.85
  87.2 2.6 shard_map.86
  89.8 15.3 %all_to_all.102.sums_ref = f32[128,1,128]{2,1,0:T(1,128)S(1)} all-to-all(f32[128,1,128]{2,1,0:T(1,128)S(1)} %get-tuple-element.161), channel_id=1, replica_groups=mesh['row'=16,'col'=8] {'row','col'}, dimensions={0} | all-to-all | bytes 131072 | tf_op jit(solution)/shard_map/all_to_all | solution.py:404
  109.7 2.0 collective-permute-start.14
  114.0 2.4 collective-permute-done.14.n2
  117.3 11.6 %all_to_all.103.x_ref = f32[16,16,128]{2,1,0:T(8,128)S(1)} all-to-all(f32[16,16,128]{2,1,0:T(8,128)S(1)} %get-tuple-element.176), channel_id=1, replica_groups=mesh['row'=16,'col'=8] {'row'}, dimensions={0} | all-to-all | bytes 262144 | tf_op jit(solution)/shard_map/all_to_all | solution.py:336
  129.5 9.7 %all_to_all.104.parts_ref = f32[8,48,128]{2,1,0:T(8,128)S(1)} all-to-all(f32[8,48,128]{2,1,0:T(8,128)S(1)} %shard_map.90), channel_id=1, replica_groups=mesh['row'=16,'col'=8] {'col'}, dimensions={0} | all-to-all | bytes 393216 | tf_op jit(solution)/shard_map/all_to_all | solution.py:343
  141.4 2.4 shard_map.92
  143.9 2.6 shard_map.93
  146.5 15.5 %all_to_all.105.sums_ref = f32[128,1,128]{2,1,0:T(1,128)S(1)} all-to-all(f32[128,1,128]{2,1,0:T(1,128)S(1)} %get-tuple-element.183), channel_id=1, replica_groups=mesh['row'=16,'col'=8] {'row','col'}, dimensions={0} | all-to-all | bytes 131072 | tf_op jit(solution)/shard_map/all_to_all | solution.py:404
  170.9 2.4 collective-permute-done.20.n2
  174.1 11.2 %all_to_all.106.x_ref = f32[16,16,128]{2,1,0:T(8,128)S(1)} all-to-all(f32[16,16,128]{2,1,0:T(8,128)S(1)} %get-tuple-element.197), channel_id=1, replica_groups=mesh['row'=16,'col'=8] {'row'}, dimensions={0} | all-to-all | bytes 262144 | tf_op jit(solution)/shard_map/all_to_all | solution.py:336
  185.9 9.7 %all_to_all.107.parts_ref = f32[8,48,128]{2,1,0:T(8,128)S(1)} all-to-all(f32[8,48,128]{2,1,0:T(8,128)S(1)} %shard_map.97), channel_id=1, replica_groups=mesh['row'=16,'col'=8] {'col'}, dimensions={0} | all-to-all | bytes 393216 | tf_op jit(solution)/shard_map/all_to_all | solution.py:343
  197.9 2.4 shard_map.99
  200.3 2.6 shard_map.100
  202.9 15.4 %all_to_all.108.sums_ref = f32[128,1,128]{2,1,0:T(1,128)S(1)} all-to-all(f32[128,1,128]{2,1,0:T(1,128)S(1)} %get-tuple-element.204), channel_id=1, replica_groups=mesh['row'=16,'col'=8] {'row','col'}, dimensions={0} | all-to-all | bytes 131072 | tf_op jit(solution)/shard_map/all_to_all | solution.py:404
  227.3 2.4 collective-permute-done.26.n2
  230.5 11.2 %all_to_all.109.x_ref = f32[16,16,128]{2,1,0:T(8,128)S(1)} all-to-all(f32[16,16,128]{2,1,0:T(8,128)S(1)} %get-tuple-element.218), channel_id=1, replica_groups=mesh['row'=16,'col'=8] {'row'}, dimensions={0} | all-to-all | bytes 262144 | tf_op jit(solution)/shard_map/all_to_all | solution.py:336
  242.3 9.7 %all_to_all.110.parts_ref = f32[8,48,128]{2,1,0:T(8,128)S(1)} all-to-all(f32[8,48,128]{2,1,0:T(8,128)S(1)} %shard_map.104), channel_id=1, replica_groups=mesh['row'=16,'col'=8] {'col'}, dimensions={0} | all-to-all | bytes 393216 | tf_op jit(solution)/shard_map/all_to_all | solution.py:343
  252.1 2.1 collective-permute-start.29
  254.3 2.4 shard_map.106
  256.7 2.6 shard_map.107
  259.3 15.6 %all_to_all.111.sums_ref = f32[128,1,128]{2,1,0:T(1,128)S(1)} all-to-all(f32[128,1,128]{2,1,0:T(1,128)S(1)} %get-tuple-element.225), channel_id=1, replica_groups=mesh['row'=16,'col'=8] {'row','col'}, dimensions={0} | all-to-all | bytes 131072 | tf_op jit(solution)/shard_map/all_to_all | solution.py:404
  283.9 2.4 collective-permute-done.32.n2
  287.1 11.2 %all_to_all.112.x_ref = f32[16,16,128]{2,1,0:T(8,128)S(1)} all-to-all(f32[16,16,128]{2,1,0:T(8,128)S(1)} %get-tuple-element.239), channel_id=1, replica_groups=mesh['row'=16,'col'=8] {'row'}, dimensions={0} | all-to-all | bytes 262144 | tf_op jit(solution)/shard_map/all_to_all | solution.py:336
  298.9 9.7 %all_to_all.113.parts_ref = f32[8,48,128]{2,1,0:T(8,128)S(1)} all-to-all(f32[8,48,128]{2,1,0:T(8,128)S(1)} %shard_map.111), channel_id=1, replica_groups=mesh['row'=16,'col'=8] {'col'}, dimensions={0} | all-to-all | bytes 393216 | tf_op jit(solution)/shard_map/all_to_all | solution.py:343
  310.9 2.4 shard_map.113
  313.3 2.6 shard_map.114
  315.9 15.4 %all_to_all.114.sums_ref = f32[128,1,128]{2,1,0:T(1,128)S(1)} all-to-all(f32[128,1,128]{2,1,0:T(1,128)S(1)} %get-tuple-element.246), channel_id=1, replica_groups=mesh['row'=16,'col'=8] {'row','col'}, dimensions={0} | all-to-all | bytes 131072 | tf_op jit(solution)/shard_map/all_to_all | solution.py:404
  335.9 2.0 collective-permute-start.38
  340.2 2.4 collective-permute-done.38.n2
  343.5 11.2 %all_to_all.115.x_ref = f32[16,16,128]{2,1,0:T(8,128)S(1)} all-to-all(f32[16,16,128]{2,1,0:T(8,128)S(1)} %get-tuple-element.260), channel_id=1, replica_groups=mesh['row'=16,'col'=8] {'row'}, dimensions={0} | all-to-all | bytes 262144 | tf_op jit(solution)/shard_map/all_to_all | solution.py:336
  355.3 9.7 %all_to_all.116.parts_ref = f32[8,48,128]{2,1,0:T(8,128)S(1)} all-to-all(f32[8,48,128]{2,1,0:T(8,128)S(1)} %shard_map.118), channel_id=1, replica_groups=mesh['row'=16,'col'=8] {'col'}, dimensions={0} | all-to-all | bytes 393216 | tf_op jit(solution)/shard_map/all_to_all | solution.py:343
  367.3 2.4 shard_map.120
  369.7 3.2 shard_map.121
  372.9 15.4 %all_to_all.117.sums_ref = f32[128,1,128]{2,1,0:T(1,128)S(1)} all-to-all(f32[128,1,128]{2,1,0:T(1,128)S(1)} %get-tuple-element.267), channel_id=1, replica_groups=mesh['row'=16,'col'=8] {'row','col'}, dimensions={0} | all-to-all | bytes 131072 | tf_op jit(solution)/shard_map/all_to_all | solution.py:404
  (118 shorter events, 77.9 us)
Async XLA Ops:
  2.1 14.1 %all-to-all-start = ((f32[16,16,128]{2,1,0:T(8,128)}), f32[16,16,128]{2,1,0:T(8,128)S(1)}, u32[]{:S(2)}, u32[]{:S(2)}) async-start(f32[16,16,128]{2,1,0:T(8,128)} %broadcast_in_dim.8), calls=%async_computation | async-start | bytes 262144 | tf_op jit(solution)/shard_map/all_to_all | solution.py:336
  11.0 23.2 %collective-permute-start.4 = (f32[104,512]{1,0:T(8,128)S(1)}, f32[104,512]{1,0:T(8,128)S(1)}, u32[]{:S(2)}, u32[]{:S(2)}) collective-permute-start(f32[104,512]{1,0:T(8,128)S(1)} %get-tuple-element.270.o3), channel_id=1, source_target_pairs={{0,1},{1,2},{2,3},{3,4},{4,5},{5,6},{6,7},{7,0},{8,9},{9,10},{10,1... | collective-permute-start | bytes 638984 | tf_op jit(solution)/shard_map/ppermute | solution.py:314
  13.5 1.6 copy-start.1
  17.4 14.0 %all-to-all-start.1 = ((f32[8,48,128]{2,1,0:T(8,128)}), f32[8,48,128]{2,1,0:T(8,128)S(1)}, u32[]{:S(2)}, u32[]{:S(2)}) async-start(f32[8,48,128]{2,1,0:T(8,128)} %shard_map.78), calls=%async_computation.1 | async-start | bytes 393216 | tf_op jit(solution)/shard_map/all_to_all | solution.py:343
  23.6 11.9 %collective-permute-start.5 = (f32[104,512]{1,0:T(8,128)S(1)}, f32[104,512]{1,0:T(8,128)}, u32[]{:S(2)}, u32[]{:S(2)}) collective-permute-start(f32[104,512]{1,0:T(8,128)S(1)} %get-tuple-element.271.o2), channel_id=1, source_target_pairs={{0,7},{1,0},{2,1},{3,2},{4,3},{5,4},{6,5},{7,6},{8,15},{9,8},{10,9... | collective-permute-start | bytes 638984 | tf_op jit(solution)/shard_map/ppermute | solution.py:314
  28.7 7.9 %collective-permute-start.2 = (f32[104,512]{1,0:T(8,128)S(1)}, f32[104,512]{1,0:T(8,128)}, u32[]{:S(2)}, u32[]{:S(2)}) collective-permute-start(f32[104,512]{1,0:T(8,128)S(1)} %get-tuple-element.272.o1), channel_id=1, source_target_pairs={{0,8},{8,16},{16,24},{24,32},{32,40},{40,48},{48,56},{56,64},{64,7... | collective-permute-start | bytes 638984 | tf_op jit(solution)/shard_map/ppermute | solution.py:314
  31.4 9.3 %collective-permute-start.3 = (f32[104,512]{1,0:T(8,128)S(1)}, f32[104,512]{1,0:T(8,128)}, u32[]{:S(2)}, u32[]{:S(2)}) collective-permute-start(f32[104,512]{1,0:T(8,128)S(1)} %get-tuple-element.273.o0), channel_id=1, source_target_pairs={{0,120},{8,0},{16,8},{24,16},{32,24},{40,32},{48,40},{56,48},{64,5... | collective-permute-start | bytes 638984 | tf_op jit(solution)/shard_map/ppermute | solution.py:314
  31.4 53.3 %copy-start = (f32[1,1,2048,2048]{3,2,1,0:T(8,128)S(1)}, f32[1,1,2048,2048]{3,2,1,0:T(8,128)}, u32[]{:S(2)}) copy-start(f32[1,1,2048,2048]{3,2,1,0:T(8,128)} %param.6) | copy-start | bytes 50331652
  31.5 10.6 %collective-permute-start.1 = (f32[32,128]{1,0:T(8,128)S(1)}, f32[32,128]{1,0:T(8,128)S(1)}, u32[]{:S(2)}, u32[]{:S(2)}) collective-permute-start(f32[32,128]{1,0:T(8,128)S(1)} %get-tuple-element.138.own_ref), channel_id=1, source_target_pairs={{0,120},{8,0},{16,8},{24,16},{32,24},{40,32},{48,40},{56,48},{64,5... | collective-permute-start | bytes 49160 | tf_op jit(solution)/shard_map/ppermute | solution.py:314
  34.2 7.9 %collective-permute-start = (f32[32,128]{1,0:T(8,128)S(1)}, f32[32,128]{1,0:T(8,128)S(1)}, u32[]{:S(2)}, u32[]{:S(2)}) collective-permute-start(f32[32,128]{1,0:T(8,128)S(1)} %get-tuple-element.138.own_ref), channel_id=1, source_target_pairs={{0,8},{8,16},{16,24},{24,32},{32,40},{40,48},{48,56},{56,64},{64,7... | collective-permute-start | bytes 49160 | tf_op jit(solution)/shard_map/ppermute | solution.py:314
  48.4 4.8 %collective-permute-start.7 = (f32[32,512]{1,0:T(8,128)S(1)}, f32[32,512]{1,0:T(8,128)S(1)}, u32[]{:S(2)}, u32[]{:S(2)}) collective-permute-start(f32[32,512]{1,0:T(8,128)S(1)} %get-tuple-element.148.a0.o0), channel_id=1, source_target_pairs={{0,120},{8,0},{16,8},{24,16},{32,24},{40,32},{48,40},{56,48},{64,5... | collective-permute-start | bytes 196616 | tf_op jit(solution)/shard_map/ppermute | solution.py:314
  49.1 4.1 %collective-permute-start.6 = (f32[32,512]{1,0:T(8,128)S(1)}, f32[32,512]{1,0:T(8,128)S(1)}, u32[]{:S(2)}, u32[]{:S(2)}) collective-permute-start(f32[32,512]{1,0:T(8,128)S(1)} %get-tuple-element.149.a1.o1), channel_id=1, source_target_pairs={{0,8},{8,16},{16,24},{24,32},{32,40},{40,48},{48,56},{56,64},{64,7... | collective-permute-start | bytes 196616 | tf_op jit(solution)/shard_map/ppermute | solution.py:314
  50.2 4.6 %collective-permute-start.9 = (f32[32,512]{1,0:T(8,128)S(1)}, f32[32,512]{1,0:T(8,128)S(1)}, u32[]{:S(2)}, u32[]{:S(2)}) collective-permute-start(f32[32,512]{1,0:T(8,128)S(1)} %get-tuple-element.150.a2.o2), channel_id=1, source_target_pairs={{0,7},{1,0},{2,1},{3,2},{4,3},{5,4},{6,5},{7,6},{8,15},{9,8},{10,9... | collective-permute-start | bytes 196616 | tf_op jit(solution)/shard_map/ppermute | solution.py:314
  53.2 6.7 %collective-permute-start.8 = (f32[32,512]{1,0:T(8,128)S(1)}, f32[32,512]{1,0:T(8,128)S(1)}, u32[]{:S(2)}, u32[]{:S(2)}) collective-permute-start(f32[32,512]{1,0:T(8,128)S(1)} %get-tuple-element.151.a3.o3), channel_id=1, source_target_pairs={{0,1},{1,2},{2,3},{3,4},{4,5},{5,6},{6,7},{7,0},{8,9},{9,10},{10,1... | collective-permute-start | bytes 196616 | tf_op jit(solution)/shard_map/ppermute | solution.py:314
  82.4 4.8 %collective-permute-start.11 = (f32[32,128]{1,0:T(8,128)S(1)}, f32[32,128]{1,0:T(8,128)S(1)}, u32[]{:S(2)}, u32[]{:S(2)}) collective-permute-start(f32[32,128]{1,0:T(8,128)S(1)} %get-tuple-element.155.own_ref), channel_id=1, source_target_pairs={{0,120},{8,0},{16,8},{24,16},{32,24},{40,32},{48,40},{56,48},{64,5... | collective-permute-start | bytes 49160 | tf_op jit(solution)/shard_map/ppermute | solution.py:314
  84.2 3.0 collective-permute-start.10
  106.9 5.8 %collective-permute-start.13 = (f32[32,512]{1,0:T(8,128)S(1)}, f32[32,512]{1,0:T(8,128)S(1)}, u32[]{:S(2)}, u32[]{:S(2)}) collective-permute-start(f32[32,512]{1,0:T(8,128)S(1)} %get-tuple-element.168.o0), channel_id=1, source_target_pairs={{0,120},{8,0},{16,8},{24,16},{32,24},{40,32},{48,40},{56,48},{64,5... | collective-permute-start | bytes 196616 | tf_op jit(solution)/shard_map/ppermute | solution.py:314
  107.6 5.1 %collective-permute-start.12 = (f32[32,512]{1,0:T(8,128)S(1)}, f32[32,512]{1,0:T(8,128)S(1)}, u32[]{:S(2)}, u32[]{:S(2)}) collective-permute-start(f32[32,512]{1,0:T(8,128)S(1)} %get-tuple-element.169.o1), channel_id=1, source_target_pairs={{0,8},{8,16},{16,24},{24,32},{32,40},{40,48},{48,56},{56,64},{64,7... | collective-permute-start | bytes 196616 | tf_op jit(solution)/shard_map/ppermute | solution.py:314
  108.7 5.3 %collective-permute-start.15 = (f32[32,512]{1,0:T(8,128)S(1)}, f32[32,512]{1,0:T(8,128)S(1)}, u32[]{:S(2)}, u32[]{:S(2)}) collective-permute-start(f32[32,512]{1,0:T(8,128)S(1)} %get-tuple-element.170.o2), channel_id=1, source_target_pairs={{0,7},{1,0},{2,1},{3,2},{4,3},{5,4},{6,5},{7,6},{8,15},{9,8},{10,9... | collective-permute-start | bytes 196616 | tf_op jit(solution)/shard_map/ppermute | solution.py:314
  109.7 6.7 %collective-permute-start.14 = (f32[32,512]{1,0:T(8,128)S(1)}, f32[32,512]{1,0:T(8,128)S(1)}, u32[]{:S(2)}, u32[]{:S(2)}) collective-permute-start(f32[32,512]{1,0:T(8,128)S(1)} %get-tuple-element.171.o3), channel_id=1, source_target_pairs={{0,1},{1,2},{2,3},{3,4},{4,5},{5,6},{6,7},{7,0},{8,9},{9,10},{10,1... | collective-permute-start | bytes 196616 | tf_op jit(solution)/shard_map/ppermute | solution.py:314
  139.3 4.6 %collective-permute-start.17 = (f32[32,128]{1,0:T(8,128)S(1)}, f32[32,128]{1,0:T(8,128)S(1)}, u32[]{:S(2)}, u32[]{:S(2)}) collective-permute-start(f32[32,128]{1,0:T(8,128)S(1)} %get-tuple-element.177.own_ref), channel_id=1, source_target_pairs={{0,120},{8,0},{16,8},{24,16},{32,24},{40,32},{48,40},{56,48},{64,5... | collective-permute-start | bytes 49160 | tf_op jit(solution)/shard_map/ppermute | solution.py:314
  141.1 2.7 collective-permute-start.16
  163.8 5.9 %collective-permute-start.19 = (f32[32,512]{1,0:T(8,128)S(1)}, f32[32,512]{1,0:T(8,128)S(1)}, u32[]{:S(2)}, u32[]{:S(2)}) collective-permute-start(f32[32,512]{1,0:T(8,128)S(1)} %get-tuple-element.189.o0), channel_id=1, source_target_pairs={{0,120},{8,0},{16,8},{24,16},{32,24},{40,32},{48,40},{56,48},{64,5... | collective-permute-start | bytes 196616 | tf_op jit(solution)/shard_map/ppermute | solution.py:314
  164.5 5.2 %collective-permute-start.18 = (f32[32,512]{1,0:T(8,128)S(1)}, f32[32,512]{1,0:T(8,128)S(1)}, u32[]{:S(2)}, u32[]{:S(2)}) collective-permute-start(f32[32,512]{1,0:T(8,128)S(1)} %get-tuple-element.190.o1), channel_id=1, source_target_pairs={{0,8},{8,16},{16,24},{24,32},{32,40},{40,48},{48,56},{56,64},{64,7... | collective-permute-start | bytes 196616 | tf_op jit(solution)/shard_map/ppermute | solution.py:314
  165.5 5.3 %collective-permute-start.21 = (f32[32,512]{1,0:T(8,128)S(1)}, f32[32,512]{1,0:T(8,128)S(1)}, u32[]{:S(2)}, u32[]{:S(2)}) collective-permute-start(f32[32,512]{1,0:T(8,128)S(1)} %get-tuple-element.191.o2), channel_id=1, source_target_pairs={{0,7},{1,0},{2,1},{3,2},{4,3},{5,4},{6,5},{7,6},{8,15},{9,8},{10,9... | collective-permute-start | bytes 196616 | tf_op jit(solution)/shard_map/ppermute | solution.py:314
  166.5 6.7 %collective-permute-start.20 = (f32[32,512]{1,0:T(8,128)S(1)}, f32[32,512]{1,0:T(8,128)S(1)}, u32[]{:S(2)}, u32[]{:S(2)}) collective-permute-start(f32[32,512]{1,0:T(8,128)S(1)} %get-tuple-element.192.o3), channel_id=1, source_target_pairs={{0,1},{1,2},{2,3},{3,4},{4,5},{5,6},{6,7},{7,0},{8,9},{9,10},{10,1... | collective-permute-start | bytes 196616 | tf_op jit(solution)/shard_map/ppermute | solution.py:314
  195.7 4.6 %collective-permute-start.23 = (f32[32,128]{1,0:T(8,128)S(1)}, f32[32,128]{1,0:T(8,128)S(1)}, u32[]{:S(2)}, u32[]{:S(2)}) collective-permute-start(f32[32,128]{1,0:T(8,128)S(1)} %get-tuple-element.198.own_ref), channel_id=1, source_target_pairs={{0,120},{8,0},{16,8},{24,16},{32,24},{40,32},{48,40},{56,48},{64,5... | collective-permute-start | bytes 49160 | tf_op jit(solution)/shard_map/ppermute | solution.py:314
  197.6 2.7 collective-permute-start.22
  220.1 6.2 %collective-permute-start.25 = (f32[32,512]{1,0:T(8,128)S(1)}, f32[32,512]{1,0:T(8,128)S(1)}, u32[]{:S(2)}, u32[]{:S(2)}) collective-permute-start(f32[32,512]{1,0:T(8,128)S(1)} %get-tuple-element.210.o0), channel_id=1, source_target_pairs={{0,120},{8,0},{16,8},{24,16},{32,24},{40,32},{48,40},{56,48},{64,5... | collective-permute-start | bytes 196616 | tf_op jit(solution)/shard_map/ppermute | solution.py:314
  220.9 5.5 %collective-permute-start.24 = (f32[32,512]{1,0:T(8,128)S(1)}, f32[32,512]{1,0:T(8,128)S(1)}, u32[]{:S(2)}, u32[]{:S(2)}) collective-permute-start(f32[32,512]{1,0:T(8,128)S(1)} %get-tuple-element.211.o1), channel_id=1, source_target_pairs={{0,8},{8,16},{16,24},{24,32},{32,40},{40,48},{48,56},{56,64},{64,7... | collective-permute-start | bytes 196616 | tf_op jit(solution)/shard_map/ppermute | solution.py:314
  221.9 5.3 %collective-permute-start.27 = (f32[32,512]{1,0:T(8,128)S(1)}, f32[32,512]{1,0:T(8,128)S(1)}, u32[]{:S(2)}, u32[]{:S(2)}) collective-permute-start(f32[32,512]{1,0:T(8,128)S(1)} %get-tuple-element.212.o2), channel_id=1, source_target_pairs={{0,7},{1,0},{2,1},{3,2},{4,3},{5,4},{6,5},{7,6},{8,15},{9,8},{10,9... | collective-permute-start | bytes 196616 | tf_op jit(solution)/shard_map/ppermute | solution.py:314
  222.9 6.7 %collective-permute-start.26 = (f32[32,512]{1,0:T(8,128)S(1)}, f32[32,512]{1,0:T(8,128)S(1)}, u32[]{:S(2)}, u32[]{:S(2)}) collective-permute-start(f32[32,512]{1,0:T(8,128)S(1)} %get-tuple-element.213.o3), channel_id=1, source_target_pairs={{0,1},{1,2},{2,3},{3,4},{4,5},{5,6},{6,7},{7,0},{8,9},{9,10},{10,1... | collective-permute-start | bytes 196616 | tf_op jit(solution)/shard_map/ppermute | solution.py:314
  252.1 4.6 %collective-permute-start.29 = (f32[32,128]{1,0:T(8,128)S(1)}, f32[32,128]{1,0:T(8,128)S(1)}, u32[]{:S(2)}, u32[]{:S(2)}) collective-permute-start(f32[32,128]{1,0:T(8,128)S(1)} %get-tuple-element.219.own_ref), channel_id=1, source_target_pairs={{0,120},{8,0},{16,8},{24,16},{32,24},{40,32},{48,40},{56,48},{64,5... | collective-permute-start | bytes 49160 | tf_op jit(solution)/shard_map/ppermute | solution.py:314
  254.2 2.6 collective-permute-start.28
  276.7 5.9 %collective-permute-start.31 = (f32[32,512]{1,0:T(8,128)S(1)}, f32[32,512]{1,0:T(8,128)S(1)}, u32[]{:S(2)}, u32[]{:S(2)}) collective-permute-start(f32[32,512]{1,0:T(8,128)S(1)} %get-tuple-element.231.o0), channel_id=1, source_target_pairs={{0,120},{8,0},{16,8},{24,16},{32,24},{40,32},{48,40},{56,48},{64,5... | collective-permute-start | bytes 196616 | tf_op jit(solution)/shard_map/ppermute | solution.py:314
  277.4 5.2 %collective-permute-start.30 = (f32[32,512]{1,0:T(8,128)S(1)}, f32[32,512]{1,0:T(8,128)S(1)}, u32[]{:S(2)}, u32[]{:S(2)}) collective-permute-start(f32[32,512]{1,0:T(8,128)S(1)} %get-tuple-element.232.o1), channel_id=1, source_target_pairs={{0,8},{8,16},{16,24},{24,32},{32,40},{40,48},{48,56},{56,64},{64,7... | collective-permute-start | bytes 196616 | tf_op jit(solution)/shard_map/ppermute | solution.py:314
  278.5 5.3 %collective-permute-start.33 = (f32[32,512]{1,0:T(8,128)S(1)}, f32[32,512]{1,0:T(8,128)S(1)}, u32[]{:S(2)}, u32[]{:S(2)}) collective-permute-start(f32[32,512]{1,0:T(8,128)S(1)} %get-tuple-element.233.o2), channel_id=1, source_target_pairs={{0,7},{1,0},{2,1},{3,2},{4,3},{5,4},{6,5},{7,6},{8,15},{9,8},{10,9... | collective-permute-start | bytes 196616 | tf_op jit(solution)/shard_map/ppermute | solution.py:314
  279.5 6.7 %collective-permute-start.32 = (f32[32,512]{1,0:T(8,128)S(1)}, f32[32,512]{1,0:T(8,128)S(1)}, u32[]{:S(2)}, u32[]{:S(2)}) collective-permute-start(f32[32,512]{1,0:T(8,128)S(1)} %get-tuple-element.234.o3), channel_id=1, source_target_pairs={{0,1},{1,2},{2,3},{3,4},{4,5},{5,6},{6,7},{7,0},{8,9},{9,10},{10,1... | collective-permute-start | bytes 196616 | tf_op jit(solution)/shard_map/ppermute | solution.py:314
  308.7 4.6 %collective-permute-start.35 = (f32[32,128]{1,0:T(8,128)S(1)}, f32[32,128]{1,0:T(8,128)S(1)}, u32[]{:S(2)}, u32[]{:S(2)}) collective-permute-start(f32[32,128]{1,0:T(8,128)S(1)} %get-tuple-element.240.own_ref), channel_id=1, source_target_pairs={{0,120},{8,0},{16,8},{24,16},{32,24},{40,32},{48,40},{56,48},{64,5... | collective-permute-start | bytes 49160 | tf_op jit(solution)/shard_map/ppermute | solution.py:314
  310.6 2.7 collective-permute-start.34
  333.1 6.0 %collective-permute-start.37 = (f32[32,512]{1,0:T(8,128)S(1)}, f32[32,512]{1,0:T(8,128)S(1)}, u32[]{:S(2)}, u32[]{:S(2)}) collective-permute-start(f32[32,512]{1,0:T(8,128)S(1)} %get-tuple-element.252.o0), channel_id=1, source_target_pairs={{0,120},{8,0},{16,8},{24,16},{32,24},{40,32},{48,40},{56,48},{64,5... | collective-permute-start | bytes 196616 | tf_op jit(solution)/shard_map/ppermute | solution.py:314
  333.8 5.3 %collective-permute-start.36 = (f32[32,512]{1,0:T(8,128)S(1)}, f32[32,512]{1,0:T(8,128)S(1)}, u32[]{:S(2)}, u32[]{:S(2)}) collective-permute-start(f32[32,512]{1,0:T(8,128)S(1)} %get-tuple-element.253.o1), channel_id=1, source_target_pairs={{0,8},{8,16},{16,24},{24,32},{32,40},{40,48},{48,56},{56,64},{64,7... | collective-permute-start | bytes 196616 | tf_op jit(solution)/shard_map/ppermute | solution.py:314
  334.9 5.3 %collective-permute-start.39 = (f32[32,512]{1,0:T(8,128)S(1)}, f32[32,512]{1,0:T(8,128)S(1)}, u32[]{:S(2)}, u32[]{:S(2)}) collective-permute-start(f32[32,512]{1,0:T(8,128)S(1)} %get-tuple-element.254.o2), channel_id=1, source_target_pairs={{0,7},{1,0},{2,1},{3,2},{4,3},{5,4},{6,5},{7,6},{8,15},{9,8},{10,9... | collective-permute-start | bytes 196616 | tf_op jit(solution)/shard_map/ppermute | solution.py:314
  335.9 6.7 %collective-permute-start.38 = (f32[32,512]{1,0:T(8,128)S(1)}, f32[32,512]{1,0:T(8,128)S(1)}, u32[]{:S(2)}, u32[]{:S(2)}) collective-permute-start(f32[32,512]{1,0:T(8,128)S(1)} %get-tuple-element.255.o3), channel_id=1, source_target_pairs={{0,1},{1,2},{2,3},{3,4},{4,5},{5,6},{6,7},{7,0},{8,9},{9,10},{10,1... | collective-permute-start | bytes 196616 | tf_op jit(solution)/shard_map/ppermute | solution.py:314
  365.1 4.6 %collective-permute-start.41 = (f32[32,128]{1,0:T(8,128)S(1)}, f32[32,128]{1,0:T(8,128)S(1)}, u32[]{:S(2)}, u32[]{:S(2)}) collective-permute-start(f32[32,128]{1,0:T(8,128)S(1)} %get-tuple-element.261.own_ref), channel_id=1, source_target_pairs={{0,120},{8,0},{16,8},{24,16},{32,24},{40,32},{48,40},{56,48},{64,5... | collective-permute-start | bytes 49160 | tf_op jit(solution)/shard_map/ppermute | solution.py:314
  367.0 2.7 collective-permute-start.40
  388.3 1.0 copy-start.2
